TPU v7x, 32 devices: a whole 2x2x4 slice. The times are simulated.
32 devices in a mesh: pipe: 4 (over z), ctx: 8 (over y, x, core).
Axes of the slice: x: 2, y: 2, z: 4, core: 2. Of those that a mesh axis runs over, the one named last changes fastest.
Arguments:
- queries: bfloat16 [4, 1024, 4096], P('pipe', 'ctx'), may hold values from -6 to 6
- stash: bfloat16 [4, 1024, 1024], P('pipe', 'ctx'), may hold values from -6 to 6
- grad_out: bfloat16 [4, 1024, 4096], P('pipe', 'ctx'), may hold values from -6 to 6
- lengths: int32 [2], replicated, may hold values from 1 to 513, 1024 in all
Outputs:
- grad_kv: bfloat16 [4, 1024, 1024], P('pipe', 'ctx')
Inputs may be any that keep to these rules, and one draw needn't show every extreme that they name: The lengths sum to 1024; one document is exactly 513 long.
All inputs are finite; a program needn't handle non-finite values.
Results may differ from a plain program's by a relative error of at most 0.0059.
Values may be sent and summed in bfloat16 or wider, within the bound.
No kernel may reach another device: no remote copies, remote signals or barrier semaphores. Data moves between devices by JAX's collectives and lax.ppermute only.
A program may use at most 64 MiB of HBM per device.

v0:
```python
import jax
import jax.numpy as jnp
from jax import lax
from jax.sharding import PartitionSpec as P

H = 32
KVH = 4
HD = 128
REACH = 5


def from_partner(block, axis, stride):
    count = lax.axis_size(axis)
    route = []
    for low in range(count):
        high = low | 1 << stride
        if high != low and high < count:
            route += [(low, high), (high, low)]
    return lax.ppermute(block, axis, route)


def from_behind(value, axis, steps):
    count = lax.axis_size(axis)
    first, last = (max(0, -steps), min(count, count - steps))
    return lax.ppermute(value, axis, [(source, source + steps) for source in range(first, last)])


def segment_of(positions, lengths):
    doc_ends = jnp.cumsum(lengths)
    return jnp.sum((doc_ends[None, :] <= positions[:, None]).astype(jnp.int32), axis=1)


def on_device(queries, stash, grad_out, lengths):
    row_count = queries.shape[1]
    group = H // KVH
    width_kv = 2 * KVH * HD
    high_bit = lax.axis_size("pipe").bit_length() - 2
    own_kv = from_partner(stash, "pipe", high_bit)[0]
    pieces = [own_kv]
    for back in range(1, REACH):
        pieces.insert(0, from_behind(own_kv, "ctx", back))
    joined = jnp.concatenate(pieces, axis=0)
    first_row = lax.axis_index("ctx") * row_count
    key_pos = first_row - (REACH - 1) * row_count + jnp.arange(REACH * row_count, dtype=jnp.int32)
    key_seg = segment_of(key_pos, lengths)
    tail = (REACH - 1) * row_count
    query_pos = key_pos[tail:]
    query_seg = key_seg[tail:]
    allowed = (
        (key_seg[None, :] == query_seg[:, None])
        & (key_pos[None, :] <= query_pos[:, None])
        & (key_pos[None, :] >= 0)
    )
    kv_heads = joined.reshape(REACH * row_count, 2, KVH, HD)
    keys_h = jnp.transpose(kv_heads[:, 0], (1, 0, 2))
    values_h = jnp.transpose(kv_heads[:, 1], (1, 0, 2))
    query_h = jnp.transpose(queries[0].reshape(row_count, KVH, group, HD), (1, 0, 2, 3))
    cot_h = jnp.transpose(grad_out[0].reshape(row_count, KVH, group, HD), (1, 0, 2, 3))
    score_scale = HD ** (-0.5)

    def head_grads(items):
        query_block, cotangent, key_block, value_block = items
        scores = (
            jnp.einsum("rgd,kd->grk", query_block, key_block, preferred_element_type=jnp.float32)
            * score_scale
        )
        scores = jnp.where(allowed[None], scores, -1e30)
        row_top = jnp.max(scores, axis=-1, keepdims=True)
        raw_weights = jnp.exp(scores - row_top)
        weights = raw_weights / jnp.sum(raw_weights, axis=-1, keepdims=True)
        weights16 = weights.astype(jnp.bfloat16)
        output = jnp.einsum(
            "grk,kd->rgd", weights16, value_block, preferred_element_type=jnp.float32
        )
        row_delta = jnp.sum(cotangent.astype(jnp.float32) * output, axis=-1)
        dweights = jnp.einsum(
            "rgd,kd->grk", cotangent, value_block, preferred_element_type=jnp.float32
        )
        dscores = (
            weights * (dweights - jnp.transpose(row_delta, (1, 0))[..., None]) * score_scale
        ).astype(jnp.bfloat16)
        grad_key = jnp.einsum(
            "grk,rgd->kd", dscores, query_block, preferred_element_type=jnp.float32
        )
        grad_value = jnp.einsum(
            "grk,rgd->kd", weights16, cotangent, preferred_element_type=jnp.float32
        )
        return (grad_key, grad_value)

    grad_key, grad_value = lax.map(head_grads, (query_h, cot_h, keys_h, values_h))
    key_grads = jnp.transpose(jnp.stack([grad_key, grad_value], axis=0), (2, 0, 1, 3))
    key_grads = key_grads.reshape(REACH, row_count, width_kv)
    total = key_grads[REACH - 1]
    for back in range(1, REACH):
        total = total + from_behind(key_grads[REACH - 1 - back], "ctx", -back)
    return total.astype(jnp.bfloat16).reshape(1, row_count, width_kv)


def solution(mesh):
    placed = (P("pipe", "ctx", None), P("pipe", "ctx", None), P("pipe", "ctx", None), P())
    return jax.shard_map(
        on_device, mesh=mesh, in_specs=placed, out_specs=P("pipe", "ctx", None), check_vma=False
    )
```

profile of v0, /device:TPU:26, one launch (start us, length us, event | category | flops | bytes accessed | tf_op | source)
XLA Modules:
  0.0 137.1 jit_solution(12066921376861813174)
XLA Ops:
  0.0 1.2 copy.25
  1.2 0.4 collective-permute-start
  1.6 14.1 %collective-permute-done = bf16[1,128,1024]{1,2,0:T(8,128)(2,1)S(1)} collective-permute-done((bf16[1,128,1024]{1,2,0:T(8,128)(2,1)S(1)}, bf16[1,128,1024]{1,2,0:T(8,128)(2,1)S(1)}, u32[]{:S(2)}, u32[]{:S(2)}) %collective-permute-start) | collective-permute-done | bytes 262176 | tf_op jit(solution)/shard_map/ppermute | solution.py:19
  15.7 3.4 %collective-permute-start.1 = (bf16[128,1024]{0,1:T(8,128)(2,1)S(1)}, bf16[128,1024]{0,1:T(8,128)(2,1)S(1)}, u32[]{:S(2)}, u32[]{:S(2)}) collective-permute-start(bf16[128,1024]{0,1:T(8,128)(2,1)S(1)} %bitcast.147), channel_id=1, source_target_pairs={{0,4},{1,5},{2,6},{3,7},{8,12},{9,13},{10,14},{11,15},{16,20},{17,... | collective-permute-start | bytes 786440 | tf_op jit(solution)/shard_map/ppermute | solution.py:25
  19.2 0.8 reduce-window.8
  20.0 1.3 collective-permute-start.2
  21.4 3.0 %collective-permute-start.3 = (bf16[128,1024]{0,1:T(8,128)(2,1)S(1)}, bf16[128,1024]{0,1:T(8,128)(2,1)S(1)}, u32[]{:S(2)}, u32[]{:S(2)}) collective-permute-start(bf16[128,1024]{0,1:T(8,128)(2,1)S(1)} %bitcast.149), channel_id=1, source_target_pairs={{0,2},{1,3},{2,4},{3,5},{4,6},{5,7},{8,10},{9,11},{10,12},{11,13},... | collective-permute-start | bytes 786440 | tf_op jit(solution)/shard_map/ppermute | solution.py:25
  24.4 1.6 %copy.27 = bf16[1,128,4096]{1,2,0:T(8,128)(2,1)S(1)} copy(bf16[1,128,4096]{2,1,0:T(8,128)(2,1)} %param.8) | data formatting | bytes 2097152 | tf_op args[2]
  26.1 1.3 copy.26
  27.4 1.9 %collective-permute-start.4 = (bf16[128,1024]{0,1:T(8,128)(2,1)S(1)}, bf16[128,1024]{0,1:T(8,128)(2,1)S(1)}, u32[]{:S(2)}, u32[]{:S(2)}) collective-permute-start(bf16[128,1024]{0,1:T(8,128)(2,1)S(1)} %bitcast.150), channel_id=1, source_target_pairs={{0,1},{1,2},{2,3},{3,4},{4,5},{5,6},{6,7},{8,9},{9,10},{10,11},{11... | collective-permute-start | bytes 786440 | tf_op jit(solution)/shard_map/ppermute | solution.py:25
  29.4 4.7 %collective-permute-done.3 = bf16[128,1024]{0,1:T(8,128)(2,1)S(1)} collective-permute-done((bf16[128,1024]{0,1:T(8,128)(2,1)S(1)}, bf16[128,1024]{0,1:T(8,128)(2,1)S(1)}, u32[]{:S(2)}, u32[]{:S(2)}) %collective-permute-start.3) | collective-permute-done | bytes 262176 | tf_op jit(solution)/shard_map/ppermute | solution.py:25
  34.2 1.8 %collective-permute-done.4 = bf16[128,1024]{0,1:T(8,128)(2,1)S(1)} collective-permute-done((bf16[128,1024]{0,1:T(8,128)(2,1)S(1)}, bf16[128,1024]{0,1:T(8,128)(2,1)S(1)}, u32[]{:S(2)}, u32[]{:S(2)}) %collective-permute-start.4) | collective-permute-done | bytes 262176 | tf_op jit(solution)/shard_map/ppermute | solution.py:25
  36.2 1.0 slice_bitcast_fusion
  37.1 46.8 %while.13 = (s32[]{:T(128)}, f32[4,640,128]{2,1,0:T(8,128)}, f32[4,640,128]{2,1,0:T(8,128)}, bf16[4,640,128]{1,2,0:T(8,128)(2,1)}, bf16[4,128,8,128]{1,3,2,0:T(8...) while((s32[]{:T(128)}, f32[4,640,128]{2,1,0:T(8,128)}, ...), condition=%wide.region_6.7_spmd.clone, body=%wide.region_2.6_spmd.clone.sunk | while | flops 846790272 | bytes 15506293 | solution.py:90
  37.7 3.5 %fusion.89 = (f32[8,128]{1,0:T(8,128)S(1)}, f32[8,128,640]{1,2,0:T(8,128)}) fusion(pred[128,640]{0,1:T(8,128)(4,1)S(1)} %and_and_fusion.2, bf16[4,128,8,128]{1,3,2,0:T(8,128)(2,1)} %get-tuple-element.245, s32[]{:T(128)} %get-tuple-element.228, bf16[4,640,128]{1,2,0:T(8,128)(2,1)} %get-tuple-element.244), kind=kOutput, calls=%fused_computation.65.clone.1 | convolution fusion | flops 170394240 | bytes 3134464 | tf_op jit(solution)/shard_map/while/body/eval_jaxpr/sub | solution.py:69
  41.2 2.0 %fusion.90 = bf16[8,128,640]{1,2,0:T(8,128)(2,1)S(1)} fusion(f32[8,128,640]{1,2,0:T(8,128)} %get-tuple-element.213, f32[8,128]{1,0:T(8,128)S(1)} %get-tuple-element.214), kind=kLoop, calls=%fused_computation.23.clone.1 | loop fusion | flops 1310720 | bytes 3936256 | tf_op jit(solution)/shard_map/while/body/eval_jaxpr/convert_element_type | solution.py:71
  43.4 0.7 fusion.91
  44.1 3.5 %fusion.92 = f32[4,640,128]{2,1,0:T(8,128)} fusion(f32[4,640,128]{2,1,0:T(8,128)} %get-tuple-element.229, s32[]{:T(128)} %get-tuple-element.228, f32[8,128]{1,0:T(8,128)S(1)} %bitcast.156, f32[8,128,640]{1,2,0:T(8,128)} %get-tuple-element.213, f32[8,128]{1,0:T(8,128)S(1)} %get-tuple-element.214, bf16[4,128,8,128]{1,3,2,0:T(8,128)(2,1)} %get-tuple-element.245, ...), kind=kOutput, calls=%fused_computation.19.clone.1 | convolution fusion | flops 338821120 | bytes 3647488 | tf_op jit(solution)/shard_map/while/body/eval_jaxpr/grk,rgd->kd/dot_general | solution.py:82
  47.6 1.2 fusion.93
  49.4 3.5 %fusion.89 = (f32[8,128]{1,0:T(8,128)S(1)}, f32[8,128,640]{1,2,0:T(8,128)}) fusion(pred[128,640]{0,1:T(8,128)(4,1)S(1)} %and_and_fusion.2, bf16[4,128,8,128]{1,3,2,0:T(8,128)(2,1)} %get-tuple-element.245, s32[]{:T(128)} %get-tuple-element.228, bf16[4,640,128]{1,2,0:T(8,128)(2,1)} %get-tuple-element.244), kind=kOutput, calls=%fused_computation.65.clone.1 | convolution fusion | flops 170394240 | bytes 3134464 | tf_op jit(solution)/shard_map/while/body/eval_jaxpr/sub | solution.py:69
  52.9 2.0 %fusion.90 = bf16[8,128,640]{1,2,0:T(8,128)(2,1)S(1)} fusion(f32[8,128,640]{1,2,0:T(8,128)} %get-tuple-element.213, f32[8,128]{1,0:T(8,128)S(1)} %get-tuple-element.214), kind=kLoop, calls=%fused_computation.23.clone.1 | loop fusion | flops 1310720 | bytes 3936256 | tf_op jit(solution)/shard_map/while/body/eval_jaxpr/convert_element_type | solution.py:71
  55.0 0.7 fusion.91
  55.8 3.5 %fusion.92 = f32[4,640,128]{2,1,0:T(8,128)} fusion(f32[4,640,128]{2,1,0:T(8,128)} %get-tuple-element.229, s32[]{:T(128)} %get-tuple-element.228, f32[8,128]{1,0:T(8,128)S(1)} %bitcast.156, f32[8,128,640]{1,2,0:T(8,128)} %get-tuple-element.213, f32[8,128]{1,0:T(8,128)S(1)} %get-tuple-element.214, bf16[4,128,8,128]{1,3,2,0:T(8,128)(2,1)} %get-tuple-element.245, ...), kind=kOutput, calls=%fused_computation.19.clone.1 | convolution fusion | flops 338821120 | bytes 3647488 | tf_op jit(solution)/shard_map/while/body/eval_jaxpr/grk,rgd->kd/dot_general | solution.py:82
  59.3 1.2 fusion.93
  61.1 3.5 %fusion.89 = (f32[8,128]{1,0:T(8,128)S(1)}, f32[8,128,640]{1,2,0:T(8,128)}) fusion(pred[128,640]{0,1:T(8,128)(4,1)S(1)} %and_and_fusion.2, bf16[4,128,8,128]{1,3,2,0:T(8,128)(2,1)} %get-tuple-element.245, s32[]{:T(128)} %get-tuple-element.228, bf16[4,640,128]{1,2,0:T(8,128)(2,1)} %get-tuple-element.244), kind=kOutput, calls=%fused_computation.65.clone.1 | convolution fusion | flops 170394240 | bytes 3134464 | tf_op jit(solution)/shard_map/while/body/eval_jaxpr/sub | solution.py:69
  64.6 2.0 %fusion.90 = bf16[8,128,640]{1,2,0:T(8,128)(2,1)S(1)} fusion(f32[8,128,640]{1,2,0:T(8,128)} %get-tuple-element.213, f32[8,128]{1,0:T(8,128)S(1)} %get-tuple-element.214), kind=kLoop, calls=%fused_computation.23.clone.1 | loop fusion | flops 1310720 | bytes 3936256 | tf_op jit(solution)/shard_map/while/body/eval_jaxpr/convert_element_type | solution.py:71
  66.7 0.7 fusion.91
  67.5 3.5 %fusion.92 = f32[4,640,128]{2,1,0:T(8,128)} fusion(f32[4,640,128]{2,1,0:T(8,128)} %get-tuple-element.229, s32[]{:T(128)} %get-tuple-element.228, f32[8,128]{1,0:T(8,128)S(1)} %bitcast.156, f32[8,128,640]{1,2,0:T(8,128)} %get-tuple-element.213, f32[8,128]{1,0:T(8,128)S(1)} %get-tuple-element.214, bf16[4,128,8,128]{1,3,2,0:T(8,128)(2,1)} %get-tuple-element.245, ...), kind=kOutput, calls=%fused_computation.19.clone.1 | convolution fusion | flops 338821120 | bytes 3647488 | tf_op jit(solution)/shard_map/while/body/eval_jaxpr/grk,rgd->kd/dot_general | solution.py:82
  71.0 1.2 fusion.93
  72.8 3.5 %fusion.89 = (f32[8,128]{1,0:T(8,128)S(1)}, f32[8,128,640]{1,2,0:T(8,128)}) fusion(pred[128,640]{0,1:T(8,128)(4,1)S(1)} %and_and_fusion.2, bf16[4,128,8,128]{1,3,2,0:T(8,128)(2,1)} %get-tuple-element.245, s32[]{:T(128)} %get-tuple-element.228, bf16[4,640,128]{1,2,0:T(8,128)(2,1)} %get-tuple-element.244), kind=kOutput, calls=%fused_computation.65.clone.1 | convolution fusion | flops 170394240 | bytes 3134464 | tf_op jit(solution)/shard_map/while/body/eval_jaxpr/sub | solution.py:69
  76.3 2.0 %fusion.90 = bf16[8,128,640]{1,2,0:T(8,128)(2,1)S(1)} fusion(f32[8,128,640]{1,2,0:T(8,128)} %get-tuple-element.213, f32[8,128]{1,0:T(8,128)S(1)} %get-tuple-element.214), kind=kLoop, calls=%fused_computation.23.clone.1 | loop fusion | flops 1310720 | bytes 3936256 | tf_op jit(solution)/shard_map/while/body/eval_jaxpr/convert_element_type | solution.py:71
  78.4 0.7 fusion.91
  79.2 3.5 %fusion.92 = f32[4,640,128]{2,1,0:T(8,128)} fusion(f32[4,640,128]{2,1,0:T(8,128)} %get-tuple-element.229, s32[]{:T(128)} %get-tuple-element.228, f32[8,128]{1,0:T(8,128)S(1)} %bitcast.156, f32[8,128,640]{1,2,0:T(8,128)} %get-tuple-element.213, f32[8,128]{1,0:T(8,128)S(1)} %get-tuple-element.214, bf16[4,128,8,128]{1,3,2,0:T(8,128)(2,1)} %get-tuple-element.245, ...), kind=kOutput, calls=%fused_computation.19.clone.1 | convolution fusion | flops 338821120 | bytes 3647488 | tf_op jit(solution)/shard_map/while/body/eval_jaxpr/grk,rgd->kd/dot_general | solution.py:82
  82.7 1.2 fusion.93
  83.9 1.9 %maximum_bitcast_fusion = f32[640,2,4,128]{3,0,2,1:T(8,128)S(1)} fusion(f32[1,4,640,128]{3,2,1,0:T(8,128)} %bitcast.146, f32[1,4,640,128]{3,2,1,0:T(8,128)} %bitcast.145), kind=kLoop, calls=%fused_computation.51 | loop fusion | flops 655360 | bytes 5242880 | tf_op jit(solution)/shard_map/transpose | solution.py:91
  86.0 0.3 copy.33
  86.6 5.2 %collective-permute-start.5 = (f32[128,1024]{1,0:T(8,128)S(1)}, f32[128,1024]{1,0:T(8,128)}, u32[]{:S(2)}, u32[]{:S(2)}) collective-permute-start(f32[128,1024]{1,0:T(8,128)S(1)} %squeeze.42), channel_id=1, source_target_pairs={{1,0},{2,1},{3,2},{4,3},{5,4},{6,5},{7,6},{9,8},{10,9},{11,10},{12... | collective-permute-start | bytes 1572872 | tf_op jit(solution)/shard_map/ppermute | solution.py:25
  91.8 0.3 copy.34
  92.1 1.0 squeeze.43
  93.1 1.9 %collective-permute-start.6 = (f32[128,1024]{1,0:T(8,128)}, f32[128,1024]{1,0:T(8,128)}, u32[]{:S(2)}, u32[]{:S(2)}) collective-permute-start(f32[128,1024]{1,0:T(8,128)} %squeeze.43), channel_id=1, source_target_pairs={{2,0},{3,1},{4,2},{5,3},{6,4},{7,5},{10,8},{11,9},{12,10},{13,11},... | collective-permute-start | bytes 1572872 | tf_op jit(solution)/shard_map/ppermute | solution.py:25
  95.6 1.3 collective-permute-start.7
  97.5 1.3 collective-permute-start.8
  98.8 0.3 copy.32
  99.3 1.8 %collective-permute-done.5 = f32[128,1024]{1,0:T(8,128)} collective-permute-done((f32[128,1024]{1,0:T(8,128)S(1)}, f32[128,1024]{1,0:T(8,128)}, u32[]{:S(2)}, u32[]{:S(2)}) %collective-permute-start.5) | collective-permute-done | bytes 524320 | tf_op jit(solution)/shard_map/ppermute | solution.py:25
  101.1 13.7 %collective-permute-done.6 = f32[128,1024]{1,0:T(8,128)} collective-permute-done((f32[128,1024]{1,0:T(8,128)}, f32[128,1024]{1,0:T(8,128)}, u32[]{:S(2)}, u32[]{:S(2)}) %collective-permute-start.6) | collective-permute-done | bytes 524320 | tf_op jit(solution)/shard_map/ppermute | solution.py:25
  114.8 3.4 %collective-permute-done.7 = f32[128,1024]{1,0:T(8,128)} collective-permute-done((f32[128,1024]{1,0:T(8,128)S(1)}, f32[128,1024]{1,0:T(8,128)}, u32[]{:S(2)}, u32[]{:S(2)}) %collective-permute-start.7) | collective-permute-done | bytes 524320 | tf_op jit(solution)/shard_map/ppermute | solution.py:25
  118.2 16.6 %collective-permute-done.8 = f32[128,1024]{1,0:T(8,128)S(1)} collective-permute-done((f32[128,1024]{1,0:T(8,128)S(1)}, f32[128,1024]{1,0:T(8,128)S(1)}, u32[]{:S(2)}, u32[]{:S(2)}) %collective-permute-start.8) | collective-permute-done | bytes 524320 | tf_op jit(solution)/shard_map/ppermute | solution.py:25
  134.8 2.2 %fusion.56 = bf16[1,128,1024]{2,1,0:T(8,128)(2,1)} fusion(f32[128,1024]{1,0:T(8,128)S(1)} %collective-permute-done.8, f32[128,1024]{1,0:T(8,128)} %collective-permute-done.7, f32[128,1024]{1,0:T(8,128)} %collective-permute-done.6, f32[128,1024]{1,0:T(8,128)S(1)} %squeeze.41, f32[128,1024]{1,0:T(8,128)} %collective-permute-done.5), kind=kLoop, calls=%fused_computation.55 | loop fusion | flops 655360 | bytes 2883584 | tf_op jit(solution)/shard_map/reshape | solution.py:96
  (67 shorter events, 5.1 us)
Async XLA Ops:
  0.0 26.0 %copy-start = (bf16[1,128,4096]{2,1,0:T(8,128)(2,1)S(1)}, bf16[1,128,4096]{2,1,0:T(8,128)(2,1)}, u32[]{:S(2)}) copy-start(bf16[1,128,4096]{2,1,0:T(8,128)(2,1)} %param.6) | copy-start | bytes 3145732
  1.2 14.5 %collective-permute-start = (bf16[1,128,1024]{1,2,0:T(8,128)(2,1)S(1)}, bf16[1,128,1024]{1,2,0:T(8,128)(2,1)S(1)}, u32[]{:S(2)}, u32[]{:S(2)}) collective-permute-start(bf16[1,128,1024]{1,2,0:T(8,128)(2,1)S(1)} %copy.25), channel_id=1, source_target_pairs={{0,16},{16,0},{8,24},{24,8},{1,17},{17,1},{9,25},{25,9},{2,18},{18... | collective-permute-start | bytes 786440 | tf_op jit(solution)/shard_map/ppermute | solution.py:19
  15.7 13.5 %collective-permute-start.1 = (bf16[128,1024]{0,1:T(8,128)(2,1)S(1)}, bf16[128,1024]{0,1:T(8,128)(2,1)S(1)}, u32[]{:S(2)}, u32[]{:S(2)}) collective-permute-start(bf16[128,1024]{0,1:T(8,128)(2,1)S(1)} %bitcast.147), channel_id=1, source_target_pairs={{0,4},{1,5},{2,6},{3,7},{8,12},{9,13},{10,14},{11,15},{16,20},{17,... | collective-permute-start | bytes 786440 | tf_op jit(solution)/shard_map/ppermute | solution.py:25
  20.0 9.3 %collective-permute-start.2 = (bf16[128,1024]{0,1:T(8,128)(2,1)S(1)}, bf16[128,1024]{0,1:T(8,128)(2,1)S(1)}, u32[]{:S(2)}, u32[]{:S(2)}) collective-permute-start(bf16[128,1024]{0,1:T(8,128)(2,1)S(1)} %bitcast.148), channel_id=1, source_target_pairs={{0,3},{1,4},{2,5},{3,6},{4,7},{8,11},{9,12},{10,13},{11,14},{12,15... | collective-permute-start | bytes 786440 | tf_op jit(solution)/shard_map/ppermute | solution.py:25
  21.4 12.7 %collective-permute-start.3 = (bf16[128,1024]{0,1:T(8,128)(2,1)S(1)}, bf16[128,1024]{0,1:T(8,128)(2,1)S(1)}, u32[]{:S(2)}, u32[]{:S(2)}) collective-permute-start(bf16[128,1024]{0,1:T(8,128)(2,1)S(1)} %bitcast.149), channel_id=1, source_target_pairs={{0,2},{1,3},{2,4},{3,5},{4,6},{5,7},{8,10},{9,11},{10,12},{11,13},... | collective-permute-start | bytes 786440 | tf_op jit(solution)/shard_map/ppermute | solution.py:25
  27.4 8.7 %collective-permute-start.4 = (bf16[128,1024]{0,1:T(8,128)(2,1)S(1)}, bf16[128,1024]{0,1:T(8,128)(2,1)S(1)}, u32[]{:S(2)}, u32[]{:S(2)}) collective-permute-start(bf16[128,1024]{0,1:T(8,128)(2,1)S(1)} %bitcast.150), channel_id=1, source_target_pairs={{0,1},{1,2},{2,3},{3,4},{4,5},{5,6},{6,7},{8,9},{9,10},{10,11},{11... | collective-permute-start | bytes 786440 | tf_op jit(solution)/shard_map/ppermute | solution.py:25
  37.1 0.5 copy-start.1
  37.1 4.0 %copy-start.3 = (s32[128]{0:T(128)}, s32[128]{0:T(128)S(1)}, u32[]{:S(2)}) copy-start(s32[128]{0:T(128)S(1)} %get-tuple-element.248) | copy-start | bytes 1540 | tf_op jit(solution)/shard_map/while
  47.6 1.2 copy-start.2
  47.6 1.2 copy-start.4
  48.8 0.5 copy-start.1
  48.8 4.0 %copy-start.3 = (s32[128]{0:T(128)}, s32[128]{0:T(128)S(1)}, u32[]{:S(2)}) copy-start(s32[128]{0:T(128)S(1)} %get-tuple-element.248) | copy-start | bytes 1540 | tf_op jit(solution)/shard_map/while
  59.3 1.2 copy-start.2
  59.3 1.2 copy-start.4
  60.5 0.5 copy-start.1
  60.5 4.0 %copy-start.3 = (s32[128]{0:T(128)}, s32[128]{0:T(128)S(1)}, u32[]{:S(2)}) copy-start(s32[128]{0:T(128)S(1)} %get-tuple-element.248) | copy-start | bytes 1540 | tf_op jit(solution)/shard_map/while
  71.0 1.2 copy-start.2
  71.0 1.2 copy-start.4
  72.2 0.5 copy-start.1
  72.2 4.0 %copy-start.3 = (s32[128]{0:T(128)}, s32[128]{0:T(128)S(1)}, u32[]{:S(2)}) copy-start(s32[128]{0:T(128)S(1)} %get-tuple-element.248) | copy-start | bytes 1540 | tf_op jit(solution)/shard_map/while
  82.7 1.2 copy-start.2
  82.7 1.2 copy-start.4
  86.6 14.5 %collective-permute-start.5 = (f32[128,1024]{1,0:T(8,128)S(1)}, f32[128,1024]{1,0:T(8,128)}, u32[]{:S(2)}, u32[]{:S(2)}) collective-permute-start(f32[128,1024]{1,0:T(8,128)S(1)} %squeeze.42), channel_id=1, source_target_pairs={{1,0},{2,1},{3,2},{4,3},{5,4},{6,5},{7,6},{9,8},{10,9},{11,10},{12... | collective-permute-start | bytes 1572872 | tf_op jit(solution)/shard_map/ppermute | solution.py:25
  93.1 21.7 %collective-permute-start.6 = (f32[128,1024]{1,0:T(8,128)}, f32[128,1024]{1,0:T(8,128)}, u32[]{:S(2)}, u32[]{:S(2)}) collective-permute-start(f32[128,1024]{1,0:T(8,128)} %squeeze.43), channel_id=1, source_target_pairs={{2,0},{3,1},{4,2},{5,3},{6,4},{7,5},{10,8},{11,9},{12,10},{13,11},... | collective-permute-start | bytes 1572872 | tf_op jit(solution)/shard_map/ppermute | solution.py:25
  95.6 22.6 %collective-permute-start.7 = (f32[128,1024]{1,0:T(8,128)S(1)}, f32[128,1024]{1,0:T(8,128)}, u32[]{:S(2)}, u32[]{:S(2)}) collective-permute-start(f32[128,1024]{1,0:T(8,128)S(1)} %squeeze.44), channel_id=1, source_target_pairs={{3,0},{4,1},{5,2},{6,3},{7,4},{11,8},{12,9},{13,10},{14,11},{15,12... | collective-permute-start | bytes 1572872 | tf_op jit(solution)/shard_map/ppermute | solution.py:25
  97.5 37.4 %collective-permute-start.8 = (f32[128,1024]{1,0:T(8,128)S(1)}, f32[128,1024]{1,0:T(8,128)S(1)}, u32[]{:S(2)}, u32[]{:S(2)}) collective-permute-start(f32[128,1024]{1,0:T(8,128)S(1)} %squeeze.45), channel_id=1, source_target_pairs={{4,0},{5,1},{6,2},{7,3},{12,8},{13,9},{14,10},{15,11},{20,16},{21,... | collective-permute-start | bytes 1572872 | tf_op jit(solution)/shard_map/ppermute | solution.py:25
where the time goes:
time: 138 us; the launch traced here: 137 us
  waiting for transfers between devices  56.2 us (41%)
  matrix products  35.8 us (26%)
  starting transfers between devices  19.7 us (14%)
  other arithmetic  14.2 us (10%)
  local copies, waits for them, and re-layouts  10.8 us (8%)
    ppermute x8, waiting for transfers between devices, from_behind(): lax.ppermute(value, axis, [(source, source + steps) for source in range(f...  42 us
    ppermute x8, starting transfers between devices, from_behind(): lax.ppermute(value, axis, [(source, source + steps) for source in range(f...  19.3 us
    ppermute x1, waiting for transfers between devices, from_partner(): return lax.ppermute(block, axis, route)  14.1 us
    sub x4, matrix products, head_grads(): raw_weights = jnp.exp(scores - row_top)  14 us
    dot_general x4, matrix products, head_grads(): jnp.einsum('grk,rgd->kd', dscores, query_block, preferred_element_type=jn...  14 us
    convert_element_type x4, other arithmetic, head_grads(): weights16 = weights.astype(jnp.bfloat16)  7.83 us
    dot_general x4, matrix products, head_grads(): jnp.einsum('grk,rgd->kd', weights16, cotangent, preferred_element_type=jn...  4.92 us
    unnamed x9, local copies, waits for them, and re-layouts  4.36 us
  transfers between devices with their start and end apart: 9, of which 7 were waited for; matrix products, arithmetic and copies ran while one was open for 5% of the time, Pallas kernels for 0%

commit v1 on v0

v1 whole, which is shorter than its diff:
```python
import functools
import math

import jax
import jax.numpy as jnp
from jax import lax
from jax.experimental import pallas as pl
from jax.experimental.pallas import tpu as pltpu
from jax.sharding import PartitionSpec as P

H = 32
KVH = 4
HD = 128
REACH = 5
GROUP = REACH - 1
SHARE = H // KVH
PARTS = ((0,), (1,), (2,), (3,))
MASKED = -1e30
F32 = jnp.float32
NT = (((1,), (1,)), ((), ()))
NN = (((1,), (0,)), ((), ()))


def rows_from(ref, first, size):
    return ref[pl.ds(pl.multiple_of(first, 16), size), :]


def doc_start(pos, len_ref):
    start = jnp.zeros_like(pos)
    end = jnp.int32(0)
    for doc in range(len_ref.shape[0]):
        end = end + len_ref[doc]
        start = jnp.where(end <= pos, end, start)
    return start


def bias_of(first_key, keys, query_pos, start):
    key_pos = first_key + lax.broadcasted_iota(jnp.int32, (keys, query_pos.shape[1]), 0)
    return jnp.where((key_pos >= start) & (key_pos <= query_pos), 0.0, MASKED)


def weigh(key, value, query, cot, bias, keep):
    scores = lax.dot_general(key, query, NT, preferred_element_type=F32) + bias
    top = jnp.max(scores, axis=0, keepdims=True)
    raw = jnp.exp2((scores - top) * (HD**-0.5 * math.log2(math.e)))
    weights = raw * (keep / jnp.sum(raw, axis=0, keepdims=True))
    dweights = lax.dot_general(value, cot, NT, preferred_element_type=F32)
    delta = jnp.sum(weights * dweights, axis=0, keepdims=True)
    dscores = weights * (dweights - delta)
    return weights.astype(jnp.bfloat16), dscores.astype(jnp.bfloat16)


def part_kernel(heads, rows, halo, *refs):
    (len_ref, q_ref, g_ref, qh_ref, gh_ref, own_ref, one_ref, two_ref, three_ref, *before_refs, after_ref,
     own_out, one_out, two_out, three_out, before_out, after_out, k_buf, v_buf, bias_ref, dk_ref, dv_ref) = refs
    count = len(heads)
    span = GROUP * rows
    me = lax.axis_index("ctx")
    rank = lax.rem(me, GROUP)
    group_first = (me - rank) * rows
    lane = lax.broadcasted_iota(jnp.int32, (1, rows), 1)
    query_pos = me * rows + lane
    start = doc_start(query_pos, len_ref)
    keep = jnp.where(start < group_first - halo, 0.0, 1.0)
    bias_ref[...] = bias_of(group_first - halo, halo + span, query_pos, start)
    keep2 = jnp.concatenate([keep, keep], axis=1)

    for at, head in enumerate(heads):
        k_cols, v_cols = pl.ds(at * HD, HD), pl.ds((count + at) * HD, HD)
        for step, ref in enumerate((own_ref, one_ref, two_ref, three_ref)):
            row = pl.multiple_of(halo + (rank ^ step) * rows, 16)
            k_buf[pl.ds(row, rows), :] = ref[:, k_cols]
            v_buf[pl.ds(row, rows), :] = ref[:, v_cols]
        all_k, all_v = pl.ds(head * HD, HD), pl.ds((KVH + head) * HD, HD)
        k_buf[:halo, :] = sum(ref[:, all_k] for ref in before_refs)
        v_buf[:halo, :] = sum(ref[:, all_v] for ref in before_refs)
        k_buf[halo + span :, :] = after_ref[:, all_k]
        v_buf[halo + span :, :] = after_ref[:, all_v]
        dk_ref[...] = jnp.zeros_like(dk_ref)
        dv_ref[...] = jnp.zeros_like(dv_ref)

        for case in range(GROUP):

            @pl.when(rank == case)
            def _():
                keys = halo + (case + 1) * rows

                def pair(index, carry):
                    col = at * SHARE * HD + index * 2 * HD
                    query = jnp.concatenate([q_ref[0, :, pl.ds(col + HD * i, HD)] for i in range(2)], axis=0)
                    cot = jnp.concatenate([g_ref[0, :, pl.ds(col + HD * i, HD)] for i in range(2)], axis=0)
                    bias = bias_ref[:keys, :]
                    weights, dscores = weigh(
                        k_buf[:keys, :], v_buf[:keys, :], query, cot, jnp.concatenate([bias, bias], axis=1), keep2
                    )
                    dv_ref[:keys, :] += lax.dot_general(weights, cot, NN, preferred_element_type=F32)
                    dk_ref[:keys, :] += lax.dot_general(dscores, query, NN, preferred_element_type=F32)
                    return carry

                lax.fori_loop(0, SHARE // 2, pair, 0)

        @pl.when(rank == 0)
        def _():
            wide = SHARE * halo
            next_pos = group_first + span + lax.rem(lax.broadcasted_iota(jnp.int32, (1, wide), 1), halo)
            next_start = doc_start(next_pos, len_ref)
            next_keep = jnp.where(next_start < group_first + span - halo, 1.0, 0.0)
            query = jnp.concatenate([qh_ref[:, pl.ds((at * SHARE + i) * HD, HD)] for i in range(SHARE)], axis=0)
            cot = jnp.concatenate([gh_ref[:, pl.ds((at * SHARE + i) * HD, HD)] for i in range(SHARE)], axis=0)
            weights, dscores = weigh(
                k_buf[halo:, :], v_buf[halo:, :], query, cot,
                bias_of(group_first, span + halo, next_pos, next_start), next_keep,
            )
            dv_ref[halo:, :] += lax.dot_general(weights, cot, NN, preferred_element_type=F32)
            dk_ref[halo:, :] += lax.dot_general(dscores, query, NN, preferred_element_type=F32)

        scale = HD**-0.5
        for step, ref in enumerate((own_out, one_out, two_out, three_out)):
            row = halo + (rank ^ step) * rows
            ref[:, k_cols] = (rows_from(dk_ref, row, rows) * scale).astype(ref.dtype)
            ref[:, v_cols] = rows_from(dv_ref, row, rows).astype(ref.dtype)
        for ref, row in ((before_out, 0), (after_out, halo + span)):
            ref[:, k_cols] = (dk_ref[row : row + halo, :] * scale).astype(ref.dtype)
            ref[:, v_cols] = dv_ref[row : row + halo, :].astype(ref.dtype)


def whole_block(shape):
    return pl.BlockSpec(shape, lambda i: (0,) * len(shape))


def part_grads(heads, halo, lengths, queries, grad_out, next_q, next_g, pieces, before, after):
    rows = queries.shape[1]
    count = len(heads)
    assert list(heads) == list(range(heads[0], heads[0] + count)) and heads[0] % count == 0
    wide = count * SHARE * HD
    nth = heads[0] // count
    kv = 2 * count * HD
    keys = halo + GROUP * rows + halo
    q_spec = pl.BlockSpec((1, rows, wide), lambda i: (0, 0, nth))
    h_spec = pl.BlockSpec((halo, wide), lambda i: (0, nth))
    out = [jax.ShapeDtypeStruct((rows, kv), F32)]
    out += [jax.ShapeDtypeStruct((rows, kv), jnp.bfloat16)] * 3
    out += [jax.ShapeDtypeStruct((halo, kv), jnp.bfloat16)] * 2
    flops = 8 * SHARE * count * rows * HD * (keys - halo)
    return pl.pallas_call(
        functools.partial(part_kernel, heads, rows, halo),
        grid=(1,),
        out_shape=out,
        in_specs=[pl.BlockSpec(memory_space=pltpu.SMEM), q_spec, q_spec, h_spec, h_spec]
        + [whole_block(piece.shape) for piece in pieces]
        + [whole_block(after.shape)] * (GROUP + 1),
        out_specs=[whole_block(o.shape) for o in out],
        scratch_shapes=[
            pltpu.VMEM((keys, HD), jnp.bfloat16),
            pltpu.VMEM((keys, HD), jnp.bfloat16),
            pltpu.VMEM((halo + GROUP * rows, rows), F32),
            pltpu.VMEM((keys, HD), F32),
            pltpu.VMEM((keys, HD), F32),
        ],
        compiler_params=pltpu.CompilerParams(vmem_limit_bytes=24 * 2**20),
        cost_estimate=pl.CostEstimate(flops=flops, bytes_accessed=2**20, transcendentals=0),
    )(lengths, queries, grad_out, next_q, next_g, *pieces, *before, after)


def sum_kernel(parts, halo, *refs):
    out_ref = refs[-1]
    at = 0
    rows = out_ref.shape[1]
    terms = len(parts) * 4
    ends = refs[terms:-1]
    for which, heads in enumerate(parts):
        own, one, two, three = refs[at : at + 4]
        at += 4
        count = len(heads)
        for half in range(2):
            for i, head in enumerate(heads):
                cols = pl.ds((half * count + i) * HD, HD)
                total = own[:, cols] + one[:, cols].astype(F32) + two[:, cols].astype(F32) + three[:, cols].astype(F32)
                low, high = total[:halo], total[rows - halo :]
                for ref in ends[: GROUP * len(parts)][which :: len(parts)]:
                    high = high + ref[:, cols].astype(F32)
                low = low + ends[GROUP * len(parts) + which][:, cols].astype(F32)
                total = jnp.concatenate([low, total[halo : rows - halo], high], axis=0)
                out_ref[0, :, pl.ds((half * KVH + head) * HD, HD)] = total.astype(out_ref.dtype)


def on_device(queries, stash, grad_out, lengths):
    rows = queries.shape[1]
    pipe, ctx = lax.axis_size("pipe"), lax.axis_size("ctx")
    halo = -(-lengths.shape[0] // 16) * 16
    high = 1 << (pipe.bit_length() - 2)
    both = ("pipe", "ctx")

    def partner(block, step):
        route = [
            ((p ^ high) * ctx + c, p * ctx + d)
            for p in range(pipe)
            for c in range(ctx)
            for d in [step(c)]
            if d is not None and 0 <= d < ctx
        ]
        return lax.ppermute(block, both, route)

    def along(block, pick):
        return lax.ppermute(block, "ctx", [(c, d) for c in range(ctx) for d in [pick(c)] if d is not None and 0 <= d < ctx])

    kv = stash[0]
    before = partner(kv[rows - halo :], lambda c: c + 1 if c % GROUP == GROUP - 1 else None)
    after = partner(kv[:halo], lambda c: c - GROUP if c % GROUP == 0 else None)
    next_q = along(queries[0, :halo], lambda c: c - GROUP if c % GROUP == 0 else None)
    next_g = along(grad_out[0, :halo], lambda c: c - GROUP if c % GROUP == 0 else None)
    held = []
    for heads in PARTS:
        first, count = heads[0], len(heads)
        block = jnp.concatenate(
            [kv[:, first * HD : (first + count) * HD], kv[:, (KVH + first) * HD : (KVH + first + count) * HD]], axis=1
        )
        held.append(partner(block, lambda c: c))
    before = [before] + [along(before, lambda c: c + step if c % GROUP == 0 else None) for step in range(1, GROUP)]
    terms, ends_before, ends_after = [], [], []
    for heads, own in zip(PARTS, held):
        pieces = [own] + [along(own, lambda c: c ^ step) for step in range(1, GROUP)]
        mine, *others, to_before, to_after = part_grads(
            heads, halo, lengths, queries, grad_out, next_q, next_g, pieces, before, after
        )
        terms += [mine] + [along(other, lambda c: c ^ step) for step, other in zip(range(1, GROUP), others)]
        ends_before.append(to_before)
        ends_after.append(to_after)
    width = [end.shape[1] for end in ends_before]
    all_before = jnp.concatenate(ends_before, axis=1)
    all_after = jnp.concatenate(ends_after, axis=1)
    ends = []
    for rank in range(GROUP):
        got = along(all_before, lambda c: c - rank - 1 if c % GROUP == rank else None)
        ends += jnp.split(got, [sum(width[: i + 1]) for i in range(len(width) - 1)], axis=1)
    got = along(all_after, lambda c: c + GROUP if c % GROUP == 0 else None)
    ends += jnp.split(got, [sum(width[: i + 1]) for i in range(len(width) - 1)], axis=1)
    return pl.pallas_call(
        functools.partial(sum_kernel, PARTS, halo),
        out_shape=jax.ShapeDtypeStruct((1, rows, kv.shape[1]), jnp.bfloat16),
        compiler_params=pltpu.CompilerParams(vmem_limit_bytes=16 * 2**20),
    )(*terms, *ends)


def solution(mesh):
    placed = (P("pipe", "ctx", None), P("pipe", "ctx", None), P("pipe", "ctx", None), P())
    return jax.shard_map(
        on_device, mesh=mesh, in_specs=placed, out_specs=P("pipe", "ctx", None), check_vma=False
    )
```

time: 138 us -> 79 us (0.57)
  the two profiles are of different devices: /device:TPU:26 before, /device:TPU:0 now
where the time goes in v1:
time: 79 us; the launch traced here: 78.5 us
  starting transfers between devices  49.7 us (63%)
  Pallas kernels  14.3 us (18%)
  waiting for transfers between devices  10.1 us (13%)
  local copies, waits for them, and re-layouts  3.96 us (5%)
    ppermute x34, starting transfers between devices, along(): lax.ppermute(block, 'ctx', [(c, d) for c in range(ctx) for d in [pick(c)]...  40.3 us
    pallas_call x4, Pallas kernels, part_grads(): pl.pallas_call(functools.partial(part_kernel, heads, rows, halo), grid=(1...  13.4 us
    ppermute x34, waiting for transfers between devices, along(): lax.ppermute(block, 'ctx', [(c, d) for c in range(ctx) for d in [pick(c)]...  10.1 us
    ppermute x6, starting transfers between devices, partner(): return lax.ppermute(block, both, route)  9.41 us
  transfers between devices with their start and end apart: 40, of which 9 were waited for; matrix products, arithmetic and copies ran while one was open for 2% of the time, Pallas kernels for 13%

profile of v1, /device:TPU:0, one launch (start us, length us, event | category | flops | bytes accessed | tf_op | source)
XLA Modules:
  0.0 78.5 jit_solution(6285287886520851233)
XLA Ops:
  0.0 0.9 %slice_bitcast_fusion.2 = (bf16[16,1024]{1,0:T(8,128)(2,1)S(1)}, bf16[16,1024]{1,0:T(8,128)(2,1)S(1)}) fusion(bf16[1,128,1024]{2,1,0:T(8,128)(2,1)} %param.5), kind=kLoop, calls=%fused_computation.7 | loop fusion | bytes 131072 | tf_op jit(solution)/shard_map/slice | solution.py:209
  0.9 1.3 %collective-permute-start.10 = (bf16[16,1024]{1,0:T(8,128)(2,1)S(1)}, bf16[16,1024]{1,0:T(8,128)(2,1)S(1)}, u32[]{:S(2)}, u32[]{:S(2)}) collective-permute-start(bf16[16,1024]{1,0:T(8,128)(2,1)S(1)} %get-tuple-element.61), channel_id=1, source_target_pairs={{20,0},{28,8},{4,16},{12,24}} | collective-permute-start | bytes 98312 | tf_op jit(solution)/shard_map/ppermute | solution.py:202
  2.2 0.7 collective-permute-start.6
  2.8 0.9 %fusion = (bf16[128,128]{1,0:T(8,128)(2,1)S(1)}, bf16[128,128]{1,0:T(8,128)(2,1)S(1)}, bf16[128,128]{1,0:T(8,128)(2,1)S(1)}, bf16[128,128]{1,0:T(8,128)(2,1)S(1)...) fusion(bf16[128,1024]{1,0:T(8,128)(2,1)} %bitcast.9), kind=kLoop, calls=%fused_computation.13 | loop fusion | bytes 524288 | tf_op jit(solution)/shard_map/slice | solution.py:216
  3.8 4.1 %collective-permute-start.2 = (bf16[128,256]{1,0:T(8,128)(2,1)S(1)}, bf16[128,256]{1,0:T(8,128)(2,1)S(1)}, u32[]{:S(2)}, u32[]{:S(2)}) collective-permute-start(bf16[128,256]{1,0:T(8,128)(2,1)S(1)} %pad_maximum_fusion), channel_id=1, source_target_pairs={{16,0},{17,1},{18,2},{19,3},{20,4},{21,5},{22,6},{23,7},{24,8},{25... | collective-permute-start | bytes 196616 | tf_op jit(solution)/shard_map/ppermute | solution.py:202
  7.9 0.1 collective-permute-start.14
  8.0 3.0 %collective-permute-start.21 = (bf16[128,256]{1,0:T(8,128)(2,1)S(1)}, bf16[128,256]{1,0:T(8,128)(2,1)S(1)}, u32[]{:S(2)}, u32[]{:S(2)}) collective-permute-start(bf16[128,256]{1,0:T(8,128)(2,1)S(1)} %pad_maximum_fusion.2), channel_id=1, source_target_pairs={{16,0},{17,1},{18,2},{19,3},{20,4},{21,5},{22,6},{23,7},{24,8},{25... | collective-permute-start | bytes 196616 | tf_op jit(solution)/shard_map/ppermute | solution.py:202
  10.9 7.9 %collective-permute-start.9 = (bf16[16,1024]{1,0:T(8,128)(2,1)S(1)}, bf16[16,1024]{1,0:T(8,128)(2,1)S(1)}, u32[]{:S(2)}, u32[]{:S(2)}) collective-permute-start(bf16[16,1024]{1,0:T(8,128)(2,1)S(1)} %collective-permute-done.6.refs_9_), channel_id=1, source_target_pairs={{0,3},{4,7},{8,11},{12,15},{16,19},{20,23},{24,27},{28,31}} | collective-permute-start | bytes 98312 | tf_op jit(solution)/shard_map/ppermute | solution.py:205
  18.9 1.3 %collective-permute-start.8 = (bf16[16,1024]{1,0:T(8,128)(2,1)S(1)}, bf16[16,1024]{1,0:T(8,128)(2,1)S(1)}, u32[]{:S(2)}, u32[]{:S(2)}) collective-permute-start(bf16[16,1024]{1,0:T(8,128)(2,1)S(1)} %collective-permute-done.6.refs_9_), channel_id=1, source_target_pairs={{0,2},{4,6},{8,10},{12,14},{16,18},{20,22},{24,26},{28,30}} | collective-permute-start | bytes 98312 | tf_op jit(solution)/shard_map/ppermute | solution.py:205
  20.2 0.2 collective-permute-done.9.refs_12_
  20.4 1.3 %collective-permute-start.7 = (bf16[16,1024]{1,0:T(8,128)(2,1)S(1)}, bf16[16,1024]{1,0:T(8,128)(2,1)S(1)}, u32[]{:S(2)}, u32[]{:S(2)}) collective-permute-start(bf16[16,1024]{1,0:T(8,128)(2,1)S(1)} %collective-permute-done.6.refs_9_), channel_id=1, source_target_pairs={{0,1},{4,5},{8,9},{12,13},{16,17},{20,21},{24,25},{28,29}} | collective-permute-start | bytes 98312 | tf_op jit(solution)/shard_map/ppermute | solution.py:205
  21.7 0.9 %slice_bitcast_fusion = bf16[16,4096]{1,0:T(8,128)(2,1)S(1)} fusion(bf16[1,128,4096]{2,1,0:T(8,128)(2,1)} %refs_2_.7), kind=kLoop, calls=%fused_computation | loop fusion | bytes 262144 | tf_op jit(solution)/shard_map/squeeze | solution.py:211
  22.7 1.3 %collective-permute-start.1 = (bf16[16,4096]{1,0:T(8,128)(2,1)S(1)}, bf16[16,4096]{1,0:T(8,128)(2,1)S(1)}, u32[]{:S(2)}, u32[]{:S(2)}) collective-permute-start(bf16[16,4096]{1,0:T(8,128)(2,1)S(1)} %slice_bitcast_fusion), channel_id=1, source_target_pairs={{4,0},{12,8},{20,16},{28,24}} | collective-permute-start | bytes 393224 | tf_op jit(solution)/shard_map/ppermute | solution.py:205
  24.0 1.3 %collective-permute-start = (bf16[16,4096]{1,0:T(8,128)(2,1)S(1)}, bf16[16,4096]{1,0:T(8,128)(2,1)S(1)}, u32[]{:S(2)}, u32[]{:S(2)}) collective-permute-start(bf16[16,4096]{1,0:T(8,128)(2,1)S(1)} %slice_bitcast_fusion.1), channel_id=1, source_target_pairs={{4,0},{12,8},{20,16},{28,24}} | collective-permute-start | bytes 393224 | tf_op jit(solution)/shard_map/ppermute | solution.py:205
  25.4 0.2 collective-permute-start.4
  25.6 1.6 %collective-permute-start.3 = (bf16[128,256]{1,0:T(8,128)(2,1)S(1)}, bf16[128,256]{1,0:T(8,128)(2,1)S(1)}, u32[]{:S(2)}, u32[]{:S(2)}) collective-permute-start(bf16[128,256]{1,0:T(8,128)(2,1)S(1)} %collective-permute-done.2.refs_5_), channel_id=1, source_target_pairs={{0,1},{1,0},{2,3},{3,2},{4,5},{5,4},{6,7},{7,6},{8,9},{9,8},{10,11... | collective-permute-start | bytes 196616 | tf_op jit(solution)/shard_map/ppermute | solution.py:205
  27.2 2.3 %collective-permute-done.1.refs_4_ = bf16[16,4096]{1,0:T(8,128)(2,1)S(1)} collective-permute-done((bf16[16,4096]{1,0:T(8,128)(2,1)S(1)}, bf16[16,4096]{1,0:T(8,128)(2,1)S(1)}, u32[]{:S(2)}, u32[]{:S(2)}) %collective-permute-start.1) | collective-permute-done | bytes 131104 | tf_op jit(solution)/shard_map/ppermute | solution.py:205
  29.5 0.3 collective-permute-start.28
  29.8 1.1 %collective-permute-done.refs_3_ = bf16[16,4096]{1,0:T(8,128)(2,1)S(1)} collective-permute-done((bf16[16,4096]{1,0:T(8,128)(2,1)S(1)}, bf16[16,4096]{1,0:T(8,128)(2,1)S(1)}, u32[]{:S(2)}, u32[]{:S(2)}) %collective-permute-start) | collective-permute-done | bytes 131104 | tf_op jit(solution)/shard_map/ppermute | solution.py:205
  31.0 1.8 %collective-permute-start.15 = (bf16[128,256]{1,0:T(8,128)(2,1)S(1)}, bf16[128,256]{1,0:T(8,128)(2,1)S(1)}, u32[]{:S(2)}, u32[]{:S(2)}) collective-permute-start(bf16[128,256]{1,0:T(8,128)(2,1)S(1)} %collective-permute-done.14.refs_5_), channel_id=1, source_target_pairs={{0,1},{1,0},{2,3},{3,2},{4,5},{5,4},{6,7},{7,6},{8,9},{9,8},{10,11... | collective-permute-start | bytes 196616 | tf_op jit(solution)/shard_map/ppermute | solution.py:205
  32.8 0.3 collective-permute-start.24
  33.1 1.2 %copy-done.1 = bf16[1,128,4096]{2,1,0:T(8,128)(2,1)S(1)} copy-done((bf16[1,128,4096]{2,1,0:T(8,128)(2,1)S(1)}, bf16[1,128,4096]{2,1,0:T(8,128)(2,1)}, u32[]{:S(2)}) %copy-start.1) | copy-done | bytes 1048600
  34.3 3.3 %shard_map.46 = (f32[128,256]{1,0:T(8,128)S(1)}, bf16[128,256]{1,0:T(8,128)(2,1)S(1)}, bf16[128,256]{1,0:T(8,128)(2,1)S(1)}, bf16[128,256]{1,0:T(8,128)(2,1)S(1)...) custom-call(s32[2]{0:T(128)S(1)} %copy-done.2, bf16[1,128,4096]{2,1,0:T(8,128)(2,1)S(1)} %copy-done, ...), custom_call_target="tpu_custom_call" | custom-call | flops 553648128 | bytes 1048576 | tf_op jit(solution)/shard_map/pallas_call | solution.py:145
  37.7 1.7 %collective-permute-start.23 = (bf16[128,256]{1,0:T(8,128)(2,1)S(1)}, bf16[128,256]{1,0:T(8,128)(2,1)S(1)}, u32[]{:S(2)}, u32[]{:S(2)}) collective-permute-start(bf16[128,256]{1,0:T(8,128)(2,1)S(1)} %collective-permute-done.21.refs_5_), channel_id=1, source_target_pairs={{0,2},{1,3},{2,0},{3,1},{4,6},{5,7},{6,4},{7,5},{8,10},{9,11},{10,... | collective-permute-start | bytes 196616 | tf_op jit(solution)/shard_map/ppermute | solution.py:205
  39.3 0.7 collective-permute-start.22
  40.1 1.6 %collective-permute-start.30 = (bf16[128,256]{1,0:T(8,128)(2,1)S(1)}, bf16[128,256]{1,0:T(8,128)(2,1)S(1)}, u32[]{:S(2)}, u32[]{:S(2)}) collective-permute-start(bf16[128,256]{1,0:T(8,128)(2,1)S(1)} %collective-permute-done.28.refs_5_), channel_id=1, source_target_pairs={{0,2},{1,3},{2,0},{3,1},{4,6},{5,7},{6,4},{7,5},{8,10},{9,11},{10,... | collective-permute-start | bytes 196616 | tf_op jit(solution)/shard_map/ppermute | solution.py:205
  41.7 3.3 %shard_map.47 = (f32[128,256]{1,0:T(8,128)S(1)}, bf16[128,256]{1,0:T(8,128)(2,1)S(1)}, bf16[128,256]{1,0:T(8,128)(2,1)S(1)}, bf16[128,256]{1,0:T(8,128)(2,1)S(1)...) custom-call(s32[2]{0:T(128)S(1)} %copy-done.2, bf16[1,128,4096]{2,1,0:T(8,128)(2,1)S(1)} %copy-done, ...), custom_call_target="tpu_custom_call" | custom-call | flops 553648128 | bytes 1048576 | tf_op jit(solution)/shard_map/pallas_call | solution.py:145
  45.1 3.3 %shard_map.48 = (f32[128,256]{1,0:T(8,128)S(1)}, bf16[128,256]{1,0:T(8,128)(2,1)S(1)}, bf16[128,256]{1,0:T(8,128)(2,1)S(1)}, bf16[128,256]{1,0:T(8,128)(2,1)S(1)...) custom-call(s32[2]{0:T(128)S(1)} %copy-done.2, bf16[1,128,4096]{2,1,0:T(8,128)(2,1)S(1)} %copy-done, ...), custom_call_target="tpu_custom_call" | custom-call | flops 553648128 | bytes 1048576 | tf_op jit(solution)/shard_map/pallas_call | solution.py:145
  48.5 3.5 %shard_map.49 = (f32[128,256]{1,0:T(8,128)S(1)}, bf16[128,256]{1,0:T(8,128)(2,1)S(1)}, bf16[128,256]{1,0:T(8,128)(2,1)S(1)}, bf16[128,256]{1,0:T(8,128)(2,1)S(1)...) custom-call(s32[2]{0:T(128)S(1)} %copy-done.2, bf16[1,128,4096]{2,1,0:T(8,128)(2,1)S(1)} %copy-done, ...), custom_call_target="tpu_custom_call" | custom-call | flops 553648128 | bytes 1048576 | tf_op jit(solution)/shard_map/pallas_call | solution.py:145
  52.0 0.7 collective-permute-start.38
  52.7 0.7 collective-permute-start.37
  53.3 0.7 collective-permute-start.36
  54.0 0.7 collective-permute-start.35
  54.8 5.1 %collective-permute-start.33 = (bf16[128,256]{1,0:T(8,128)(2,1)S(1)}, bf16[128,256]{1,0:T(8,128)(2,1)S(1)}, u32[]{:S(2)}, u32[]{:S(2)}) collective-permute-start(bf16[128,256]{1,0:T(8,128)(2,1)S(1)} %get-tuple-element.43), channel_id=1, source_target_pairs={{0,2},{1,3},{2,0},{3,1},{4,6},{5,7},{6,4},{7,5},{8,10},{9,11},{10,... | collective-permute-start | bytes 196616 | tf_op jit(solution)/shard_map/ppermute | solution.py:205
  59.9 0.9 %collective-permute-start.34 = (bf16[128,256]{1,0:T(8,128)(2,1)S(1)}, bf16[128,256]{1,0:T(8,128)(2,1)S(1)}, u32[]{:S(2)}, u32[]{:S(2)}) collective-permute-start(bf16[128,256]{1,0:T(8,128)(2,1)S(1)} %get-tuple-element.44), channel_id=1, source_target_pairs={{0,3},{1,2},{2,1},{3,0},{4,7},{5,6},{6,5},{7,4},{8,11},{9,10},{10,... | collective-permute-start | bytes 196616 | tf_op jit(solution)/shard_map/ppermute | solution.py:205
  60.8 4.6 %collective-permute-start.39 = (bf16[16,1024]{1,0:T(8,128)(2,1)S(1)}, bf16[16,1024]{1,0:T(8,128)(2,1)S(1)}, u32[]{:S(2)}, u32[]{:S(2)}) collective-permute-start(bf16[16,1024]{1,0:T(8,128)(2,1)S(1)} %pad_maximum_fusion.4), channel_id=1, source_target_pairs={{0,4},{8,12},{16,20},{24,28}} | collective-permute-start | bytes 98312 | tf_op jit(solution)/shard_map/ppermute | solution.py:205
  65.5 1.5 %collective-permute-done.39 = bf16[16,1024]{1,0:T(8,128)(2,1)S(1)} collective-permute-done((bf16[16,1024]{1,0:T(8,128)(2,1)S(1)}, bf16[16,1024]{1,0:T(8,128)(2,1)S(1)}, u32[]{:S(2)}, u32[]{:S(2)}) %collective-permute-start.39) | collective-permute-done | bytes 32800 | tf_op jit(solution)/shard_map/ppermute | solution.py:205
  67.0 0.4 collective-permute-start.27
  67.4 1.8 %collective-permute-start.18 = (bf16[128,256]{1,0:T(8,128)(2,1)S(1)}, bf16[128,256]{1,0:T(8,128)(2,1)S(1)}, u32[]{:S(2)}, u32[]{:S(2)}) collective-permute-start(bf16[128,256]{1,0:T(8,128)(2,1)S(1)} %get-tuple-element.34), channel_id=1, source_target_pairs={{0,1},{1,0},{2,3},{3,2},{4,5},{5,4},{6,7},{7,6},{8,9},{9,8},{10,11... | collective-permute-start | bytes 196616 | tf_op jit(solution)/shard_map/ppermute | solution.py:205
  69.2 1.4 %collective-permute-start.20 = (bf16[128,256]{1,0:T(8,128)(2,1)S(1)}, bf16[128,256]{1,0:T(8,128)(2,1)S(1)}, u32[]{:S(2)}, u32[]{:S(2)}) collective-permute-start(bf16[128,256]{1,0:T(8,128)(2,1)S(1)} %get-tuple-element.36), channel_id=1, source_target_pairs={{0,3},{1,2},{2,1},{3,0},{4,7},{5,6},{6,5},{7,4},{8,11},{9,10},{10,... | collective-permute-start | bytes 196616 | tf_op jit(solution)/shard_map/ppermute | solution.py:205
  70.6 0.8 %collective-permute-done.26.refs_10_ = bf16[128,256]{1,0:T(8,128)(2,1)S(1)} collective-permute-done((bf16[128,256]{1,0:T(8,128)(2,1)S(1)}, bf16[128,256]{1,0:T(8,128)(2,1)S(1)}, u32[]{:S(2)}, u32[]{:S(2)}) %collective-permute-start.26) | collective-permute-done | bytes 65568 | tf_op jit(solution)/shard_map/ppermute | solution.py:205
  71.4 1.3 %collective-permute-start.12 = (bf16[128,256]{1,0:T(8,128)(2,1)S(1)}, bf16[128,256]{1,0:T(8,128)(2,1)S(1)}, u32[]{:S(2)}, u32[]{:S(2)}) collective-permute-start(bf16[128,256]{1,0:T(8,128)(2,1)S(1)} %get-tuple-element.31), channel_id=1, source_target_pairs={{0,2},{1,3},{2,0},{3,1},{4,6},{5,7},{6,4},{7,5},{8,10},{9,11},{10,... | collective-permute-start | bytes 196616 | tf_op jit(solution)/shard_map/ppermute | solution.py:205
  72.7 0.8 %collective-permute-start.13 = (bf16[128,256]{1,0:T(8,128)(2,1)S(1)}, bf16[128,256]{1,0:T(8,128)(2,1)S(1)}, u32[]{:S(2)}, u32[]{:S(2)}) collective-permute-start(bf16[128,256]{1,0:T(8,128)(2,1)S(1)} %get-tuple-element.32), channel_id=1, source_target_pairs={{0,3},{1,2},{2,1},{3,0},{4,7},{5,6},{6,5},{7,4},{8,11},{9,10},{10,... | collective-permute-start | bytes 196616 | tf_op jit(solution)/shard_map/ppermute | solution.py:205
  73.5 0.5 collective-permute-done.19.refs_6_
  74.1 0.3 collective-permute-done.20.refs_7_
  74.3 2.0 %collective-permute-done.12.refs_2_ = bf16[128,256]{1,0:T(8,128)(2,1)S(1)} collective-permute-done((bf16[128,256]{1,0:T(8,128)(2,1)S(1)}, bf16[128,256]{1,0:T(8,128)(2,1)S(1)}, u32[]{:S(2)}, u32[]{:S(2)}) %collective-permute-start.12) | collective-permute-done | bytes 65568 | tf_op jit(solution)/shard_map/ppermute | solution.py:205
  76.4 1.3 %collective-permute-done.13.refs_3_ = bf16[128,256]{1,0:T(8,128)(2,1)S(1)} collective-permute-done((bf16[128,256]{1,0:T(8,128)(2,1)S(1)}, bf16[128,256]{1,0:T(8,128)(2,1)S(1)}, u32[]{:S(2)}, u32[]{:S(2)}) %collective-permute-start.13) | collective-permute-done | bytes 65568 | tf_op jit(solution)/shard_map/ppermute | solution.py:205
  77.7 0.9 %shard_map.50 = bf16[1,128,1024]{2,1,0:T(8,128)(2,1)} custom-call(f32[128,256]{1,0:T(8,128)S(1)} %get-tuple-element.29.refs_0_, bf16[128,256]{1,0:T(8,128)(2,1)S(1)} %collective-permute-done.11.refs_1_, bf16[128,256]{1,0:T(8,128)(2,1)S(1)} %collective-permute-done.12.refs_2_, bf16[128,256]{1,0:T(8,128)(2,1)S(1)} %collective-permute-done.13.refs_3_, ...), custom_call_target="tpu_custom_call" | custom-call | tf_op jit(solution)/shard_map/pallas_call | solution.py:238
  (61 shorter events, 0.6 us)
Async XLA Ops:
  0.0 18.9 %copy-start = (bf16[1,128,4096]{2,1,0:T(8,128)(2,1)S(1)}, bf16[1,128,4096]{2,1,0:T(8,128)(2,1)}, u32[]{:S(2)}) copy-start(bf16[1,128,4096]{2,1,0:T(8,128)(2,1)} %refs_1_.7) | copy-start | bytes 3145732
  0.9 18.0 %collective-permute-start.10 = (bf16[16,1024]{1,0:T(8,128)(2,1)S(1)}, bf16[16,1024]{1,0:T(8,128)(2,1)S(1)}, u32[]{:S(2)}, u32[]{:S(2)}) collective-permute-start(bf16[16,1024]{1,0:T(8,128)(2,1)S(1)} %get-tuple-element.61), channel_id=1, source_target_pairs={{20,0},{28,8},{4,16},{12,24}} | collective-permute-start | bytes 98312 | tf_op jit(solution)/shard_map/ppermute | solution.py:202
  2.2 8.8 %collective-permute-start.6 = (bf16[16,1024]{1,0:T(8,128)(2,1)S(1)}, bf16[16,1024]{1,0:T(8,128)(2,1)S(1)}, u32[]{:S(2)}, u32[]{:S(2)}) collective-permute-start(bf16[16,1024]{1,0:T(8,128)(2,1)S(1)} %get-tuple-element.62), channel_id=1, source_target_pairs={{19,4},{27,12},{3,20},{11,28}} | collective-permute-start | bytes 98312 | tf_op jit(solution)/shard_map/ppermute | solution.py:202
  3.8 21.5 %collective-permute-start.2 = (bf16[128,256]{1,0:T(8,128)(2,1)S(1)}, bf16[128,256]{1,0:T(8,128)(2,1)S(1)}, u32[]{:S(2)}, u32[]{:S(2)}) collective-permute-start(bf16[128,256]{1,0:T(8,128)(2,1)S(1)} %pad_maximum_fusion), channel_id=1, source_target_pairs={{16,0},{17,1},{18,2},{19,3},{20,4},{21,5},{22,6},{23,7},{24,8},{25... | collective-permute-start | bytes 196616 | tf_op jit(solution)/shard_map/ppermute | solution.py:202
  7.9 17.5 %collective-permute-start.14 = (bf16[128,256]{1,0:T(8,128)(2,1)S(1)}, bf16[128,256]{1,0:T(8,128)(2,1)S(1)}, u32[]{:S(2)}, u32[]{:S(2)}) collective-permute-start(bf16[128,256]{1,0:T(8,128)(2,1)S(1)} %pad_maximum_fusion.1), channel_id=1, source_target_pairs={{16,0},{17,1},{18,2},{19,3},{20,4},{21,5},{22,6},{23,7},{24,8},{25... | collective-permute-start | bytes 196616 | tf_op jit(solution)/shard_map/ppermute | solution.py:202
  8.0 17.7 %collective-permute-start.21 = (bf16[128,256]{1,0:T(8,128)(2,1)S(1)}, bf16[128,256]{1,0:T(8,128)(2,1)S(1)}, u32[]{:S(2)}, u32[]{:S(2)}) collective-permute-start(bf16[128,256]{1,0:T(8,128)(2,1)S(1)} %pad_maximum_fusion.2), channel_id=1, source_target_pairs={{16,0},{17,1},{18,2},{19,3},{20,4},{21,5},{22,6},{23,7},{24,8},{25... | collective-permute-start | bytes 196616 | tf_op jit(solution)/shard_map/ppermute | solution.py:202
  10.9 9.5 %collective-permute-start.9 = (bf16[16,1024]{1,0:T(8,128)(2,1)S(1)}, bf16[16,1024]{1,0:T(8,128)(2,1)S(1)}, u32[]{:S(2)}, u32[]{:S(2)}) collective-permute-start(bf16[16,1024]{1,0:T(8,128)(2,1)S(1)} %collective-permute-done.6.refs_9_), channel_id=1, source_target_pairs={{0,3},{4,7},{8,11},{12,15},{16,19},{20,23},{24,27},{28,31}} | collective-permute-start | bytes 98312 | tf_op jit(solution)/shard_map/ppermute | solution.py:205
  18.9 3.7 %collective-permute-start.8 = (bf16[16,1024]{1,0:T(8,128)(2,1)S(1)}, bf16[16,1024]{1,0:T(8,128)(2,1)S(1)}, u32[]{:S(2)}, u32[]{:S(2)}) collective-permute-start(bf16[16,1024]{1,0:T(8,128)(2,1)S(1)} %collective-permute-done.6.refs_9_), channel_id=1, source_target_pairs={{0,2},{4,6},{8,10},{12,14},{16,18},{20,22},{24,26},{28,30}} | collective-permute-start | bytes 98312 | tf_op jit(solution)/shard_map/ppermute | solution.py:205
  20.4 3.5 %collective-permute-start.7 = (bf16[16,1024]{1,0:T(8,128)(2,1)S(1)}, bf16[16,1024]{1,0:T(8,128)(2,1)S(1)}, u32[]{:S(2)}, u32[]{:S(2)}) collective-permute-start(bf16[16,1024]{1,0:T(8,128)(2,1)S(1)} %collective-permute-done.6.refs_9_), channel_id=1, source_target_pairs={{0,1},{4,5},{8,9},{12,13},{16,17},{20,21},{24,25},{28,29}} | collective-permute-start | bytes 98312 | tf_op jit(solution)/shard_map/ppermute | solution.py:205
  22.7 6.9 %collective-permute-start.1 = (bf16[16,4096]{1,0:T(8,128)(2,1)S(1)}, bf16[16,4096]{1,0:T(8,128)(2,1)S(1)}, u32[]{:S(2)}, u32[]{:S(2)}) collective-permute-start(bf16[16,4096]{1,0:T(8,128)(2,1)S(1)} %slice_bitcast_fusion), channel_id=1, source_target_pairs={{4,0},{12,8},{20,16},{28,24}} | collective-permute-start | bytes 393224 | tf_op jit(solution)/shard_map/ppermute | solution.py:205
  24.0 7.0 %collective-permute-start = (bf16[16,4096]{1,0:T(8,128)(2,1)S(1)}, bf16[16,4096]{1,0:T(8,128)(2,1)S(1)}, u32[]{:S(2)}, u32[]{:S(2)}) collective-permute-start(bf16[16,4096]{1,0:T(8,128)(2,1)S(1)} %slice_bitcast_fusion.1), channel_id=1, source_target_pairs={{4,0},{12,8},{20,16},{28,24}} | collective-permute-start | bytes 393224 | tf_op jit(solution)/shard_map/ppermute | solution.py:205
  25.3 5.7 %collective-permute-start.5 = (bf16[128,256]{1,0:T(8,128)(2,1)S(1)}, bf16[128,256]{1,0:T(8,128)(2,1)S(1)}, u32[]{:S(2)}, u32[]{:S(2)}) collective-permute-start(bf16[128,256]{1,0:T(8,128)(2,1)S(1)} %collective-permute-done.2.refs_5_), channel_id=1, source_target_pairs={{0,3},{1,2},{2,1},{3,0},{4,7},{5,6},{6,5},{7,4},{8,11},{9,10},{10,... | collective-permute-start | bytes 196616 | tf_op jit(solution)/shard_map/ppermute | solution.py:205
  25.4 5.6 %collective-permute-start.4 = (bf16[128,256]{1,0:T(8,128)(2,1)S(1)}, bf16[128,256]{1,0:T(8,128)(2,1)S(1)}, u32[]{:S(2)}, u32[]{:S(2)}) collective-permute-start(bf16[128,256]{1,0:T(8,128)(2,1)S(1)} %collective-permute-done.2.refs_5_), channel_id=1, source_target_pairs={{0,2},{1,3},{2,0},{3,1},{4,6},{5,7},{6,4},{7,5},{8,10},{9,11},{10,... | collective-permute-start | bytes 196616 | tf_op jit(solution)/shard_map/ppermute | solution.py:205
  25.6 7.2 %collective-permute-start.3 = (bf16[128,256]{1,0:T(8,128)(2,1)S(1)}, bf16[128,256]{1,0:T(8,128)(2,1)S(1)}, u32[]{:S(2)}, u32[]{:S(2)}) collective-permute-start(bf16[128,256]{1,0:T(8,128)(2,1)S(1)} %collective-permute-done.2.refs_5_), channel_id=1, source_target_pairs={{0,1},{1,0},{2,3},{3,2},{4,5},{5,4},{6,7},{7,6},{8,9},{9,8},{10,11... | collective-permute-start | bytes 196616 | tf_op jit(solution)/shard_map/ppermute | solution.py:205
  27.2 5.9 %copy-start.2 = (s32[2]{0:T(128)S(1)}, s32[2]{0:T(128)}, u32[]{:S(2)}) copy-start(s32[2]{0:T(128)} %refs_0_.7) | copy-start | bytes 28
  29.5 8.1 %collective-permute-start.28 = (bf16[128,256]{1,0:T(8,128)(2,1)S(1)}, bf16[128,256]{1,0:T(8,128)(2,1)S(1)}, u32[]{:S(2)}, u32[]{:S(2)}) collective-permute-start(bf16[128,256]{1,0:T(8,128)(2,1)S(1)} %pad_maximum_fusion.3), channel_id=1, source_target_pairs={{16,0},{17,1},{18,2},{19,3},{20,4},{21,5},{22,6},{23,7},{24,8},{25... | collective-permute-start | bytes 196616 | tf_op jit(solution)/shard_map/ppermute | solution.py:202
  30.9 8.4 %collective-permute-start.17 = (bf16[128,256]{1,0:T(8,128)(2,1)S(1)}, bf16[128,256]{1,0:T(8,128)(2,1)S(1)}, u32[]{:S(2)}, u32[]{:S(2)}) collective-permute-start(bf16[128,256]{1,0:T(8,128)(2,1)S(1)} %collective-permute-done.14.refs_5_), channel_id=1, source_target_pairs={{0,3},{1,2},{2,1},{3,0},{4,7},{5,6},{6,5},{7,4},{8,11},{9,10},{10,... | collective-permute-start | bytes 196616 | tf_op jit(solution)/shard_map/ppermute | solution.py:205
  30.9 9.1 %collective-permute-start.16 = (bf16[128,256]{1,0:T(8,128)(2,1)S(1)}, bf16[128,256]{1,0:T(8,128)(2,1)S(1)}, u32[]{:S(2)}, u32[]{:S(2)}) collective-permute-start(bf16[128,256]{1,0:T(8,128)(2,1)S(1)} %collective-permute-done.14.refs_5_), channel_id=1, source_target_pairs={{0,2},{1,3},{2,0},{3,1},{4,6},{5,7},{6,4},{7,5},{8,10},{9,11},{10,... | collective-permute-start | bytes 196616 | tf_op jit(solution)/shard_map/ppermute | solution.py:205
  31.0 9.1 %collective-permute-start.15 = (bf16[128,256]{1,0:T(8,128)(2,1)S(1)}, bf16[128,256]{1,0:T(8,128)(2,1)S(1)}, u32[]{:S(2)}, u32[]{:S(2)}) collective-permute-start(bf16[128,256]{1,0:T(8,128)(2,1)S(1)} %collective-permute-done.14.refs_5_), channel_id=1, source_target_pairs={{0,1},{1,0},{2,3},{3,2},{4,5},{5,4},{6,7},{7,6},{8,9},{9,8},{10,11... | collective-permute-start | bytes 196616 | tf_op jit(solution)/shard_map/ppermute | solution.py:205
  32.8 12.2 %collective-permute-start.24 = (bf16[128,256]{1,0:T(8,128)(2,1)S(1)}, bf16[128,256]{1,0:T(8,128)(2,1)S(1)}, u32[]{:S(2)}, u32[]{:S(2)}) collective-permute-start(bf16[128,256]{1,0:T(8,128)(2,1)S(1)} %collective-permute-done.21.refs_5_), channel_id=1, source_target_pairs={{0,3},{1,2},{2,1},{3,0},{4,7},{5,6},{6,5},{7,4},{8,11},{9,10},{10,... | collective-permute-start | bytes 196616 | tf_op jit(solution)/shard_map/ppermute | solution.py:205
  33.1 1.2 %copy-start.1 = (bf16[1,128,4096]{2,1,0:T(8,128)(2,1)S(1)}, bf16[1,128,4096]{2,1,0:T(8,128)(2,1)}, u32[]{:S(2)}) copy-start(bf16[1,128,4096]{2,1,0:T(8,128)(2,1)} %refs_2_.7) | copy-start | bytes 3145732
  37.7 7.4 %collective-permute-start.23 = (bf16[128,256]{1,0:T(8,128)(2,1)S(1)}, bf16[128,256]{1,0:T(8,128)(2,1)S(1)}, u32[]{:S(2)}, u32[]{:S(2)}) collective-permute-start(bf16[128,256]{1,0:T(8,128)(2,1)S(1)} %collective-permute-done.21.refs_5_), channel_id=1, source_target_pairs={{0,2},{1,3},{2,0},{3,1},{4,6},{5,7},{6,4},{7,5},{8,10},{9,11},{10,... | collective-permute-start | bytes 196616 | tf_op jit(solution)/shard_map/ppermute | solution.py:205
  39.3 5.8 %collective-permute-start.22 = (bf16[128,256]{1,0:T(8,128)(2,1)S(1)}, bf16[128,256]{1,0:T(8,128)(2,1)S(1)}, u32[]{:S(2)}, u32[]{:S(2)}) collective-permute-start(bf16[128,256]{1,0:T(8,128)(2,1)S(1)} %collective-permute-done.21.refs_5_), channel_id=1, source_target_pairs={{0,1},{1,0},{2,3},{3,2},{4,5},{5,4},{6,7},{7,6},{8,9},{9,8},{10,11... | collective-permute-start | bytes 196616 | tf_op jit(solution)/shard_map/ppermute | solution.py:205
  40.0 8.5 %collective-permute-start.31 = (bf16[128,256]{1,0:T(8,128)(2,1)S(1)}, bf16[128,256]{1,0:T(8,128)(2,1)S(1)}, u32[]{:S(2)}, u32[]{:S(2)}) collective-permute-start(bf16[128,256]{1,0:T(8,128)(2,1)S(1)} %collective-permute-done.28.refs_5_), channel_id=1, source_target_pairs={{0,3},{1,2},{2,1},{3,0},{4,7},{5,6},{6,5},{7,4},{8,11},{9,10},{10,... | collective-permute-start | bytes 196616 | tf_op jit(solution)/shard_map/ppermute | solution.py:205
  40.1 8.4 %collective-permute-start.30 = (bf16[128,256]{1,0:T(8,128)(2,1)S(1)}, bf16[128,256]{1,0:T(8,128)(2,1)S(1)}, u32[]{:S(2)}, u32[]{:S(2)}) collective-permute-start(bf16[128,256]{1,0:T(8,128)(2,1)S(1)} %collective-permute-done.28.refs_5_), channel_id=1, source_target_pairs={{0,2},{1,3},{2,0},{3,1},{4,6},{5,7},{6,4},{7,5},{8,10},{9,11},{10,... | collective-permute-start | bytes 196616 | tf_op jit(solution)/shard_map/ppermute | solution.py:205
  45.0 3.5 %collective-permute-start.29 = (bf16[128,256]{1,0:T(8,128)(2,1)S(1)}, bf16[128,256]{1,0:T(8,128)(2,1)S(1)}, u32[]{:S(2)}, u32[]{:S(2)}) collective-permute-start(bf16[128,256]{1,0:T(8,128)(2,1)S(1)} %collective-permute-done.28.refs_5_), channel_id=1, source_target_pairs={{0,1},{1,0},{2,3},{3,2},{4,5},{5,4},{6,7},{7,6},{8,9},{9,8},{10,11... | collective-permute-start | bytes 196616 | tf_op jit(solution)/shard_map/ppermute | solution.py:205
  52.0 2.8 %collective-permute-start.38 = (bf16[16,1024]{1,0:T(8,128)(2,1)S(1)}, bf16[16,1024]{1,0:T(8,128)(2,1)S(1)}, u32[]{:S(2)}, u32[]{:S(2)}) collective-permute-start(bf16[16,1024]{1,0:T(8,128)(2,1)S(1)} %constant_dynamic-update-slice_fusion), channel_id=1, source_target_pairs={{7,3},{15,11},{23,19},{31,27}} | collective-permute-start | bytes 98312 | tf_op jit(solution)/shard_map/ppermute | solution.py:205
  52.7 7.3 %collective-permute-start.37 = (bf16[16,1024]{1,0:T(8,128)(2,1)S(1)}, bf16[16,1024]{1,0:T(8,128)(2,1)S(1)}, u32[]{:S(2)}, u32[]{:S(2)}) collective-permute-start(bf16[16,1024]{1,0:T(8,128)(2,1)S(1)} %constant_dynamic-update-slice_fusion), channel_id=1, source_target_pairs={{6,3},{14,11},{22,19},{30,27}} | collective-permute-start | bytes 98312 | tf_op jit(solution)/shard_map/ppermute | solution.py:205
  53.3 7.5 %collective-permute-start.36 = (bf16[16,1024]{1,0:T(8,128)(2,1)S(1)}, bf16[16,1024]{1,0:T(8,128)(2,1)S(1)}, u32[]{:S(2)}, u32[]{:S(2)}) collective-permute-start(bf16[16,1024]{1,0:T(8,128)(2,1)S(1)} %constant_dynamic-update-slice_fusion), channel_id=1, source_target_pairs={{5,3},{13,11},{21,19},{29,27}} | collective-permute-start | bytes 98312 | tf_op jit(solution)/shard_map/ppermute | solution.py:205
  54.0 11.4 %collective-permute-start.35 = (bf16[16,1024]{1,0:T(8,128)(2,1)S(1)}, bf16[16,1024]{1,0:T(8,128)(2,1)S(1)}, u32[]{:S(2)}, u32[]{:S(2)}) collective-permute-start(bf16[16,1024]{1,0:T(8,128)(2,1)S(1)} %constant_dynamic-update-slice_fusion), channel_id=1, source_target_pairs={{4,3},{12,11},{20,19},{28,27}} | collective-permute-start | bytes 98312 | tf_op jit(solution)/shard_map/ppermute | solution.py:205
  54.7 12.3 %collective-permute-start.32 = (bf16[128,256]{1,0:T(8,128)(2,1)S(1)}, bf16[128,256]{1,0:T(8,128)(2,1)S(1)}, u32[]{:S(2)}, u32[]{:S(2)}) collective-permute-start(bf16[128,256]{1,0:T(8,128)(2,1)S(1)} %get-tuple-element.42), channel_id=1, source_target_pairs={{0,1},{1,0},{2,3},{3,2},{4,5},{5,4},{6,7},{7,6},{8,9},{9,8},{10,11... | collective-permute-start | bytes 196616 | tf_op jit(solution)/shard_map/ppermute | solution.py:205
  54.8 12.6 %collective-permute-start.33 = (bf16[128,256]{1,0:T(8,128)(2,1)S(1)}, bf16[128,256]{1,0:T(8,128)(2,1)S(1)}, u32[]{:S(2)}, u32[]{:S(2)}) collective-permute-start(bf16[128,256]{1,0:T(8,128)(2,1)S(1)} %get-tuple-element.43), channel_id=1, source_target_pairs={{0,2},{1,3},{2,0},{3,1},{4,6},{5,7},{6,4},{7,5},{8,10},{9,11},{10,... | collective-permute-start | bytes 196616 | tf_op jit(solution)/shard_map/ppermute | solution.py:205
  59.9 9.2 %collective-permute-start.34 = (bf16[128,256]{1,0:T(8,128)(2,1)S(1)}, bf16[128,256]{1,0:T(8,128)(2,1)S(1)}, u32[]{:S(2)}, u32[]{:S(2)}) collective-permute-start(bf16[128,256]{1,0:T(8,128)(2,1)S(1)} %get-tuple-element.44), channel_id=1, source_target_pairs={{0,3},{1,2},{2,1},{3,0},{4,7},{5,6},{6,5},{7,4},{8,11},{9,10},{10,... | collective-permute-start | bytes 196616 | tf_op jit(solution)/shard_map/ppermute | solution.py:205
  60.8 6.2 %collective-permute-start.39 = (bf16[16,1024]{1,0:T(8,128)(2,1)S(1)}, bf16[16,1024]{1,0:T(8,128)(2,1)S(1)}, u32[]{:S(2)}, u32[]{:S(2)}) collective-permute-start(bf16[16,1024]{1,0:T(8,128)(2,1)S(1)} %pad_maximum_fusion.4), channel_id=1, source_target_pairs={{0,4},{8,12},{16,20},{24,28}} | collective-permute-start | bytes 98312 | tf_op jit(solution)/shard_map/ppermute | solution.py:205
  65.4 3.8 %collective-permute-start.25 = (bf16[128,256]{1,0:T(8,128)(2,1)S(1)}, bf16[128,256]{1,0:T(8,128)(2,1)S(1)}, u32[]{:S(2)}, u32[]{:S(2)}) collective-permute-start(bf16[128,256]{1,0:T(8,128)(2,1)S(1)} %get-tuple-element.38), channel_id=1, source_target_pairs={{0,1},{1,0},{2,3},{3,2},{4,5},{5,4},{6,7},{7,6},{8,9},{9,8},{10,11... | collective-permute-start | bytes 196616 | tf_op jit(solution)/shard_map/ppermute | solution.py:205
  67.0 4.4 %collective-permute-start.26 = (bf16[128,256]{1,0:T(8,128)(2,1)S(1)}, bf16[128,256]{1,0:T(8,128)(2,1)S(1)}, u32[]{:S(2)}, u32[]{:S(2)}) collective-permute-start(bf16[128,256]{1,0:T(8,128)(2,1)S(1)} %get-tuple-element.39), channel_id=1, source_target_pairs={{0,2},{1,3},{2,0},{3,1},{4,6},{5,7},{6,4},{7,5},{8,10},{9,11},{10,... | collective-permute-start | bytes 196616 | tf_op jit(solution)/shard_map/ppermute | solution.py:205
  67.0 4.4 %collective-permute-start.27 = (bf16[128,256]{1,0:T(8,128)(2,1)S(1)}, bf16[128,256]{1,0:T(8,128)(2,1)S(1)}, u32[]{:S(2)}, u32[]{:S(2)}) collective-permute-start(bf16[128,256]{1,0:T(8,128)(2,1)S(1)} %get-tuple-element.40), channel_id=1, source_target_pairs={{0,3},{1,2},{2,1},{3,0},{4,7},{5,6},{6,5},{7,4},{8,11},{9,10},{10,... | collective-permute-start | bytes 196616 | tf_op jit(solution)/shard_map/ppermute | solution.py:205
  67.4 5.3 %collective-permute-start.18 = (bf16[128,256]{1,0:T(8,128)(2,1)S(1)}, bf16[128,256]{1,0:T(8,128)(2,1)S(1)}, u32[]{:S(2)}, u32[]{:S(2)}) collective-permute-start(bf16[128,256]{1,0:T(8,128)(2,1)S(1)} %get-tuple-element.34), channel_id=1, source_target_pairs={{0,1},{1,0},{2,3},{3,2},{4,5},{5,4},{6,7},{7,6},{8,9},{9,8},{10,11... | collective-permute-start | bytes 196616 | tf_op jit(solution)/shard_map/ppermute | solution.py:205
  69.1 4.9 %collective-permute-start.19 = (bf16[128,256]{1,0:T(8,128)(2,1)S(1)}, bf16[128,256]{1,0:T(8,128)(2,1)S(1)}, u32[]{:S(2)}, u32[]{:S(2)}) collective-permute-start(bf16[128,256]{1,0:T(8,128)(2,1)S(1)} %get-tuple-element.35), channel_id=1, source_target_pairs={{0,2},{1,3},{2,0},{3,1},{4,6},{5,7},{6,4},{7,5},{8,10},{9,11},{10,... | collective-permute-start | bytes 196616 | tf_op jit(solution)/shard_map/ppermute | solution.py:205
  69.2 5.1 %collective-permute-start.20 = (bf16[128,256]{1,0:T(8,128)(2,1)S(1)}, bf16[128,256]{1,0:T(8,128)(2,1)S(1)}, u32[]{:S(2)}, u32[]{:S(2)}) collective-permute-start(bf16[128,256]{1,0:T(8,128)(2,1)S(1)} %get-tuple-element.36), channel_id=1, source_target_pairs={{0,3},{1,2},{2,1},{3,0},{4,7},{5,6},{6,5},{7,4},{8,11},{9,10},{10,... | collective-permute-start | bytes 196616 | tf_op jit(solution)/shard_map/ppermute | solution.py:205
  71.4 2.9 %collective-permute-start.11 = (bf16[128,256]{1,0:T(8,128)(2,1)S(1)}, bf16[128,256]{1,0:T(8,128)(2,1)S(1)}, u32[]{:S(2)}, u32[]{:S(2)}) collective-permute-start(bf16[128,256]{1,0:T(8,128)(2,1)S(1)} %get-tuple-element.30), channel_id=1, source_target_pairs={{0,1},{1,0},{2,3},{3,2},{4,5},{5,4},{6,7},{7,6},{8,9},{9,8},{10,11... | collective-permute-start | bytes 196616 | tf_op jit(solution)/shard_map/ppermute | solution.py:205
  71.4 5.0 %collective-permute-start.12 = (bf16[128,256]{1,0:T(8,128)(2,1)S(1)}, bf16[128,256]{1,0:T(8,128)(2,1)S(1)}, u32[]{:S(2)}, u32[]{:S(2)}) collective-permute-start(bf16[128,256]{1,0:T(8,128)(2,1)S(1)} %get-tuple-element.31), channel_id=1, source_target_pairs={{0,2},{1,3},{2,0},{3,1},{4,6},{5,7},{6,4},{7,5},{8,10},{9,11},{10,... | collective-permute-start | bytes 196616 | tf_op jit(solution)/shard_map/ppermute | solution.py:205
  72.7 5.0 %collective-permute-start.13 = (bf16[128,256]{1,0:T(8,128)(2,1)S(1)}, bf16[128,256]{1,0:T(8,128)(2,1)S(1)}, u32[]{:S(2)}, u32[]{:S(2)}) collective-permute-start(bf16[128,256]{1,0:T(8,128)(2,1)S(1)} %get-tuple-element.32), channel_id=1, source_target_pairs={{0,3},{1,2},{2,1},{3,0},{4,7},{5,6},{6,5},{7,4},{8,11},{9,10},{10,... | collective-permute-start | bytes 196616 | tf_op jit(solution)/shard_map/ppermute | solution.py:205

commit v2 on v0

v2 whole, which is shorter than its diff:
```python
import functools
import math

import jax
import jax.numpy as jnp
from jax import lax
from jax.experimental import pallas as pl
from jax.experimental.pallas import tpu as pltpu
from jax.sharding import PartitionSpec as P

H = 32
KVH = 4
HD = 128
REACH = 5
GROUP = REACH - 1
SHARE = H // KVH
PARTS = KVH // 2
WIDE = SHARE * HD
MASKED = -1e30
F32 = jnp.float32
BF16 = jnp.bfloat16
NT = (((1,), (1,)), ((), ()))
NN = (((1,), (0,)), ((), ()))


def place():
    me = lax.axis_index("ctx")
    rank = lax.rem(me, GROUP)
    return me, rank, lax.rem(rank, 2)


def call(body, out, mib=8, flops=1000, **more):
    return pl.pallas_call(
        body,
        out_shape=out,
        compiler_params=pltpu.CompilerParams(vmem_limit_bytes=mib * 2**20),
        cost_estimate=pl.CostEstimate(flops=flops, bytes_accessed=1000, transcendentals=0),
        **more,
    )


def columns(head):
    return pl.ds(pl.multiple_of(head * HD, HD), HD)


def split_kernel(kv_ref, own, far):
    _, _, core = place()
    for part in range(PARTS):
        for half, ref in ((core, own), (1 - core, far)):
            for kind in range(2):
                ref[:, pl.ds((part * 2 + kind) * HD, HD)] = kv_ref[0, :, columns(half * PARTS + part + kind * KVH)]


def edge_rows(docs):
    return -(-SHARE * docs // 16) * 16


def hand_kernel(halo, docs, q_ref, g_ref, far, edge0, edge1, q_top, g_top, sem):
    _, _, core = place()
    rows = q_ref.shape[1]
    wide = PARTS * WIDE
    start = pl.multiple_of((1 - core) * wide, wide)
    tops = [(ref.at[0, pl.ds(0, halo)], top) for ref, top in ((q_ref, q_top), (g_ref, g_top))]
    whole = [
        (ref.at[0, :, pl.ds(start, wide)], far.at[pl.ds(at * rows, rows)]) for at, ref in enumerate((q_ref, g_ref))
    ]
    copies = [pltpu.make_async_copy(*copy, sem.at[at]) for at, copy in enumerate(tops + whole)]
    for copy in copies:
        copy.start()
    size = edge_rows(docs)
    to = lax.broadcasted_iota(jnp.int32, (size, SHARE * halo), 0)
    at = lax.broadcasted_iota(jnp.int32, (size, SHARE * halo), 1)
    picked = ((at // halo == to // docs) & (at % halo == to % docs)).astype(BF16)
    for copy in copies[:2]:
        copy.wait()
    for kind, top in enumerate((q_top, g_top)):
        for half, edge in enumerate((edge0, edge1)):
            for part in range(PARTS):
                heads = [(half * PARTS + part) * SHARE + head for head in range(SHARE)]
                block = jnp.concatenate([top[:, pl.ds(head * HD, HD)] for head in heads], axis=0)
                chosen = lax.dot_general(picked, block, NN, preferred_element_type=F32).astype(BF16)
                edge[pl.ds((kind * PARTS + part) * size, size), :] = chosen
    for copy in copies[2:]:
        copy.wait()


def edge_kernel(own, one, edge):
    _, rank, _ = place()
    halo = edge.shape[0]
    first = pl.ds(pl.multiple_of(jnp.where(rank < 2, 0, own.shape[0] - halo), 16), halo)
    edge[...] = jnp.where((rank == 0) | (rank == GROUP - 1), own[first, :], one[first, :])


def stage_kernel(q_ref, g_ref, far, edge0, edge1, q_buf, g_buf, sem):
    _, _, core = place()
    rows = q_ref.shape[1]
    copies = []
    for kind, (ref, buf) in enumerate(((q_ref, q_buf), (g_ref, g_buf))):
        for part in range(PARTS):
            for head in range(SHARE):
                here = head * rows
                mine = ref.at[0, :, columns((core * PARTS + part) * SHARE + head)]
                other = far.at[pl.ds(kind * rows, rows), pl.ds((part * SHARE + head) * HD, HD)]
                for slot, block in ((core, mine), (1 - core, other)):
                    at = pl.ds(pl.multiple_of(slot * WIDE + here, 16), rows)
                    copies.append((block, buf.at[part, at]))
    copies = [pltpu.make_async_copy(*copy, sem.at[at]) for at, copy in enumerate(copies)]
    for copy in copies:
        copy.start()
    size = edge0.shape[0] // (2 * PARTS)
    for half, edge in enumerate((edge0, edge1)):

        @pl.when(core == half)
        def _():
            extra = []
            for kind, buf in enumerate((q_buf, g_buf)):
                for part in range(PARTS):
                    block = edge.at[pl.ds((kind * PARTS + part) * size, size)]
                    to = buf.at[part, pl.ds(2 * WIDE, size)]
                    extra.append(pltpu.make_async_copy(block, to, sem.at[len(copies) + len(extra)]))
            for copy in extra:
                copy.start()
            for copy in extra:
                copy.wait()

    for copy in copies:
        copy.wait()


def doc_start(pos, len_ref):
    start = jnp.zeros_like(pos)
    end = jnp.int32(0)
    for doc in range(len_ref.shape[0]):
        end = end + len_ref[doc]
        start = jnp.where(end <= pos, end, start)
    return start


def bias_of(first_key, keys, query_pos, start):
    key_pos = first_key + lax.broadcasted_iota(jnp.int32, (keys, query_pos.shape[1]), 0)
    return jnp.where((key_pos >= start) & (key_pos <= query_pos), 0.0, MASKED)


def weigh(key, value, query, cot, bias, keep):
    scores = lax.dot_general(key, query, NT, preferred_element_type=F32) + bias
    top = jnp.max(scores, axis=0, keepdims=True)
    raw = jnp.exp2((scores - top) * (HD**-0.5 * math.log2(math.e)))
    weights = raw * (keep / jnp.sum(raw, axis=0, keepdims=True))
    dweights = lax.dot_general(value, cot, NT, preferred_element_type=F32)
    delta = jnp.sum(weights * dweights, axis=0, keepdims=True)
    dscores = weights * (dweights - delta)
    return weights.astype(BF16), dscores.astype(BF16)


def grad_kernel(halo, len_ref, q_buf, g_buf, own_ref, one_ref, two_ref, three_ref, edge_a, edge_b,
                own_out, one_out, two_out, three_out, end_a, end_b, k_buf, v_buf, dk_ref, dv_ref):
    rows = own_ref.shape[0]
    span = GROUP * rows
    me, rank, _ = place()
    first = (me - rank) * rows
    docs = len_ref.shape[0]
    scale = HD**-0.5

    for part in range(PARTS):
        here = part * 2 * HD
        k_cols, v_cols = pl.ds(here, HD), pl.ds(here + HD, HD)
        for buf, cols in ((k_buf, k_cols), (v_buf, v_cols)):
            for step, ref in enumerate((own_ref, one_ref, two_ref, three_ref)):
                buf[pl.ds(pl.multiple_of(halo + (rank ^ step) * rows, 16), rows), :] = ref[:, cols]
            buf[:halo, :] = jnp.where(rank < 2, edge_a[:, cols], edge_b[:, cols])
            buf[halo + span :, :] = edge_a[:, cols]
        dk_ref[...] = jnp.zeros_like(dk_ref)
        dv_ref[...] = jnp.zeros_like(dv_ref)

        for chip in range(2):

            @pl.when(rank // 2 == chip)
            def _():
                for slot in range(2):
                    block = 2 * chip + slot
                    keys = halo + (block + 1) * rows
                    cols = pl.ds(slot * WIDE, WIDE)
                    query_pos = first + block * rows + lax.broadcasted_iota(jnp.int32, (1, rows), 1)
                    start = doc_start(query_pos, len_ref)
                    keep = [jnp.where(start < first - halo, 0.0, 1.0)] * SHARE
                    if block == GROUP - 1:
                        keys = keys + halo
                        size = edge_rows(docs)
                        cols = pl.ds(slot * WIDE, WIDE + size)
                        lane = lax.broadcasted_iota(jnp.int32, (1, size), 1)
                        next_pos = first + span + lax.rem(lane, docs)
                        next_start = doc_start(next_pos, len_ref)
                        keep.append(jnp.where((next_start < first + span - halo) & (lane < SHARE * docs), 1.0, 0.0))
                    bias = [bias_of(first - halo, keys, query_pos, start)] * SHARE
                    if block == GROUP - 1:
                        bias.append(bias_of(first - halo, keys, next_pos, next_start))
                    query, cot = q_buf[part, cols, :], g_buf[part, cols, :]
                    weights, dscores = weigh(
                        k_buf[:keys, :], v_buf[:keys, :], query, cot,
                        jnp.concatenate(bias, axis=1), jnp.concatenate(keep, axis=1),
                    )
                    dv_ref[:keys, :] += lax.dot_general(weights, cot, NN, preferred_element_type=F32)
                    dk_ref[:keys, :] += lax.dot_general(dscores, query, NN, preferred_element_type=F32)

        def terms(row, size):
            at = pl.ds(pl.multiple_of(row, 16), size)
            return ((k_cols, dk_ref[at, :] * scale), (v_cols, dv_ref[at, :]))

        for step, ref in enumerate((own_out, one_out)):
            for cols, term in terms(halo + (rank ^ step) * rows, rows):
                ref[:, cols] = term.astype(ref.dtype)
        for step, ref in ((2, two_out), (3, three_out)):
            for cols, term in terms(jnp.where(rank < 2, 0, halo + (rank ^ step) * rows), rows):
                ref[:, cols] = term.astype(ref.dtype)
        for ref, giver in ((end_a, 2), (end_b, 3)):
            for cols, term in terms(jnp.where(rank == giver, halo + span, 0), halo):
                ref[:, cols] = term.astype(ref.dtype)


def grads(halo, *inputs):
    rows = inputs[3].shape[0]
    wide = 2 * PARTS * HD
    total = (halo + GROUP * rows + halo, HD)
    out = [jax.ShapeDtypeStruct((rows, wide), F32)]
    out += [jax.ShapeDtypeStruct((rows, wide), BF16)] * 3
    out += [jax.ShapeDtypeStruct((halo, wide), BF16)] * 2
    vmem = pl.BlockSpec(memory_space=pltpu.VMEM)
    return call(
        functools.partial(grad_kernel, halo),
        out,
        in_specs=[pl.BlockSpec(memory_space=pltpu.SMEM)] + [vmem] * (len(inputs) - 1),
        scratch_shapes=[
            pltpu.VMEM(total, BF16),
            pltpu.VMEM(total, BF16),
            pltpu.VMEM(total, F32),
            pltpu.VMEM(total, F32),
        ],
        mib=24,
        flops=COST,
    )(*inputs)


COST = 4 * 10**9


def sum_kernel(halo, own, one, two, three, end_a, end_b, out_ref):
    _, rank, core = place()
    rows = out_ref.shape[1]
    chip0, last = rank < 2, rank == GROUP - 1
    for part in range(PARTS):
        for kind in range(2):
            cols = pl.ds((part * 2 + kind) * HD, HD)
            ones, twos, threes, a, b = (ref[:, cols].astype(F32) for ref in (one, two, three, end_a, end_b))
            mine = own[:, cols] + jnp.where(chip0, twos, 0.0)
            other = ones + jnp.where(chip0, threes, 0.0)
            highs = (threes[:halo] + b, twos[:halo] + a)
            lows = (a, b)
            for half in range(2):
                total = jnp.where(core == half, mine, other)
                high = jnp.where(last, highs[half], 0.0)
                low = jnp.where(rank == 0, lows[half], 0.0)
                total = jnp.concatenate(
                    [total[:halo] + low, total[halo : rows - halo], total[rows - halo :] + high], axis=0
                )
                out_ref[0, :, pl.ds((kind * KVH + half * PARTS + part) * HD, HD)] = total.astype(out_ref.dtype)


def on_device(queries, stash, grad_out, lengths):
    rows = queries.shape[1]
    pipe, ctx = lax.axis_size("pipe"), lax.axis_size("ctx")
    halo = -(-lengths.shape[0] // 16) * 16
    high = 1 << (pipe.bit_length() - 2)

    def pairs(pick):
        return [(c, (c + pick[c % GROUP]) % ctx) for c in range(ctx)]

    def partner(block, pick):
        route = [((p ^ high) * ctx + c, p * ctx + d) for p in range(pipe) for c, d in pairs(pick)]
        return lax.ppermute(block, ("pipe", "ctx"), route)

    def along(block, pick):
        return lax.ppermute(block, "ctx", pairs(pick))

    stay = (0,) * GROUP
    flip = [tuple((rank ^ step) - rank for rank in range(GROUP)) for step in range(GROUP)]

    def shape(*dims):
        return jax.ShapeDtypeStruct(dims, BF16)

    def after(value, *others):
        return lax.optimization_barrier((value, *others))[0]

    edge_wide = 2 * PARTS * HD
    hbm = pl.BlockSpec(memory_space=pltpu.HBM)
    held = partner(stash, stay)

    wide = PARTS * WIDE
    size = edge_rows(lengths.shape[0])

    def beside(queries, grad_out):
        far, edge0, edge1 = call(
            functools.partial(hand_kernel, halo, lengths.shape[0]),
            [shape(2 * rows, wide), *[shape(2 * PARTS * size, HD)] * 2],
            in_specs=[hbm] * 2,
            scratch_shapes=[pltpu.VMEM((halo, 2 * wide), BF16)] * 2 + [pltpu.SemaphoreType.DMA((4,))],
        )(queries, grad_out)
        return along(far, flip[1]), along(edge0, (-2, -2, 2, 2)), along(edge1, (-1, -3, 3, 1))

    def nothing(*_):
        return jnp.zeros((2 * rows, wide), BF16), *[jnp.zeros((2 * PARTS * size, HD), BF16)] * 2

    far, edge0, edge1 = lax.cond(lengths[0] > 0, beside, nothing, queries, grad_out)
    q_buf, g_buf = call(
        stage_kernel,
        [shape(PARTS, 2 * WIDE + size, HD)] * 2,
        in_specs=[hbm] * 5,
        scratch_shapes=[pltpu.SemaphoreType.DMA((4 * PARTS * SHARE + 2 * PARTS,))],
    )(queries, grad_out, far, edge0, edge1)
    held, q_buf, g_buf = lax.optimization_barrier((held, q_buf, g_buf))
    own, far = call(split_kernel, [shape(rows, edge_wide)] * 2)(held)

    got = [own, along(far, flip[1]), along(own, flip[2]), along(far, flip[3])]
    edge = call(edge_kernel, shape(halo, edge_wide))(own, got[1])
    edge_a, edge_b = along(edge, (-2, -2, 2, 2)), along(edge, (4, 4, 4, 4))
    own, one, two, three, end_a, end_b = grads(halo, lengths, q_buf, g_buf, *got, edge_a, edge_b)
    back = (
        along(one, flip[1]),
        along(two, (-2, -2, -2, -2)),
        along(three, (-1, -3, -1, -3)),
        along(end_a, (-2, 4, 2, -4)),
        along(end_b, (-2, 4, -3, 1)),
    )
    return call(functools.partial(sum_kernel, halo), shape(1, rows, 2 * KVH * HD))(own, *back)


def solution(mesh):
    placed = (P("pipe", "ctx", None), P("pipe", "ctx", None), P("pipe", "ctx", None), P())
    return jax.shard_map(
        on_device, mesh=mesh, in_specs=placed, out_specs=P("pipe", "ctx", None), check_vma=False
    )
```

time: 138 us -> 44.1 us (0.32)
  the two profiles are of different devices: /device:TPU:26 before, /device:TPU:0 now
where the time goes in v2:
time: 44.1 us; the launch traced here: 43.8 us
  starting transfers between devices  20.4 us (46%)
  waiting for transfers between devices  14.2 us (32%)
  Pallas kernels  8.49 us (19%)
  between operations  0.7 us (2%)
    ppermute x13, starting transfers between devices, along(): return lax.ppermute(block, 'ctx', pairs(pick))  16.3 us
    ppermute x13, waiting for transfers between devices, along(): return lax.ppermute(block, 'ctx', pairs(pick))  13.1 us
    ppermute x1, starting transfers between devices, partner(): return lax.ppermute(block, ('pipe', 'ctx'), route)  4.04 us
    pallas_call x1, Pallas kernels, grads(): call(functools.partial(grad_kernel, halo), out, in_specs=[pl.BlockSpec(me...  4.01 us
    pallas_call x1, Pallas kernels, on_device(): call(stage_kernel, [shape(PARTS, 2 * WIDE + size, HD)] * 2, in_specs=[hbm...  2.19 us
    pallas_call x1, Pallas kernels, beside(): call(functools.partial(hand_kernel, halo, lengths.shape[0]), [shape(2 * r...  1.38 us
    ppermute x1, waiting for transfers between devices, partner(): return lax.ppermute(block, ('pipe', 'ctx'), route)  1.11 us
  transfers between devices with their start and end apart: 14, of which 8 were waited for; matrix products, arithmetic and copies ran while one was open for 0% of the time, Pallas kernels for 8%

profile of v2, /device:TPU:0, one launch (start us, length us, event | category | flops | bytes accessed | tf_op | source)
XLA Modules:
  0.0 43.8 jit_solution(737740934446263647)
XLA Ops:
  0.0 4.0 %collective-permute-start.3 = (bf16[1,128,1024]{2,1,0:T(8,128)(2,1)}, bf16[1,128,1024]{2,1,0:T(8,128)(2,1)S(1)}, u32[]{:S(2)}, u32[]{:S(2)}) collective-permute-start(bf16[1,128,1024]{2,1,0:T(8,128)(2,1)} %param.7), channel_id=1, source_target_pairs={{16,0},{17,1},{18,2},{19,3},{20,4},{21,5},{22,6},{23,7},{24,8},{25... | collective-permute-start | bytes 786440 | tf_op jit(solution)/shard_map/ppermute | solution.py:279
  4.7 8.2 %conditional.1 = (bf16[256,2048]{1,0:T(8,128)(2,1)}, bf16[64,128]{1,0:T(8,128)(2,1)}, bf16[64,128]{1,0:T(8,128)(2,1)}) conditional(s32[]{:T(128)} %bitcast, () %tuple.14, (bf16[1,128,4096]{2,1,0:T(8,128)(2,1)}, bf16[1,128,4096]{2,1,0:T(8,128)(2,1)}) %tuple.15), branch_computations={%region_0.0_spmd, %region_1.0_spmd} | conditional | flops 1000 | bytes 4326520 | solution.py:312
  4.7 1.4 %branch_1_fun.1 = (bf16[256,2048]{1,0:T(8,128)(2,1)S(1)}, bf16[64,128]{1,0:T(8,128)(2,1)S(1)}, bf16[64,128]{1,0:T(8,128)(2,1)S(1)}) custom-call(bf16[1,128,4096]{2,1,0:T(8,128)(2,1)} %get-tuple-element.9.q_ref, bf16[1,128,4096]{2,1,0:T(8,128)(2,1)} %get-tuple-element.10.g_ref), custom_call_target="tpu_custom_call" | custom-call | flops 1000 | bytes 1000 | tf_op jit(solution)/shard_map/cond/branch_1_fun/pallas_call | solution.py:301
  6.1 0.1 collective-permute-start
  6.2 2.5 %collective-permute-start.1 = (bf16[64,128]{1,0:T(8,128)(2,1)S(1)}, bf16[64,128]{1,0:T(8,128)(2,1)}, u32[]{:S(2)}, u32[]{:S(2)}) collective-permute-start(bf16[64,128]{1,0:T(8,128)(2,1)S(1)} %get-tuple-element.12), channel_id=1, source_target_pairs={{0,6},{1,7},{2,4},{3,5},{4,2},{5,3},{6,0},{7,1},{8,14},{9,15},{10,... | collective-permute-start | bytes 49160 | tf_op jit(solution)/shard_map/cond/branch_1_fun/ppermute | solution.py:282
  8.7 0.2 collective-permute-start.2
  8.9 2.0 %collective-permute-done.1 = bf16[64,128]{1,0:T(8,128)(2,1)} collective-permute-done((bf16[64,128]{1,0:T(8,128)(2,1)S(1)}, bf16[64,128]{1,0:T(8,128)(2,1)}, u32[]{:S(2)}, u32[]{:S(2)}) %collective-permute-start.1) | collective-permute-done | bytes 16416 | tf_op jit(solution)/shard_map/cond/branch_1_fun/ppermute | solution.py:282
  11.0 1.9 %collective-permute-done.2 = bf16[64,128]{1,0:T(8,128)(2,1)} collective-permute-done((bf16[64,128]{1,0:T(8,128)(2,1)S(1)}, bf16[64,128]{1,0:T(8,128)(2,1)}, u32[]{:S(2)}, u32[]{:S(2)}) %collective-permute-start.2) | collective-permute-done | bytes 16416 | tf_op jit(solution)/shard_map/cond/branch_1_fun/ppermute | solution.py:282
  12.9 0.0 collective-permute-done
  12.9 0.0 copy-start
  12.9 2.2 %shard_map.46 = (bf16[2,2064,128]{2,1,0:T(8,128)(2,1)S(1)}, bf16[2,2064,128]{2,1,0:T(8,128)(2,1)S(1)}) custom-call(bf16[1,128,4096]{2,1,0:T(8,128)(2,1)} %q_ref.1, bf16[1,128,4096]{2,1,0:T(8,128)(2,1)} %g_ref.1, bf16[256,2048]{1,0:T(8,128)(2,1)} %get-tuple-element.30.far, bf16[64,128]{1,0:T(8,128)(2,1)} %get-tuple-element.31.edge0, ...), custom_call_target="tpu_custom_call" | custom-call | flops 1000 | bytes 1000 | tf_op jit(solution)/shard_map/pallas_call | solution.py:313
  15.1 1.1 %collective-permute-done.3.kv_ref = bf16[1,128,1024]{2,1,0:T(8,128)(2,1)S(1)} collective-permute-done((bf16[1,128,1024]{2,1,0:T(8,128)(2,1)}, bf16[1,128,1024]{2,1,0:T(8,128)(2,1)S(1)}, u32[]{:S(2)}, u32[]{:S(2)}) %collective-permute-start.3) | collective-permute-done | bytes 262176 | tf_op jit(solution)/shard_map/ppermute | solution.py:279
  16.2 0.1 shard_map.47
  16.2 0.1 collective-permute-start.4
  16.3 1.6 %collective-permute-start.5 = (bf16[128,512]{1,0:T(8,128)(2,1)S(1)}, bf16[128,512]{1,0:T(8,128)(2,1)S(1)}, u32[]{:S(2)}, u32[]{:S(2)}) collective-permute-start(bf16[128,512]{1,0:T(8,128)(2,1)S(1)} %get-tuple-element.38.own.own_ref), channel_id=1, source_target_pairs={{0,2},{1,3},{2,0},{3,1},{4,6},{5,7},{6,4},{7,5},{8,10},{9,11},{10,... | collective-permute-start | bytes 393224 | tf_op jit(solution)/shard_map/ppermute | solution.py:282
  17.9 0.3 collective-permute-start.6
  18.2 0.0 collective-permute-done.4.one.one_ref
  18.2 2.6 %collective-permute-start.7 = (bf16[16,512]{1,0:T(8,128)(2,1)S(1)}, bf16[16,512]{1,0:T(8,128)(2,1)S(1)}, u32[]{:S(2)}, u32[]{:S(2)}) collective-permute-start(bf16[16,512]{1,0:T(8,128)(2,1)S(1)} %shard_map.48), channel_id=1, source_target_pairs={{0,6},{1,7},{2,4},{3,5},{4,2},{5,3},{6,0},{7,1},{8,14},{9,15},{10,... | collective-permute-start | bytes 49160 | tf_op jit(solution)/shard_map/ppermute | solution.py:282
  20.8 0.5 %collective-permute-start.8 = (bf16[16,512]{1,0:T(8,128)(2,1)S(1)}, bf16[16,512]{1,0:T(8,128)(2,1)S(1)}, u32[]{:S(2)}, u32[]{:S(2)}) collective-permute-start(bf16[16,512]{1,0:T(8,128)(2,1)S(1)} %shard_map.48), channel_id=1, source_target_pairs={{0,4},{1,5},{2,6},{3,7},{4,0},{5,1},{6,2},{7,3},{8,12},{9,13},{10,... | collective-permute-start | bytes 49160 | tf_op jit(solution)/shard_map/ppermute | solution.py:282
  21.3 1.4 %collective-permute-done.5.two_ref = bf16[128,512]{1,0:T(8,128)(2,1)S(1)} collective-permute-done((bf16[128,512]{1,0:T(8,128)(2,1)S(1)}, bf16[128,512]{1,0:T(8,128)(2,1)S(1)}, u32[]{:S(2)}, u32[]{:S(2)}) %collective-permute-start.5) | collective-permute-done | bytes 131104 | tf_op jit(solution)/shard_map/ppermute | solution.py:282
  22.7 1.9 %collective-permute-done.6.three_ref = bf16[128,512]{1,0:T(8,128)(2,1)S(1)} collective-permute-done((bf16[128,512]{1,0:T(8,128)(2,1)S(1)}, bf16[128,512]{1,0:T(8,128)(2,1)S(1)}, u32[]{:S(2)}, u32[]{:S(2)}) %collective-permute-start.6) | collective-permute-done | bytes 131104 | tf_op jit(solution)/shard_map/ppermute | solution.py:282
  24.6 1.8 %collective-permute-done.7.edge_a = bf16[16,512]{1,0:T(8,128)(2,1)S(1)} collective-permute-done((bf16[16,512]{1,0:T(8,128)(2,1)S(1)}, bf16[16,512]{1,0:T(8,128)(2,1)S(1)}, u32[]{:S(2)}, u32[]{:S(2)}) %collective-permute-start.7) | collective-permute-done | bytes 16416 | tf_op jit(solution)/shard_map/ppermute | solution.py:282
  26.4 0.0 collective-permute-done.8.edge_b
  26.4 0.0 copy-done
  26.4 4.0 %shard_map.49 = (f32[128,512]{1,0:T(8,128)S(1)}, bf16[128,512]{1,0:T(8,128)(2,1)S(1)}, bf16[128,512]{1,0:T(8,128)(2,1)S(1)}, bf16[128,512]{1,0:T(8,128)(2,1)S(1)...) custom-call(s32[2]{0:T(128)S(1)} %copy-done, bf16[2,2064,128]{2,1,0:T(8,128)(2,1)S(1)} %get-tuple-element.35.q_buf, ...), custom_call_target="tpu_custom_call" | custom-call | flops 4000000000 | bytes 1000 | tf_op jit(solution)/shard_map/pallas_call | solution.py:228
  30.4 5.4 %collective-permute-start.10 = (bf16[128,512]{1,0:T(8,128)(2,1)S(1)}, bf16[128,512]{1,0:T(8,128)(2,1)S(1)}, u32[]{:S(2)}, u32[]{:S(2)}) collective-permute-start(bf16[128,512]{1,0:T(8,128)(2,1)S(1)} %get-tuple-element.42), channel_id=1, source_target_pairs={{0,6},{1,7},{2,0},{3,1},{4,2},{5,3},{6,4},{7,5},{8,14},{9,15},{10,... | collective-permute-start | bytes 393224 | tf_op jit(solution)/shard_map/ppermute | solution.py:282
  35.8 0.0 collective-permute-start.11
  35.8 0.2 collective-permute-start.9
  36.0 2.9 %collective-permute-start.12 = (bf16[16,512]{1,0:T(8,128)(2,1)S(1)}, bf16[16,512]{1,0:T(8,128)(2,1)S(1)}, u32[]{:S(2)}, u32[]{:S(2)}) collective-permute-start(bf16[16,512]{1,0:T(8,128)(2,1)S(1)} %get-tuple-element.44), channel_id=1, source_target_pairs={{0,6},{1,5},{2,4},{3,7},{4,2},{5,1},{6,0},{7,3},{8,14},{9,13},{10,... | collective-permute-start | bytes 49160 | tf_op jit(solution)/shard_map/ppermute | solution.py:282
  38.9 0.0 collective-permute-start.13
  38.9 3.4 %collective-permute-done.12.end_a = bf16[16,512]{1,0:T(8,128)(2,1)S(1)} collective-permute-done((bf16[16,512]{1,0:T(8,128)(2,1)S(1)}, bf16[16,512]{1,0:T(8,128)(2,1)S(1)}, u32[]{:S(2)}, u32[]{:S(2)}) %collective-permute-start.12) | collective-permute-done | bytes 16416 | tf_op jit(solution)/shard_map/ppermute | solution.py:282
  42.3 0.7 %collective-permute-done.13.end_b = bf16[16,512]{1,0:T(8,128)(2,1)S(1)} collective-permute-done((bf16[16,512]{1,0:T(8,128)(2,1)S(1)}, bf16[16,512]{1,0:T(8,128)(2,1)S(1)}, u32[]{:S(2)}, u32[]{:S(2)}) %collective-permute-start.13) | collective-permute-done | bytes 16416 | tf_op jit(solution)/shard_map/ppermute | solution.py:282
  43.0 0.0 collective-permute-done.10.two
  43.0 0.0 collective-permute-done.11.three
  43.0 0.0 collective-permute-done.9.one
  43.0 0.8 %shard_map.50 = bf16[1,128,1024]{2,1,0:T(8,128)(2,1)} custom-call(f32[128,512]{1,0:T(8,128)S(1)} %get-tuple-element.40.own, bf16[128,512]{1,0:T(8,128)(2,1)S(1)} %collective-permute-done.9.one, bf16[128,512]{1,0:T(8,128)(2,1)S(1)} %collective-permute-done.10.two, bf16[128,512]{1,0:T(8,128)(2,1)S(1)} %collective-permute-done.11.three, ...), custom_call_target="tpu_custom_call" | custom-call | flops 1000 | bytes 1000 | tf_op jit(solution)/shard_map/pallas_call | solution.py:333
  (1 shorter events, 0.0 us)
Async XLA Ops:
  0.0 16.2 %collective-permute-start.3 = (bf16[1,128,1024]{2,1,0:T(8,128)(2,1)}, bf16[1,128,1024]{2,1,0:T(8,128)(2,1)S(1)}, u32[]{:S(2)}, u32[]{:S(2)}) collective-permute-start(bf16[1,128,1024]{2,1,0:T(8,128)(2,1)} %param.7), channel_id=1, source_target_pairs={{16,0},{17,1},{18,2},{19,3},{20,4},{21,5},{22,6},{23,7},{24,8},{25... | collective-permute-start | bytes 786440 | tf_op jit(solution)/shard_map/ppermute | solution.py:279
  6.1 6.8 %collective-permute-start = (bf16[256,2048]{1,0:T(8,128)(2,1)S(1)}, bf16[256,2048]{1,0:T(8,128)(2,1)}, u32[]{:S(2)}, u32[]{:S(2)}) collective-permute-start(bf16[256,2048]{1,0:T(8,128)(2,1)S(1)} %get-tuple-element.11), channel_id=1, source_target_pairs={{0,1},{1,0},{2,3},{3,2},{4,5},{5,4},{6,7},{7,6},{8,9},{9,8},{10,11... | collective-permute-start | bytes 3145736 | tf_op jit(solution)/shard_map/cond/branch_1_fun/ppermute | solution.py:282
  6.2 4.8 %collective-permute-start.1 = (bf16[64,128]{1,0:T(8,128)(2,1)S(1)}, bf16[64,128]{1,0:T(8,128)(2,1)}, u32[]{:S(2)}, u32[]{:S(2)}) collective-permute-start(bf16[64,128]{1,0:T(8,128)(2,1)S(1)} %get-tuple-element.12), channel_id=1, source_target_pairs={{0,6},{1,7},{2,4},{3,5},{4,2},{5,3},{6,0},{7,1},{8,14},{9,15},{10,... | collective-permute-start | bytes 49160 | tf_op jit(solution)/shard_map/cond/branch_1_fun/ppermute | solution.py:282
  8.7 4.2 %collective-permute-start.2 = (bf16[64,128]{1,0:T(8,128)(2,1)S(1)}, bf16[64,128]{1,0:T(8,128)(2,1)}, u32[]{:S(2)}, u32[]{:S(2)}) collective-permute-start(bf16[64,128]{1,0:T(8,128)(2,1)S(1)} %get-tuple-element.13), channel_id=1, source_target_pairs={{0,7},{1,6},{2,5},{3,4},{4,3},{5,2},{6,1},{7,0},{8,15},{9,14},{10,... | collective-permute-start | bytes 49160 | tf_op jit(solution)/shard_map/cond/branch_1_fun/ppermute | solution.py:282
  12.9 13.5 %copy-start = (s32[2]{0:T(128)S(1)}, s32[2]{0:T(128)}, u32[]{:S(2)}) copy-start(s32[2]{0:T(128)} %len_ref.1) | copy-start | bytes 28
  16.2 1.9 %collective-permute-start.4 = (bf16[128,512]{1,0:T(8,128)(2,1)S(1)}, bf16[128,512]{1,0:T(8,128)(2,1)S(1)}, u32[]{:S(2)}, u32[]{:S(2)}) collective-permute-start(bf16[128,512]{1,0:T(8,128)(2,1)S(1)} %get-tuple-element.39), channel_id=1, source_target_pairs={{0,1},{1,0},{2,3},{3,2},{4,5},{5,4},{6,7},{7,6},{8,9},{9,8},{10,11... | collective-permute-start | bytes 393224 | tf_op jit(solution)/shard_map/ppermute | solution.py:282
  16.3 6.4 %collective-permute-start.5 = (bf16[128,512]{1,0:T(8,128)(2,1)S(1)}, bf16[128,512]{1,0:T(8,128)(2,1)S(1)}, u32[]{:S(2)}, u32[]{:S(2)}) collective-permute-start(bf16[128,512]{1,0:T(8,128)(2,1)S(1)} %get-tuple-element.38.own.own_ref), channel_id=1, source_target_pairs={{0,2},{1,3},{2,0},{3,1},{4,6},{5,7},{6,4},{7,5},{8,10},{9,11},{10,... | collective-permute-start | bytes 393224 | tf_op jit(solution)/shard_map/ppermute | solution.py:282
  17.9 6.7 %collective-permute-start.6 = (bf16[128,512]{1,0:T(8,128)(2,1)S(1)}, bf16[128,512]{1,0:T(8,128)(2,1)S(1)}, u32[]{:S(2)}, u32[]{:S(2)}) collective-permute-start(bf16[128,512]{1,0:T(8,128)(2,1)S(1)} %get-tuple-element.39), channel_id=1, source_target_pairs={{0,3},{1,2},{2,1},{3,0},{4,7},{5,6},{6,5},{7,4},{8,11},{9,10},{10,... | collective-permute-start | bytes 393224 | tf_op jit(solution)/shard_map/ppermute | solution.py:282
  18.2 8.2 %collective-permute-start.7 = (bf16[16,512]{1,0:T(8,128)(2,1)S(1)}, bf16[16,512]{1,0:T(8,128)(2,1)S(1)}, u32[]{:S(2)}, u32[]{:S(2)}) collective-permute-start(bf16[16,512]{1,0:T(8,128)(2,1)S(1)} %shard_map.48), channel_id=1, source_target_pairs={{0,6},{1,7},{2,4},{3,5},{4,2},{5,3},{6,0},{7,1},{8,14},{9,15},{10,... | collective-permute-start | bytes 49160 | tf_op jit(solution)/shard_map/ppermute | solution.py:282
  20.8 5.7 %collective-permute-start.8 = (bf16[16,512]{1,0:T(8,128)(2,1)S(1)}, bf16[16,512]{1,0:T(8,128)(2,1)S(1)}, u32[]{:S(2)}, u32[]{:S(2)}) collective-permute-start(bf16[16,512]{1,0:T(8,128)(2,1)S(1)} %shard_map.48), channel_id=1, source_target_pairs={{0,4},{1,5},{2,6},{3,7},{4,0},{5,1},{6,2},{7,3},{8,12},{9,13},{10,... | collective-permute-start | bytes 49160 | tf_op jit(solution)/shard_map/ppermute | solution.py:282
  30.4 12.5 %collective-permute-start.10 = (bf16[128,512]{1,0:T(8,128)(2,1)S(1)}, bf16[128,512]{1,0:T(8,128)(2,1)S(1)}, u32[]{:S(2)}, u32[]{:S(2)}) collective-permute-start(bf16[128,512]{1,0:T(8,128)(2,1)S(1)} %get-tuple-element.42), channel_id=1, source_target_pairs={{0,6},{1,7},{2,0},{3,1},{4,2},{5,3},{6,4},{7,5},{8,14},{9,15},{10,... | collective-permute-start | bytes 393224 | tf_op jit(solution)/shard_map/ppermute | solution.py:282
  35.8 7.2 %collective-permute-start.11 = (bf16[128,512]{1,0:T(8,128)(2,1)S(1)}, bf16[128,512]{1,0:T(8,128)(2,1)S(1)}, u32[]{:S(2)}, u32[]{:S(2)}) collective-permute-start(bf16[128,512]{1,0:T(8,128)(2,1)S(1)} %get-tuple-element.43), channel_id=1, source_target_pairs={{0,7},{1,6},{2,1},{3,0},{4,3},{5,2},{6,5},{7,4},{8,15},{9,14},{10,... | collective-permute-start | bytes 393224 | tf_op jit(solution)/shard_map/ppermute | solution.py:282
  35.8 7.2 %collective-permute-start.9 = (bf16[128,512]{1,0:T(8,128)(2,1)S(1)}, bf16[128,512]{1,0:T(8,128)(2,1)S(1)}, u32[]{:S(2)}, u32[]{:S(2)}) collective-permute-start(bf16[128,512]{1,0:T(8,128)(2,1)S(1)} %get-tuple-element.41), channel_id=1, source_target_pairs={{0,1},{1,0},{2,3},{3,2},{4,5},{5,4},{6,7},{7,6},{8,9},{9,8},{10,11... | collective-permute-start | bytes 393224 | tf_op jit(solution)/shard_map/ppermute | solution.py:282
  36.0 6.3 %collective-permute-start.12 = (bf16[16,512]{1,0:T(8,128)(2,1)S(1)}, bf16[16,512]{1,0:T(8,128)(2,1)S(1)}, u32[]{:S(2)}, u32[]{:S(2)}) collective-permute-start(bf16[16,512]{1,0:T(8,128)(2,1)S(1)} %get-tuple-element.44), channel_id=1, source_target_pairs={{0,6},{1,5},{2,4},{3,7},{4,2},{5,1},{6,0},{7,3},{8,14},{9,13},{10,... | collective-permute-start | bytes 49160 | tf_op jit(solution)/shard_map/ppermute | solution.py:282
  38.9 4.1 %collective-permute-start.13 = (bf16[16,512]{1,0:T(8,128)(2,1)S(1)}, bf16[16,512]{1,0:T(8,128)(2,1)S(1)}, u32[]{:S(2)}, u32[]{:S(2)}) collective-permute-start(bf16[16,512]{1,0:T(8,128)(2,1)S(1)} %get-tuple-element.45), channel_id=1, source_target_pairs={{0,6},{1,5},{2,7},{3,4},{4,2},{5,1},{6,3},{7,0},{8,14},{9,13},{10,... | collective-permute-start | bytes 49160 | tf_op jit(solution)/shard_map/ppermute | solution.py:282

commit v3 on v2

v3 whole, which is shorter than its diff:
```python
import functools
import math

import jax
import jax.numpy as jnp
from jax import lax
from jax.experimental import pallas as pl
from jax.experimental.pallas import tpu as pltpu
from jax.sharding import PartitionSpec as P

H = 32
KVH = 4
HD = 128
REACH = 5
GROUP = REACH - 1
SHARE = H // KVH
PARTS = KVH // 2
WIDE = SHARE * HD
MASKED = -1e30
F32 = jnp.float32
BF16 = jnp.bfloat16
NT = (((1,), (1,)), ((), ()))
NN = (((1,), (0,)), ((), ()))


def place():
    me = lax.axis_index("ctx")
    rank = lax.rem(me, GROUP)
    return me, rank, lax.rem(rank, 2)


def call(body, out, mib=8, flops=1000, **more):
    return pl.pallas_call(
        body,
        out_shape=out,
        compiler_params=pltpu.CompilerParams(vmem_limit_bytes=mib * 2**20),
        cost_estimate=pl.CostEstimate(flops=flops, bytes_accessed=1000, transcendentals=0),
        **more,
    )


def columns(head):
    return pl.ds(pl.multiple_of(head * HD, HD), HD)


def split_kernel(kv_ref, far, *parts):
    _, _, core = place()
    for half, refs in ((core, parts[:PARTS]), (1 - core, parts[PARTS:])):
        for part, ref in enumerate(refs):
            for kind in range(2):
                block = kv_ref[0, :, columns(half * PARTS + part + kind * KVH)]
                ref[:, pl.ds(kind * HD, HD)] = block
                if half is not core:
                    far[:, pl.ds((part * 2 + kind) * HD, HD)] = block


def edge_rows(docs):
    return -(-SHARE * docs // 16) * 16


def hand_kernel(halo, docs, q_ref, g_ref, far, edge0, edge1, q_top, g_top, sem):
    _, _, core = place()
    rows = q_ref.shape[1]
    wide = PARTS * WIDE
    start = pl.multiple_of((1 - core) * wide, wide)
    tops = [(ref.at[0, pl.ds(0, halo)], top) for ref, top in ((q_ref, q_top), (g_ref, g_top))]
    whole = [
        (ref.at[0, :, pl.ds(start, wide)], far.at[pl.ds(at * rows, rows)]) for at, ref in enumerate((q_ref, g_ref))
    ]
    copies = [pltpu.make_async_copy(*copy, sem.at[at]) for at, copy in enumerate(tops + whole)]
    for copy in copies:
        copy.start()
    size = edge_rows(docs)
    to = lax.broadcasted_iota(jnp.int32, (size, SHARE * halo), 0)
    at = lax.broadcasted_iota(jnp.int32, (size, SHARE * halo), 1)
    picked = ((at // halo == to // docs) & (at % halo == to % docs)).astype(BF16)
    for copy in copies[:2]:
        copy.wait()
    for kind, top in enumerate((q_top, g_top)):
        for half, edge in enumerate((edge0, edge1)):
            for part in range(PARTS):
                heads = [(half * PARTS + part) * SHARE + head for head in range(SHARE)]
                block = jnp.concatenate([top[:, pl.ds(head * HD, HD)] for head in heads], axis=0)
                chosen = lax.dot_general(picked, block, NN, preferred_element_type=F32).astype(BF16)
                edge[pl.ds((kind * PARTS + part) * size, size), :] = chosen
    for copy in copies[2:]:
        copy.wait()


def edge_kernel(*refs):
    *own, one, edge = refs
    _, rank, _ = place()
    halo = edge.shape[0]
    first = pl.ds(pl.multiple_of(jnp.where(rank < 2, 0, one.shape[0] - halo), 16), halo)
    for part, ref in enumerate(own):
        cols = pl.ds(part * 2 * HD, 2 * HD)
        edge[:, cols] = jnp.where((rank == 0) | (rank == GROUP - 1), ref[first, :], one[first, cols])


def stage_kernel(q_ref, g_ref, far, edge0, edge1, q_buf, g_buf, sem):
    _, _, core = place()
    rows = q_ref.shape[1]
    copies = []
    for kind, (ref, buf) in enumerate(((q_ref, q_buf), (g_ref, g_buf))):
        for part in range(PARTS):
            for head in range(SHARE):
                here = head * rows
                mine = ref.at[0, :, columns((core * PARTS + part) * SHARE + head)]
                other = far.at[pl.ds(kind * rows, rows), pl.ds((part * SHARE + head) * HD, HD)]
                for slot, block in ((core, mine), (1 - core, other)):
                    at = pl.ds(pl.multiple_of(slot * WIDE + here, 16), rows)
                    copies.append((block, buf.at[part, at]))
    copies = [pltpu.make_async_copy(*copy, sem.at[at]) for at, copy in enumerate(copies)]
    for copy in copies:
        copy.start()
    size = edge0.shape[0] // (2 * PARTS)
    for half, edge in enumerate((edge0, edge1)):

        @pl.when(core == half)
        def _():
            extra = []
            for kind, buf in enumerate((q_buf, g_buf)):
                for part in range(PARTS):
                    block = edge.at[pl.ds((kind * PARTS + part) * size, size)]
                    to = buf.at[part, pl.ds(2 * WIDE, size)]
                    extra.append(pltpu.make_async_copy(block, to, sem.at[len(copies) + len(extra)]))
            for copy in extra:
                copy.start()
            for copy in extra:
                copy.wait()

    for copy in copies:
        copy.wait()


def doc_start(pos, len_ref):
    start = jnp.zeros_like(pos)
    end = jnp.int32(0)
    for doc in range(len_ref.shape[0]):
        end = end + len_ref[doc]
        start = jnp.where(end <= pos, end, start)
    return start


def bias_of(first_key, keys, query_pos, start):
    key_pos = first_key + lax.broadcasted_iota(jnp.int32, (keys, query_pos.shape[1]), 0)
    return jnp.where((key_pos >= start) & (key_pos <= query_pos), 0.0, MASKED)


def weigh(key, value, query, cot, bias, keep):
    scores = lax.dot_general(key, query, NT, preferred_element_type=F32) + bias
    top = jnp.max(scores, axis=0, keepdims=True)
    raw = jnp.exp2((scores - top) * (HD**-0.5 * math.log2(math.e)))
    dweights = lax.dot_general(value, cot, NT, preferred_element_type=F32)
    share = keep / jnp.sum(raw, axis=0, keepdims=True)
    delta = jnp.sum(raw * dweights, axis=0, keepdims=True) * share
    weights = raw * share
    dscores = weights * (dweights - delta)
    return weights.astype(BF16), dscores.astype(BF16)


def grad_kernel(stage, halo, len_ref, q_buf, g_buf, *refs):
    if stage:
        dk_last, dv_last, *refs = refs
    *got, edge_a, edge_b, dk_ref, dv_ref, k_buf, v_buf = refs
    rows = got[0].shape[0]
    span = GROUP * rows
    me, rank, _ = place()
    first = (me - rank) * rows
    docs = len_ref.shape[0]

    def load(part, blocks):
        here = pl.ds(part * 2 * HD, 2 * HD)
        low, high = jnp.where(rank < 2, edge_a[:, here], edge_b[:, here]), edge_b[:, here]
        for buf, kind in ((k_buf, 0), (v_buf, HD)):
            for step, block in enumerate(blocks):
                at = pl.ds(pl.multiple_of(halo + (rank ^ step) * rows, 16), rows)
                buf[part, at, :] = block[:, kind : kind + HD]
            buf[part, :halo, :] = low[:, kind : kind + HD]
            buf[part, halo + span :, :] = high[:, kind : kind + HD]

    own, one, two, three = got[:4]
    here = pl.ds(stage * 2 * HD, 2 * HD)
    load(stage, (own[...], one[:, here], two[...], three[...]))
    if stage:
        dk_ref[...] = dk_last[...]
        dv_ref[...] = dv_last[...]
    else:
        for part, own in enumerate(got[4:], 1):
            load(part, (own[...], one[:, pl.ds(part * 2 * HD, 2 * HD)]))
        dk_ref[...] = jnp.zeros_like(dk_ref)
        dv_ref[...] = jnp.zeros_like(dv_ref)

    for chip in range(2):

        @pl.when(rank // 2 == chip)
        def _():
            tiles = []
            for part in (stage,) if chip else range(0 if stage == 0 else PARTS, PARTS):
                for slot in range(2):
                    block = 2 * chip + slot
                    query_pos = first + block * rows + lax.broadcasted_iota(jnp.int32, (1, rows), 1)
                    start = doc_start(query_pos, len_ref)
                    keep = jnp.where(start < first - halo, 0.0, 1.0)
                    tiles.append((part, pl.ds(slot * WIDE, WIDE), 0, halo + (block + 1) * rows, query_pos, start, keep, SHARE))
            if chip == 0:
                size = edge_rows(docs)
                lane = lax.broadcasted_iota(jnp.int32, (1, size), 1)
                query_pos = first + span + lax.rem(lane, docs)
                start = doc_start(query_pos, len_ref)
                keep = jnp.where((start < first + span - halo) & (lane < SHARE * docs), 1.0, 0.0)
                tiles.append((stage, pl.ds(2 * WIDE, size), halo, halo + span + halo, query_pos, start, keep, 1))
            for part, cols, low, high, query_pos, start, keep, times in tiles:
                keys = pl.ds(low, high - low)
                bias = bias_of(first - halo + low, high - low, query_pos, start)
                query, cot = q_buf[part, cols, :], g_buf[part, cols, :]
                weights, dscores = weigh(
                    k_buf[part, keys, :], v_buf[part, keys, :], query, cot,
                    jnp.concatenate([bias] * times, axis=1), jnp.concatenate([keep] * times, axis=1),
                )
                dv_ref[part, keys, :] += lax.dot_general(weights, cot, NN, preferred_element_type=F32)
                dk_ref[part, keys, :] += lax.dot_general(dscores, query, NN, preferred_element_type=F32)


def terms(dk_ref, dv_ref, part, row, size):
    at = pl.ds(row if isinstance(row, int) else pl.multiple_of(row, 16), size)
    return jnp.concatenate([dk_ref[part, at, :] * HD**-0.5, dv_ref[part, at, :]], axis=1)


def across_kernel(part, halo, dk_ref, dv_ref, across):
    _, rank, _ = place()
    kv = 2 * HD
    rows = across.shape[0] - (0 if part else halo)
    for which in range(PARTS):
        cols = pl.ds(which * kv, kv)
        across[:rows, cols] = terms(dk_ref, dv_ref, part, halo + (rank ^ (2 + which)) * rows, rows).astype(BF16)
        if not part:
            across[rows:, cols] = terms(dk_ref, dv_ref, which, 0, halo).astype(BF16)


def ends_kernel(halo, dk_ref, dv_ref, across, ends):
    _, rank, _ = place()
    kv = 2 * HD
    rows = across.shape[0] - halo
    for part in range(PARTS):
        cols = pl.ds(part * kv, kv)
        before = terms(dk_ref, dv_ref, part, 0, halo) + across[rows:, cols].astype(F32)
        behind = terms(dk_ref, dv_ref, part, halo + GROUP * rows, halo)
        ends[:, cols] = jnp.where(rank < 2, behind, before).astype(BF16)


def join_kernel(dk_ref, dv_ref, across0, across1, ends, mine, other):
    kv = 2 * HD
    halo, (rows, _) = ends.shape[0], mine.shape
    _, rank, _ = place()
    for ref, step, first, last in ((mine, 0, 0, GROUP - 1), (other, 1, 1, GROUP - 2)):
        for part, across in enumerate((across0, across1)):
            cols = pl.ds(part * kv, kv)
            total = terms(dk_ref, dv_ref, part, halo + (rank ^ step) * rows, rows)
            total = total + across[:rows, pl.ds(step * kv, kv)].astype(F32)
            end = ends[:, cols].astype(F32)
            low = total[:halo] + jnp.where(rank == first, end, 0.0)
            high = total[rows - halo :] + jnp.where(rank == last, end, 0.0)
            ref[:, cols] = jnp.concatenate([low, total[halo : rows - halo], high], axis=0).astype(ref.dtype)


def grads(stage, halo, rows, *inputs):
    total = (PARTS, halo + GROUP * rows + halo, HD)
    vmem = pl.BlockSpec(memory_space=pltpu.VMEM)
    return call(
        functools.partial(grad_kernel, stage, halo),
        [jax.ShapeDtypeStruct(total, F32)] * 2,
        in_specs=[pl.BlockSpec(memory_space=pltpu.SMEM)] + [vmem] * (len(inputs) - 1),
        scratch_shapes=[pltpu.VMEM(total, BF16)] * 2,
        mib=24,
        flops=COST,
    )(*inputs)


COST = 4 * 10**9


def place_kernel(mine, other, out_ref):
    _, _, core = place()
    for part in range(PARTS):
        for kind in range(2):
            cols = pl.ds((part * 2 + kind) * HD, HD)
            for half in range(2):
                total = jnp.where(core == half, mine[:, cols], other[:, cols].astype(F32))
                out_ref[0, :, pl.ds((kind * KVH + half * PARTS + part) * HD, HD)] = total.astype(out_ref.dtype)


def on_device(queries, stash, grad_out, lengths):
    rows = queries.shape[1]
    pipe, ctx = lax.axis_size("pipe"), lax.axis_size("ctx")
    halo = -(-lengths.shape[0] // 16) * 16
    high = 1 << (pipe.bit_length() - 2)

    def pairs(pick):
        return [(c, (c + pick[c % GROUP]) % ctx) for c in range(ctx)]

    def partner(block, pick):
        route = [((p ^ high) * ctx + c, p * ctx + d) for p in range(pipe) for c, d in pairs(pick)]
        return lax.ppermute(block, ("pipe", "ctx"), route)

    def along(block, pick):
        return lax.ppermute(block, "ctx", pairs(pick))

    stay = (0,) * GROUP
    flip = [tuple((rank ^ step) - rank for rank in range(GROUP)) for step in range(GROUP)]

    def shape(*dims):
        return jax.ShapeDtypeStruct(dims, BF16)

    def after(value, *others):
        return lax.optimization_barrier((value, *others))[0]

    edge_wide = 2 * PARTS * HD
    hbm = pl.BlockSpec(memory_space=pltpu.HBM)
    held = partner(stash, stay)

    wide = PARTS * WIDE
    size = edge_rows(lengths.shape[0])

    def beside(queries, grad_out):
        far, edge0, edge1 = call(
            functools.partial(hand_kernel, halo, lengths.shape[0]),
            [shape(2 * rows, wide), *[shape(2 * PARTS * size, HD)] * 2],
            in_specs=[hbm] * 2,
            scratch_shapes=[pltpu.VMEM((halo, 2 * wide), BF16)] * 2 + [pltpu.SemaphoreType.DMA((4,))],
        )(queries, grad_out)
        return along(far, flip[1]), along(edge0, (-4, -4, 4, 4)), along(edge1, (-3, -5, 5, 3))

    def nothing(*_):
        return jnp.zeros((2 * rows, wide), BF16), *[jnp.zeros((2 * PARTS * size, HD), BF16)] * 2

    far, edge0, edge1 = lax.cond(lengths[0] > 0, beside, nothing, queries, grad_out)
    q_buf, g_buf = call(
        stage_kernel,
        [shape(PARTS, 2 * WIDE + size, HD)] * 2,
        in_specs=[hbm] * 5,
        scratch_shapes=[pltpu.SemaphoreType.DMA((4 * PARTS * SHARE + 2 * PARTS,))],
    )(queries, grad_out, far, edge0, edge1)
    held, q_buf, g_buf = lax.optimization_barrier((held, q_buf, g_buf))
    far, *parts = call(split_kernel, [shape(rows, edge_wide), *[shape(rows, 2 * HD)] * (2 * PARTS)])(held)
    owns, fars = parts[:PARTS], parts[PARTS:]

    one = along(far, flip[1])
    got = [(own, one, along(own, flip[2]), along(far, flip[3])) for own, far in zip(owns, fars)]
    edge = call(edge_kernel, shape(halo, edge_wide))(*owns, one)
    edges = along(edge, (2, 2, 2, 2)), along(edge, (-4, -4, 4, 4))
    raw = grads(0, halo, rows, lengths, q_buf, g_buf, *got[0], *owns[1:], *edges)
    first = call(functools.partial(across_kernel, 0, halo), shape(rows + halo, edge_wide))(*raw)
    first = along(first, flip[2])
    raw = grads(1, halo, rows, lengths, q_buf, g_buf, *raw, *got[1], *edges)
    second = along(call(functools.partial(across_kernel, 1, halo), shape(rows, edge_wide))(*raw), flip[2])
    ends = along(call(functools.partial(ends_kernel, halo), shape(halo, edge_wide))(*raw, first), (4, 4, -4, -4))
    mine, other = call(
        join_kernel, [jax.ShapeDtypeStruct((rows, edge_wide), F32), shape(rows, edge_wide)]
    )(*raw, first, second, ends)
    return call(place_kernel, shape(1, rows, 2 * KVH * HD))(mine, along(other, flip[1]))


def solution(mesh):
    placed = (P("pipe", "ctx", None), P("pipe", "ctx", None), P("pipe", "ctx", None), P())
    return jax.shard_map(
        on_device, mesh=mesh, in_specs=placed, out_specs=P("pipe", "ctx", None), check_vma=False
    )
```

time: 44.1 us -> 41.3 us (0.937)
  starting transfers between devices: 20.4 us -> 17.4 us
  Pallas kernels: 8.49 us -> 10.1 us
  waiting for transfers between devices: 14.2 us -> 12.8 us
    ppermute x13 -> x14, waiting for transfers between devices: 13.1 us -> 9.88 us  [along(): return lax.ppermute(block, 'ctx', pairs(pick))]
    ppermute x13 -> x14, starting transfers between devices: 16.3 us -> 13.4 us  [along(): return lax.ppermute(block, 'ctx', pairs(pick))]
    ppermute x1, waiting for transfers between devices: 1.11 us -> 2.93 us  [partner(): return lax.ppermute(block, ('pipe', 'ctx'), route)]
    pallas_call x4 -> x9, Pallas kernels: 4.93 us -> 6.48 us  [the longest x2 5.48 us: grads(): call(functools.partial(grad_kernel, stage, halo), [jax.ShapeDtypeStruct(t...]
  transfers between devices with their start and end apart: 14 -> 15, of which waited for: 8 -> 8; matrix products, arithmetic and copies ran while one was open for 0% -> 0% of each run, Pallas kernels for 8% -> 22%
where the time goes in v3:
time: 41.3 us; the launch traced here: 41 us
  starting transfers between devices  17.4 us (42%)
  waiting for transfers between devices  12.8 us (31%)
  Pallas kernels  10.1 us (24%)
  between operations  0.73 us (2%)
    ppermute x14, starting transfers between devices, along(): return lax.ppermute(block, 'ctx', pairs(pick))  13.4 us
    ppermute x14, waiting for transfers between devices, along(): return lax.ppermute(block, 'ctx', pairs(pick))  9.88 us
    pallas_call x2, Pallas kernels, grads(): call(functools.partial(grad_kernel, stage, halo), [jax.ShapeDtypeStruct(t...  5.48 us
    ppermute x1, starting transfers between devices, partner(): return lax.ppermute(block, ('pipe', 'ctx'), route)  4.04 us
    ppermute x1, waiting for transfers between devices, partner(): return lax.ppermute(block, ('pipe', 'ctx'), route)  2.93 us
    pallas_call x1, Pallas kernels, on_device(): call(stage_kernel, [shape(PARTS, 2 * WIDE + size, HD)] * 2, in_specs=[hbm...  2.2 us
    pallas_call x1, Pallas kernels, beside(): call(functools.partial(hand_kernel, halo, lengths.shape[0]), [shape(2 * r...  1.38 us
  transfers between devices with their start and end apart: 15, of which 8 were waited for; matrix products, arithmetic and copies ran while one was open for 0% of the time, Pallas kernels for 22%

profile of v3, /device:TPU:0, one launch (start us, length us, event | category | flops | bytes accessed | tf_op | source)
XLA Modules:
  0.0 41.0 jit_solution(10825508705283340053)
XLA Ops:
  0.0 4.0 %collective-permute-start.3 = (bf16[1,128,1024]{2,1,0:T(8,128)(2,1)}, bf16[1,128,1024]{2,1,0:T(8,128)(2,1)S(1)}, u32[]{:S(2)}, u32[]{:S(2)}) collective-permute-start(bf16[1,128,1024]{2,1,0:T(8,128)(2,1)} %param.7), channel_id=1, source_target_pairs={{16,0},{17,1},{18,2},{19,3},{20,4},{21,5},{22,6},{23,7},{24,8},{25... | collective-permute-start | bytes 786440 | tf_op jit(solution)/shard_map/ppermute | solution.py:304
  4.7 6.3 %conditional.1 = (bf16[256,2048]{1,0:T(8,128)(2,1)}, bf16[64,128]{1,0:T(8,128)(2,1)}, bf16[64,128]{1,0:T(8,128)(2,1)}) conditional(s32[]{:T(128)} %bitcast, () %tuple.14, (bf16[1,128,4096]{2,1,0:T(8,128)(2,1)}, bf16[1,128,4096]{2,1,0:T(8,128)(2,1)}) %tuple.15), branch_computations={%region_0.0_spmd, %region_1.0_spmd} | conditional | flops 1000 | bytes 4326520 | solution.py:337
  4.7 1.4 %branch_1_fun.1 = (bf16[256,2048]{1,0:T(8,128)(2,1)S(1)}, bf16[64,128]{1,0:T(8,128)(2,1)S(1)}, bf16[64,128]{1,0:T(8,128)(2,1)S(1)}) custom-call(bf16[1,128,4096]{2,1,0:T(8,128)(2,1)} %get-tuple-element.9.q_ref, bf16[1,128,4096]{2,1,0:T(8,128)(2,1)} %get-tuple-element.10.g_ref), custom_call_target="tpu_custom_call" | custom-call | flops 1000 | bytes 1000 | tf_op jit(solution)/shard_map/cond/branch_1_fun/pallas_call | solution.py:326
  6.1 0.1 collective-permute-start
  6.2 1.6 %collective-permute-start.1 = (bf16[64,128]{1,0:T(8,128)(2,1)S(1)}, bf16[64,128]{1,0:T(8,128)(2,1)}, u32[]{:S(2)}, u32[]{:S(2)}) collective-permute-start(bf16[64,128]{1,0:T(8,128)(2,1)S(1)} %get-tuple-element.12), channel_id=1, source_target_pairs={{0,4},{1,5},{2,6},{3,7},{4,0},{5,1},{6,2},{7,3},{8,12},{9,13},{10,... | collective-permute-start | bytes 49160 | tf_op jit(solution)/shard_map/cond/branch_1_fun/ppermute | solution.py:307
  7.8 0.3 collective-permute-start.2
  8.0 2.0 %collective-permute-done.1 = bf16[64,128]{1,0:T(8,128)(2,1)} collective-permute-done((bf16[64,128]{1,0:T(8,128)(2,1)S(1)}, bf16[64,128]{1,0:T(8,128)(2,1)}, u32[]{:S(2)}, u32[]{:S(2)}) %collective-permute-start.1) | collective-permute-done | bytes 16416 | tf_op jit(solution)/shard_map/cond/branch_1_fun/ppermute | solution.py:307
  10.1 0.9 %collective-permute-done.2 = bf16[64,128]{1,0:T(8,128)(2,1)} collective-permute-done((bf16[64,128]{1,0:T(8,128)(2,1)S(1)}, bf16[64,128]{1,0:T(8,128)(2,1)}, u32[]{:S(2)}, u32[]{:S(2)}) %collective-permute-start.2) | collective-permute-done | bytes 16416 | tf_op jit(solution)/shard_map/cond/branch_1_fun/ppermute | solution.py:307
  11.0 0.0 collective-permute-done
  11.0 0.0 copy-start
  11.0 2.2 %shard_map.46 = (bf16[2,2064,128]{2,1,0:T(8,128)(2,1)S(1)}, bf16[2,2064,128]{2,1,0:T(8,128)(2,1)S(1)}) custom-call(bf16[1,128,4096]{2,1,0:T(8,128)(2,1)} %q_ref.1, bf16[1,128,4096]{2,1,0:T(8,128)(2,1)} %g_ref.1, bf16[256,2048]{1,0:T(8,128)(2,1)} %get-tuple-element.33.far, bf16[64,128]{1,0:T(8,128)(2,1)} %get-tuple-element.34.edge0, ...), custom_call_target="tpu_custom_call" | custom-call | flops 1000 | bytes 1000 | tf_op jit(solution)/shard_map/pallas_call | solution.py:338
  13.2 2.9 %collective-permute-done.3.kv_ref = bf16[1,128,1024]{2,1,0:T(8,128)(2,1)S(1)} collective-permute-done((bf16[1,128,1024]{2,1,0:T(8,128)(2,1)}, bf16[1,128,1024]{2,1,0:T(8,128)(2,1)S(1)}, u32[]{:S(2)}, u32[]{:S(2)}) %collective-permute-start.3) | collective-permute-done | bytes 262176 | tf_op jit(solution)/shard_map/ppermute | solution.py:304
  16.2 0.1 shard_map.47
  16.2 0.1 collective-permute-start.4
  16.3 1.7 %collective-permute-start.6 = (bf16[128,256]{1,0:T(8,128)(2,1)S(1)}, bf16[128,256]{1,0:T(8,128)(2,1)S(1)}, u32[]{:S(2)}, u32[]{:S(2)}) collective-permute-start(bf16[128,256]{1,0:T(8,128)(2,1)S(1)} %get-tuple-element.43), channel_id=1, source_target_pairs={{0,3},{1,2},{2,1},{3,0},{4,7},{5,6},{6,5},{7,4},{8,11},{9,10},{10,... | collective-permute-start | bytes 196616 | tf_op jit(solution)/shard_map/ppermute | solution.py:307
  18.0 0.5 %collective-permute-start.5 = (bf16[128,256]{1,0:T(8,128)(2,1)S(1)}, bf16[128,256]{1,0:T(8,128)(2,1)S(1)}, u32[]{:S(2)}, u32[]{:S(2)}) collective-permute-start(bf16[128,256]{1,0:T(8,128)(2,1)S(1)} %get-tuple-element.41.refs_0_), channel_id=1, source_target_pairs={{0,2},{1,3},{2,0},{3,1},{4,6},{5,7},{6,4},{7,5},{8,10},{9,11},{10,... | collective-permute-start | bytes 196616 | tf_op jit(solution)/shard_map/ppermute | solution.py:307
  18.5 0.0 collective-permute-done.4.refs_2_.refs_1_.refs_3_
  18.5 1.6 %collective-permute-start.8 = (bf16[16,512]{1,0:T(8,128)(2,1)S(1)}, bf16[16,512]{1,0:T(8,128)(2,1)S(1)}, u32[]{:S(2)}, u32[]{:S(2)}) collective-permute-start(bf16[16,512]{1,0:T(8,128)(2,1)S(1)} %shard_map.48), channel_id=1, source_target_pairs={{0,4},{1,5},{2,6},{3,7},{4,0},{5,1},{6,2},{7,3},{8,12},{9,13},{10,... | collective-permute-start | bytes 49160 | tf_op jit(solution)/shard_map/ppermute | solution.py:307
  20.1 1.5 %collective-permute-start.7 = (bf16[16,512]{1,0:T(8,128)(2,1)S(1)}, bf16[16,512]{1,0:T(8,128)(2,1)S(1)}, u32[]{:S(2)}, u32[]{:S(2)}) collective-permute-start(bf16[16,512]{1,0:T(8,128)(2,1)S(1)} %shard_map.48), channel_id=1, source_target_pairs={{0,2},{1,3},{2,4},{3,5},{4,6},{5,7},{6,0},{7,1},{8,10},{9,11},{10,... | collective-permute-start | bytes 49160 | tf_op jit(solution)/shard_map/ppermute | solution.py:307
  21.6 0.4 %collective-permute-start.9 = (bf16[128,256]{1,0:T(8,128)(2,1)S(1)}, bf16[128,256]{1,0:T(8,128)(2,1)S(1)}, u32[]{:S(2)}, u32[]{:S(2)}) collective-permute-start(bf16[128,256]{1,0:T(8,128)(2,1)S(1)} %get-tuple-element.44.refs_1_.refs_4_.refs_2_), channel_id=1, source_target_pairs={{0,2},{1,3},{2,0},{3,1},{4,6},{5,7},{6,4},{7,5},{8,10},{9,11},{10,... | collective-permute-start | bytes 196616 | tf_op jit(solution)/shard_map/ppermute | solution.py:307
  22.0 0.0 collective-permute-done.6.refs_3_
  22.0 0.3 collective-permute-start.10
  22.3 0.1 collective-permute-done.5.refs_2_
  22.4 0.0 collective-permute-done.8.refs_6_.refs_7_
  22.4 2.3 %collective-permute-done.7.refs_5_.refs_6_ = bf16[16,512]{1,0:T(8,128)(2,1)S(1)} collective-permute-done((bf16[16,512]{1,0:T(8,128)(2,1)S(1)}, bf16[16,512]{1,0:T(8,128)(2,1)S(1)}, u32[]{:S(2)}, u32[]{:S(2)}) %collective-permute-start.7) | collective-permute-done | bytes 16416 | tf_op jit(solution)/shard_map/ppermute | solution.py:307
  24.7 0.0 copy-done
  24.7 4.1 %shard_map.49 = (f32[2,544,128]{2,1,0:T(8,128)S(1)}, f32[2,544,128]{2,1,0:T(8,128)S(1)}) custom-call(s32[2]{0:T(128)S(1)} %copy-done, bf16[2,2064,128]{2,1,0:T(8,128)(2,1)S(1)} %get-tuple-element.38.q_buf, bf16[2,2064,128]{2,1,0:T(8,128)(2,1)S(1)} %get-tuple-element.39.g_buf, bf16[128,256]{1,0:T(8,128)(2,1)S(1)} %get-tuple-element.41.refs_0_, ...), custom_call_target="tpu_custom_call" | custom-call | flops 4000000000 | bytes 1000 | tf_op jit(solution)/shard_map/pallas_call | solution.py:270
  28.9 0.3 collective-permute-start.11
  29.2 0.0 collective-permute-done.10.refs_5_
  29.2 0.0 collective-permute-done.9.refs_4_
  29.2 1.3 %shard_map.50 = (f32[2,544,128]{2,1,0:T(8,128)S(1)}, f32[2,544,128]{2,1,0:T(8,128)S(1)}) custom-call(s32[2]{0:T(128)S(1)} %copy-done, bf16[2,2064,128]{2,1,0:T(8,128)(2,1)S(1)} %get-tuple-element.38.q_buf, bf16[2,2064,128]{2,1,0:T(8,128)(2,1)S(1)} %get-tuple-element.39.g_buf, f32[2,544,128]{2,1,0:T(8,128)S(1)} %get-tuple-element.45.refs_0_.dk_ref, ...), custom_call_target="tpu_custom_call" | custom-call | flops 4000000000 | bytes 1000 | tf_op jit(solution)/shard_map/pallas_call | solution.py:270
  30.6 4.3 %collective-permute-start.12 = (bf16[128,512]{1,0:T(8,128)(2,1)S(1)}, bf16[128,512]{1,0:T(8,128)(2,1)S(1)}, u32[]{:S(2)}, u32[]{:S(2)}) collective-permute-start(bf16[128,512]{1,0:T(8,128)(2,1)S(1)} %shard_map.52), channel_id=1, source_target_pairs={{0,2},{1,3},{2,0},{3,1},{4,6},{5,7},{6,4},{7,5},{8,10},{9,11},{10,... | collective-permute-start | bytes 393224 | tf_op jit(solution)/shard_map/ppermute | solution.py:307
  34.9 0.0 collective-permute-done.11.across.across0
  35.0 0.7 %collective-permute-start.13 = (bf16[16,512]{1,0:T(8,128)(2,1)S(1)}, bf16[16,512]{1,0:T(8,128)(2,1)S(1)}, u32[]{:S(2)}, u32[]{:S(2)}) collective-permute-start(bf16[16,512]{1,0:T(8,128)(2,1)S(1)} %shard_map.53), channel_id=1, source_target_pairs={{0,4},{1,5},{2,6},{3,7},{4,0},{5,1},{6,2},{7,3},{8,12},{9,13},{10,... | collective-permute-start | bytes 49160 | tf_op jit(solution)/shard_map/ppermute | solution.py:307
  35.6 2.2 %collective-permute-done.12.across1 = bf16[128,512]{1,0:T(8,128)(2,1)S(1)} collective-permute-done((bf16[128,512]{1,0:T(8,128)(2,1)S(1)}, bf16[128,512]{1,0:T(8,128)(2,1)S(1)}, u32[]{:S(2)}, u32[]{:S(2)}) %collective-permute-start.12) | collective-permute-done | bytes 131104 | tf_op jit(solution)/shard_map/ppermute | solution.py:307
  37.9 0.9 %collective-permute-done.13.ends = bf16[16,512]{1,0:T(8,128)(2,1)S(1)} collective-permute-done((bf16[16,512]{1,0:T(8,128)(2,1)S(1)}, bf16[16,512]{1,0:T(8,128)(2,1)S(1)}, u32[]{:S(2)}, u32[]{:S(2)}) %collective-permute-start.13) | collective-permute-done | bytes 16416 | tf_op jit(solution)/shard_map/ppermute | solution.py:307
  38.8 0.1 shard_map.54
  38.8 0.1 collective-permute-start.14
  38.9 1.3 %collective-permute-done.14.other = bf16[128,512]{1,0:T(8,128)(2,1)S(1)} collective-permute-done((bf16[128,512]{1,0:T(8,128)(2,1)S(1)}, bf16[128,512]{1,0:T(8,128)(2,1)S(1)}, u32[]{:S(2)}, u32[]{:S(2)}) %collective-permute-start.14) | collective-permute-done | bytes 131104 | tf_op jit(solution)/shard_map/ppermute | solution.py:307
  40.2 0.8 %shard_map.55 = bf16[1,128,1024]{2,1,0:T(8,128)(2,1)} custom-call(f32[128,512]{1,0:T(8,128)S(1)} %get-tuple-element.50.mine, bf16[128,512]{1,0:T(8,128)(2,1)S(1)} %collective-permute-done.14.other), custom_call_target="tpu_custom_call" | custom-call | flops 1000 | bytes 1000 | tf_op jit(solution)/shard_map/pallas_call | solution.py:361
  (4 shorter events, 0.1 us)
Async XLA Ops:
  0.0 16.2 %collective-permute-start.3 = (bf16[1,128,1024]{2,1,0:T(8,128)(2,1)}, bf16[1,128,1024]{2,1,0:T(8,128)(2,1)S(1)}, u32[]{:S(2)}, u32[]{:S(2)}) collective-permute-start(bf16[1,128,1024]{2,1,0:T(8,128)(2,1)} %param.7), channel_id=1, source_target_pairs={{16,0},{17,1},{18,2},{19,3},{20,4},{21,5},{22,6},{23,7},{24,8},{25... | collective-permute-start | bytes 786440 | tf_op jit(solution)/shard_map/ppermute | solution.py:304
  6.1 4.9 %collective-permute-start = (bf16[256,2048]{1,0:T(8,128)(2,1)S(1)}, bf16[256,2048]{1,0:T(8,128)(2,1)}, u32[]{:S(2)}, u32[]{:S(2)}) collective-permute-start(bf16[256,2048]{1,0:T(8,128)(2,1)S(1)} %get-tuple-element.11), channel_id=1, source_target_pairs={{0,1},{1,0},{2,3},{3,2},{4,5},{5,4},{6,7},{7,6},{8,9},{9,8},{10,11... | collective-permute-start | bytes 3145736 | tf_op jit(solution)/shard_map/cond/branch_1_fun/ppermute | solution.py:307
  6.2 3.9 %collective-permute-start.1 = (bf16[64,128]{1,0:T(8,128)(2,1)S(1)}, bf16[64,128]{1,0:T(8,128)(2,1)}, u32[]{:S(2)}, u32[]{:S(2)}) collective-permute-start(bf16[64,128]{1,0:T(8,128)(2,1)S(1)} %get-tuple-element.12), channel_id=1, source_target_pairs={{0,4},{1,5},{2,6},{3,7},{4,0},{5,1},{6,2},{7,3},{8,12},{9,13},{10,... | collective-permute-start | bytes 49160 | tf_op jit(solution)/shard_map/cond/branch_1_fun/ppermute | solution.py:307
  7.8 3.3 %collective-permute-start.2 = (bf16[64,128]{1,0:T(8,128)(2,1)S(1)}, bf16[64,128]{1,0:T(8,128)(2,1)}, u32[]{:S(2)}, u32[]{:S(2)}) collective-permute-start(bf16[64,128]{1,0:T(8,128)(2,1)S(1)} %get-tuple-element.13), channel_id=1, source_target_pairs={{0,5},{1,4},{2,7},{3,6},{4,1},{5,0},{6,3},{7,2},{8,13},{9,12},{10,... | collective-permute-start | bytes 49160 | tf_op jit(solution)/shard_map/cond/branch_1_fun/ppermute | solution.py:307
  11.0 13.7 %copy-start = (s32[2]{0:T(128)S(1)}, s32[2]{0:T(128)}, u32[]{:S(2)}) copy-start(s32[2]{0:T(128)} %len_ref.3) | copy-start | bytes 28
  16.2 2.2 %collective-permute-start.4 = (bf16[128,512]{1,0:T(8,128)(2,1)S(1)}, bf16[128,512]{1,0:T(8,128)(2,1)S(1)}, u32[]{:S(2)}, u32[]{:S(2)}) collective-permute-start(bf16[128,512]{1,0:T(8,128)(2,1)S(1)} %get-tuple-element.42), channel_id=1, source_target_pairs={{0,1},{1,0},{2,3},{3,2},{4,5},{5,4},{6,7},{7,6},{8,9},{9,8},{10,11... | collective-permute-start | bytes 393224 | tf_op jit(solution)/shard_map/ppermute | solution.py:307
  16.3 5.7 %collective-permute-start.6 = (bf16[128,256]{1,0:T(8,128)(2,1)S(1)}, bf16[128,256]{1,0:T(8,128)(2,1)S(1)}, u32[]{:S(2)}, u32[]{:S(2)}) collective-permute-start(bf16[128,256]{1,0:T(8,128)(2,1)S(1)} %get-tuple-element.43), channel_id=1, source_target_pairs={{0,3},{1,2},{2,1},{3,0},{4,7},{5,6},{6,5},{7,4},{8,11},{9,10},{10,... | collective-permute-start | bytes 196616 | tf_op jit(solution)/shard_map/ppermute | solution.py:307
  18.0 4.4 %collective-permute-start.5 = (bf16[128,256]{1,0:T(8,128)(2,1)S(1)}, bf16[128,256]{1,0:T(8,128)(2,1)S(1)}, u32[]{:S(2)}, u32[]{:S(2)}) collective-permute-start(bf16[128,256]{1,0:T(8,128)(2,1)S(1)} %get-tuple-element.41.refs_0_), channel_id=1, source_target_pairs={{0,2},{1,3},{2,0},{3,1},{4,6},{5,7},{6,4},{7,5},{8,10},{9,11},{10,... | collective-permute-start | bytes 196616 | tf_op jit(solution)/shard_map/ppermute | solution.py:307
  18.5 4.0 %collective-permute-start.8 = (bf16[16,512]{1,0:T(8,128)(2,1)S(1)}, bf16[16,512]{1,0:T(8,128)(2,1)S(1)}, u32[]{:S(2)}, u32[]{:S(2)}) collective-permute-start(bf16[16,512]{1,0:T(8,128)(2,1)S(1)} %shard_map.48), channel_id=1, source_target_pairs={{0,4},{1,5},{2,6},{3,7},{4,0},{5,1},{6,2},{7,3},{8,12},{9,13},{10,... | collective-permute-start | bytes 49160 | tf_op jit(solution)/shard_map/ppermute | solution.py:307
  20.1 4.6 %collective-permute-start.7 = (bf16[16,512]{1,0:T(8,128)(2,1)S(1)}, bf16[16,512]{1,0:T(8,128)(2,1)S(1)}, u32[]{:S(2)}, u32[]{:S(2)}) collective-permute-start(bf16[16,512]{1,0:T(8,128)(2,1)S(1)} %shard_map.48), channel_id=1, source_target_pairs={{0,2},{1,3},{2,4},{3,5},{4,6},{5,7},{6,0},{7,1},{8,10},{9,11},{10,... | collective-permute-start | bytes 49160 | tf_op jit(solution)/shard_map/ppermute | solution.py:307
  21.6 7.6 %collective-permute-start.9 = (bf16[128,256]{1,0:T(8,128)(2,1)S(1)}, bf16[128,256]{1,0:T(8,128)(2,1)S(1)}, u32[]{:S(2)}, u32[]{:S(2)}) collective-permute-start(bf16[128,256]{1,0:T(8,128)(2,1)S(1)} %get-tuple-element.44.refs_1_.refs_4_.refs_2_), channel_id=1, source_target_pairs={{0,2},{1,3},{2,0},{3,1},{4,6},{5,7},{6,4},{7,5},{8,10},{9,11},{10,... | collective-permute-start | bytes 196616 | tf_op jit(solution)/shard_map/ppermute | solution.py:307
  22.0 7.2 %collective-permute-start.10 = (bf16[128,256]{1,0:T(8,128)(2,1)S(1)}, bf16[128,256]{1,0:T(8,128)(2,1)S(1)}, u32[]{:S(2)}, u32[]{:S(2)}) collective-permute-start(bf16[128,256]{1,0:T(8,128)(2,1)S(1)} %get-tuple-element.47), channel_id=1, source_target_pairs={{0,3},{1,2},{2,1},{3,0},{4,7},{5,6},{6,5},{7,4},{8,11},{9,10},{10,... | collective-permute-start | bytes 196616 | tf_op jit(solution)/shard_map/ppermute | solution.py:307
  28.9 6.0 %collective-permute-start.11 = (bf16[144,512]{1,0:T(8,128)(2,1)S(1)}, bf16[144,512]{1,0:T(8,128)(2,1)S(1)}, u32[]{:S(2)}, u32[]{:S(2)}) collective-permute-start(bf16[144,512]{1,0:T(8,128)(2,1)S(1)} %shard_map.51), channel_id=1, source_target_pairs={{0,2},{1,3},{2,0},{3,1},{4,6},{5,7},{6,4},{7,5},{8,10},{9,11},{10,... | collective-permute-start | bytes 442376 | tf_op jit(solution)/shard_map/ppermute | solution.py:307
  30.6 7.3 %collective-permute-start.12 = (bf16[128,512]{1,0:T(8,128)(2,1)S(1)}, bf16[128,512]{1,0:T(8,128)(2,1)S(1)}, u32[]{:S(2)}, u32[]{:S(2)}) collective-permute-start(bf16[128,512]{1,0:T(8,128)(2,1)S(1)} %shard_map.52), channel_id=1, source_target_pairs={{0,2},{1,3},{2,0},{3,1},{4,6},{5,7},{6,4},{7,5},{8,10},{9,11},{10,... | collective-permute-start | bytes 393224 | tf_op jit(solution)/shard_map/ppermute | solution.py:307
  35.0 3.8 %collective-permute-start.13 = (bf16[16,512]{1,0:T(8,128)(2,1)S(1)}, bf16[16,512]{1,0:T(8,128)(2,1)S(1)}, u32[]{:S(2)}, u32[]{:S(2)}) collective-permute-start(bf16[16,512]{1,0:T(8,128)(2,1)S(1)} %shard_map.53), channel_id=1, source_target_pairs={{0,4},{1,5},{2,6},{3,7},{4,0},{5,1},{6,2},{7,3},{8,12},{9,13},{10,... | collective-permute-start | bytes 49160 | tf_op jit(solution)/shard_map/ppermute | solution.py:307
  38.8 1.4 %collective-permute-start.14 = (bf16[128,512]{1,0:T(8,128)(2,1)S(1)}, bf16[128,512]{1,0:T(8,128)(2,1)S(1)}, u32[]{:S(2)}, u32[]{:S(2)}) collective-permute-start(bf16[128,512]{1,0:T(8,128)(2,1)S(1)} %get-tuple-element.51), channel_id=1, source_target_pairs={{0,1},{1,0},{2,3},{3,2},{4,5},{5,4},{6,7},{7,6},{8,9},{9,8},{10,11... | collective-permute-start | bytes 393224 | tf_op jit(solution)/shard_map/ppermute | solution.py:307

commit v4 on v3

--- a/solution.py
+++ b/solution.py
@@ -147,16 +147,14 @@
     return jnp.where((key_pos >= start) & (key_pos <= query_pos), 0.0, MASKED)
 
 
-def weigh(key, value, query, cot, bias, keep):
-    scores = lax.dot_general(key, query, NT, preferred_element_type=F32) + bias
+def raise_scores(key, query, bias):
+    return lax.dot_general(key, query, NT, preferred_element_type=F32) + bias
+
+
+def softmax(scores, keep):
     top = jnp.max(scores, axis=0, keepdims=True)
     raw = jnp.exp2((scores - top) * (HD**-0.5 * math.log2(math.e)))
-    dweights = lax.dot_general(value, cot, NT, preferred_element_type=F32)
-    share = keep / jnp.sum(raw, axis=0, keepdims=True)
-    delta = jnp.sum(raw * dweights, axis=0, keepdims=True) * share
-    weights = raw * share
-    dscores = weights * (dweights - delta)
-    return weights.astype(BF16), dscores.astype(BF16)
+    return raw * (keep / jnp.sum(raw, axis=0, keepdims=True))
 
 
 def grad_kernel(stage, halo, len_ref, q_buf, g_buf, *refs):
@@ -210,15 +208,23 @@
                 start = doc_start(query_pos, len_ref)
                 keep = jnp.where((start < first + span - halo) & (lane < SHARE * docs), 1.0, 0.0)
                 tiles.append((stage, pl.ds(2 * WIDE, size), halo, halo + span + halo, query_pos, start, keep, 1))
-            for part, cols, low, high, query_pos, start, keep, times in tiles:
+            def raised(tile):
+                part, cols, low, high, query_pos, start, keep, times = tile
+                bias = bias_of(first - halo + low, high - low, query_pos, start)
+                bias = jnp.concatenate([bias] * times, axis=1)
+                return raise_scores(k_buf[part, pl.ds(low, high - low), :], q_buf[part, cols, :], bias)
+
+            scores = raised(tiles[0])
+            for at, (part, cols, low, high, query_pos, start, keep, times) in enumerate(tiles):
                 keys = pl.ds(low, high - low)
-                bias = bias_of(first - halo + low, high - low, query_pos, start)
                 query, cot = q_buf[part, cols, :], g_buf[part, cols, :]
-                weights, dscores = weigh(
-                    k_buf[part, keys, :], v_buf[part, keys, :], query, cot,
-                    jnp.concatenate([bias] * times, axis=1), jnp.concatenate([keep] * times, axis=1),
-                )
-                dv_ref[part, keys, :] += lax.dot_general(weights, cot, NN, preferred_element_type=F32)
+                weights = softmax(scores, jnp.concatenate([keep] * times, axis=1))
+                dweights = lax.dot_general(v_buf[part, keys, :], cot, NT, preferred_element_type=F32)
+                dv_ref[part, keys, :] += lax.dot_general(weights.astype(BF16), cot, NN, preferred_element_type=F32)
+                if at + 1 < len(tiles):
+                    scores = raised(tiles[at + 1])
+                delta = jnp.sum(weights * dweights, axis=0, keepdims=True)
+                dscores = (weights * (dweights - delta)).astype(BF16)
                 dk_ref[part, keys, :] += lax.dot_general(dscores, query, NN, preferred_element_type=F32)
 
 

time: 41.3 us -> 40.8 us (0.988)
  no operation moved by 1% of the time
where the time goes in v4:
time: 40.8 us; the launch traced here: 40.6 us
  starting transfers between devices  17.1 us (42%)
  waiting for transfers between devices  12.8 us (31%)
  Pallas kernels  9.87 us (24%)
  between operations  0.73 us (2%)
    ppermute x14, starting transfers between devices, along(): return lax.ppermute(block, 'ctx', pairs(pick))  13.1 us
    ppermute x14, waiting for transfers between devices, along(): return lax.ppermute(block, 'ctx', pairs(pick))  9.88 us
    pallas_call x2, Pallas kernels, grads(): call(functools.partial(grad_kernel, stage, halo), [jax.ShapeDtypeStruct(t...  5.3 us
    ppermute x1, starting transfers between devices, partner(): return lax.ppermute(block, ('pipe', 'ctx'), route)  4.04 us
    ppermute x1, waiting for transfers between devices, partner(): return lax.ppermute(block, ('pipe', 'ctx'), route)  2.93 us
    pallas_call x1, Pallas kernels, on_device(): call(stage_kernel, [shape(PARTS, 2 * WIDE + size, HD)] * 2, in_specs=[hbm...  2.2 us
    pallas_call x1, Pallas kernels, beside(): call(functools.partial(hand_kernel, halo, lengths.shape[0]), [shape(2 * r...  1.38 us
  transfers between devices with their start and end apart: 15, of which 8 were waited for; matrix products, arithmetic and copies ran while one was open for 0% of the time, Pallas kernels for 22%

profile of v4, /device:TPU:0, one launch (start us, length us, event | category | flops | bytes accessed | tf_op | source)
XLA Modules:
  0.0 40.6 jit_solution(8533219572381376799)
XLA Ops:
  0.0 4.0 %collective-permute-start.3 = (bf16[1,128,1024]{2,1,0:T(8,128)(2,1)}, bf16[1,128,1024]{2,1,0:T(8,128)(2,1)S(1)}, u32[]{:S(2)}, u32[]{:S(2)}) collective-permute-start(bf16[1,128,1024]{2,1,0:T(8,128)(2,1)} %param.7), channel_id=1, source_target_pairs={{16,0},{17,1},{18,2},{19,3},{20,4},{21,5},{22,6},{23,7},{24,8},{25... | collective-permute-start | bytes 786440 | tf_op jit(solution)/shard_map/ppermute | solution.py:310
  4.7 6.3 %conditional.1 = (bf16[256,2048]{1,0:T(8,128)(2,1)}, bf16[64,128]{1,0:T(8,128)(2,1)}, bf16[64,128]{1,0:T(8,128)(2,1)}) conditional(s32[]{:T(128)} %bitcast, () %tuple.14, (bf16[1,128,4096]{2,1,0:T(8,128)(2,1)}, bf16[1,128,4096]{2,1,0:T(8,128)(2,1)}) %tuple.15), branch_computations={%region_0.0_spmd, %region_1.0_spmd} | conditional | flops 1000 | bytes 4326520 | solution.py:343
  4.7 1.4 %branch_1_fun.1 = (bf16[256,2048]{1,0:T(8,128)(2,1)S(1)}, bf16[64,128]{1,0:T(8,128)(2,1)S(1)}, bf16[64,128]{1,0:T(8,128)(2,1)S(1)}) custom-call(bf16[1,128,4096]{2,1,0:T(8,128)(2,1)} %get-tuple-element.9.q_ref, bf16[1,128,4096]{2,1,0:T(8,128)(2,1)} %get-tuple-element.10.g_ref), custom_call_target="tpu_custom_call" | custom-call | flops 1000 | bytes 1000 | tf_op jit(solution)/shard_map/cond/branch_1_fun/pallas_call | solution.py:332
  6.1 0.1 collective-permute-start
  6.2 1.6 %collective-permute-start.1 = (bf16[64,128]{1,0:T(8,128)(2,1)S(1)}, bf16[64,128]{1,0:T(8,128)(2,1)}, u32[]{:S(2)}, u32[]{:S(2)}) collective-permute-start(bf16[64,128]{1,0:T(8,128)(2,1)S(1)} %get-tuple-element.12), channel_id=1, source_target_pairs={{0,4},{1,5},{2,6},{3,7},{4,0},{5,1},{6,2},{7,3},{8,12},{9,13},{10,... | collective-permute-start | bytes 49160 | tf_op jit(solution)/shard_map/cond/branch_1_fun/ppermute | solution.py:313
  7.8 0.3 collective-permute-start.2
  8.0 2.0 %collective-permute-done.1 = bf16[64,128]{1,0:T(8,128)(2,1)} collective-permute-done((bf16[64,128]{1,0:T(8,128)(2,1)S(1)}, bf16[64,128]{1,0:T(8,128)(2,1)}, u32[]{:S(2)}, u32[]{:S(2)}) %collective-permute-start.1) | collective-permute-done | bytes 16416 | tf_op jit(solution)/shard_map/cond/branch_1_fun/ppermute | solution.py:313
  10.1 0.9 %collective-permute-done.2 = bf16[64,128]{1,0:T(8,128)(2,1)} collective-permute-done((bf16[64,128]{1,0:T(8,128)(2,1)S(1)}, bf16[64,128]{1,0:T(8,128)(2,1)}, u32[]{:S(2)}, u32[]{:S(2)}) %collective-permute-start.2) | collective-permute-done | bytes 16416 | tf_op jit(solution)/shard_map/cond/branch_1_fun/ppermute | solution.py:313
  11.0 0.0 collective-permute-done
  11.0 0.0 copy-start
  11.0 2.2 %shard_map.46 = (bf16[2,2064,128]{2,1,0:T(8,128)(2,1)S(1)}, bf16[2,2064,128]{2,1,0:T(8,128)(2,1)S(1)}) custom-call(bf16[1,128,4096]{2,1,0:T(8,128)(2,1)} %q_ref.1, bf16[1,128,4096]{2,1,0:T(8,128)(2,1)} %g_ref.1, bf16[256,2048]{1,0:T(8,128)(2,1)} %get-tuple-element.33.far, bf16[64,128]{1,0:T(8,128)(2,1)} %get-tuple-element.34.edge0, ...), custom_call_target="tpu_custom_call" | custom-call | flops 1000 | bytes 1000 | tf_op jit(solution)/shard_map/pallas_call | solution.py:344
  13.2 2.9 %collective-permute-done.3.kv_ref = bf16[1,128,1024]{2,1,0:T(8,128)(2,1)S(1)} collective-permute-done((bf16[1,128,1024]{2,1,0:T(8,128)(2,1)}, bf16[1,128,1024]{2,1,0:T(8,128)(2,1)S(1)}, u32[]{:S(2)}, u32[]{:S(2)}) %collective-permute-start.3) | collective-permute-done | bytes 262176 | tf_op jit(solution)/shard_map/ppermute | solution.py:310
  16.2 0.1 shard_map.47
  16.2 0.1 collective-permute-start.4
  16.3 1.7 %collective-permute-start.6 = (bf16[128,256]{1,0:T(8,128)(2,1)S(1)}, bf16[128,256]{1,0:T(8,128)(2,1)S(1)}, u32[]{:S(2)}, u32[]{:S(2)}) collective-permute-start(bf16[128,256]{1,0:T(8,128)(2,1)S(1)} %get-tuple-element.43), channel_id=1, source_target_pairs={{0,3},{1,2},{2,1},{3,0},{4,7},{5,6},{6,5},{7,4},{8,11},{9,10},{10,... | collective-permute-start | bytes 196616 | tf_op jit(solution)/shard_map/ppermute | solution.py:313
  18.0 0.5 %collective-permute-start.5 = (bf16[128,256]{1,0:T(8,128)(2,1)S(1)}, bf16[128,256]{1,0:T(8,128)(2,1)S(1)}, u32[]{:S(2)}, u32[]{:S(2)}) collective-permute-start(bf16[128,256]{1,0:T(8,128)(2,1)S(1)} %get-tuple-element.41.refs_0_), channel_id=1, source_target_pairs={{0,2},{1,3},{2,0},{3,1},{4,6},{5,7},{6,4},{7,5},{8,10},{9,11},{10,... | collective-permute-start | bytes 196616 | tf_op jit(solution)/shard_map/ppermute | solution.py:313
  18.5 0.0 collective-permute-done.4.refs_2_.refs_1_.refs_3_
  18.5 1.6 %collective-permute-start.8 = (bf16[16,512]{1,0:T(8,128)(2,1)S(1)}, bf16[16,512]{1,0:T(8,128)(2,1)S(1)}, u32[]{:S(2)}, u32[]{:S(2)}) collective-permute-start(bf16[16,512]{1,0:T(8,128)(2,1)S(1)} %shard_map.48), channel_id=1, source_target_pairs={{0,4},{1,5},{2,6},{3,7},{4,0},{5,1},{6,2},{7,3},{8,12},{9,13},{10,... | collective-permute-start | bytes 49160 | tf_op jit(solution)/shard_map/ppermute | solution.py:313
  20.1 1.5 %collective-permute-start.7 = (bf16[16,512]{1,0:T(8,128)(2,1)S(1)}, bf16[16,512]{1,0:T(8,128)(2,1)S(1)}, u32[]{:S(2)}, u32[]{:S(2)}) collective-permute-start(bf16[16,512]{1,0:T(8,128)(2,1)S(1)} %shard_map.48), channel_id=1, source_target_pairs={{0,2},{1,3},{2,4},{3,5},{4,6},{5,7},{6,0},{7,1},{8,10},{9,11},{10,... | collective-permute-start | bytes 49160 | tf_op jit(solution)/shard_map/ppermute | solution.py:313
  21.6 0.4 %collective-permute-start.9 = (bf16[128,256]{1,0:T(8,128)(2,1)S(1)}, bf16[128,256]{1,0:T(8,128)(2,1)S(1)}, u32[]{:S(2)}, u32[]{:S(2)}) collective-permute-start(bf16[128,256]{1,0:T(8,128)(2,1)S(1)} %get-tuple-element.44.refs_1_.refs_4_.refs_2_), channel_id=1, source_target_pairs={{0,2},{1,3},{2,0},{3,1},{4,6},{5,7},{6,4},{7,5},{8,10},{9,11},{10,... | collective-permute-start | bytes 196616 | tf_op jit(solution)/shard_map/ppermute | solution.py:313
  22.0 0.0 collective-permute-done.6.refs_3_
  22.0 0.3 collective-permute-start.10
  22.3 0.1 collective-permute-done.5.refs_2_
  22.4 0.0 collective-permute-done.8.refs_6_.refs_7_
  22.4 2.3 %collective-permute-done.7.refs_5_.refs_6_ = bf16[16,512]{1,0:T(8,128)(2,1)S(1)} collective-permute-done((bf16[16,512]{1,0:T(8,128)(2,1)S(1)}, bf16[16,512]{1,0:T(8,128)(2,1)S(1)}, u32[]{:S(2)}, u32[]{:S(2)}) %collective-permute-start.7) | collective-permute-done | bytes 16416 | tf_op jit(solution)/shard_map/ppermute | solution.py:313
  24.7 0.0 copy-done
  24.7 3.9 %shard_map.49 = (f32[2,544,128]{2,1,0:T(8,128)S(1)}, f32[2,544,128]{2,1,0:T(8,128)S(1)}) custom-call(s32[2]{0:T(128)S(1)} %copy-done, bf16[2,2064,128]{2,1,0:T(8,128)(2,1)S(1)} %get-tuple-element.38.q_buf, bf16[2,2064,128]{2,1,0:T(8,128)(2,1)S(1)} %get-tuple-element.39.g_buf, bf16[128,256]{1,0:T(8,128)(2,1)S(1)} %get-tuple-element.41.refs_0_, ...), custom_call_target="tpu_custom_call" | custom-call | flops 4000000000 | bytes 1000 | tf_op jit(solution)/shard_map/pallas_call | solution.py:276
  28.7 0.4 collective-permute-start.11
  29.0 0.0 collective-permute-done.10.refs_5_
  29.0 0.0 collective-permute-done.9.refs_4_
  29.1 1.4 %shard_map.50 = (f32[2,544,128]{2,1,0:T(8,128)S(1)}, f32[2,544,128]{2,1,0:T(8,128)S(1)}) custom-call(s32[2]{0:T(128)S(1)} %copy-done, bf16[2,2064,128]{2,1,0:T(8,128)(2,1)S(1)} %get-tuple-element.38.q_buf, bf16[2,2064,128]{2,1,0:T(8,128)(2,1)S(1)} %get-tuple-element.39.g_buf, f32[2,544,128]{2,1,0:T(8,128)S(1)} %get-tuple-element.45.refs_0_.dk_ref, ...), custom_call_target="tpu_custom_call" | custom-call | flops 4000000000 | bytes 1000 | tf_op jit(solution)/shard_map/pallas_call | solution.py:276
  30.5 4.0 %collective-permute-start.12 = (bf16[128,512]{1,0:T(8,128)(2,1)S(1)}, bf16[128,512]{1,0:T(8,128)(2,1)S(1)}, u32[]{:S(2)}, u32[]{:S(2)}) collective-permute-start(bf16[128,512]{1,0:T(8,128)(2,1)S(1)} %shard_map.52), channel_id=1, source_target_pairs={{0,2},{1,3},{2,0},{3,1},{4,6},{5,7},{6,4},{7,5},{8,10},{9,11},{10,... | collective-permute-start | bytes 393224 | tf_op jit(solution)/shard_map/ppermute | solution.py:313
  34.5 0.0 collective-permute-done.11.across.across0
  34.5 0.7 %collective-permute-start.13 = (bf16[16,512]{1,0:T(8,128)(2,1)S(1)}, bf16[16,512]{1,0:T(8,128)(2,1)S(1)}, u32[]{:S(2)}, u32[]{:S(2)}) collective-permute-start(bf16[16,512]{1,0:T(8,128)(2,1)S(1)} %shard_map.53), channel_id=1, source_target_pairs={{0,4},{1,5},{2,6},{3,7},{4,0},{5,1},{6,2},{7,3},{8,12},{9,13},{10,... | collective-permute-start | bytes 49160 | tf_op jit(solution)/shard_map/ppermute | solution.py:313
  35.2 2.2 %collective-permute-done.12.across1 = bf16[128,512]{1,0:T(8,128)(2,1)S(1)} collective-permute-done((bf16[128,512]{1,0:T(8,128)(2,1)S(1)}, bf16[128,512]{1,0:T(8,128)(2,1)S(1)}, u32[]{:S(2)}, u32[]{:S(2)}) %collective-permute-start.12) | collective-permute-done | bytes 131104 | tf_op jit(solution)/shard_map/ppermute | solution.py:313
  37.4 0.9 %collective-permute-done.13.ends = bf16[16,512]{1,0:T(8,128)(2,1)S(1)} collective-permute-done((bf16[16,512]{1,0:T(8,128)(2,1)S(1)}, bf16[16,512]{1,0:T(8,128)(2,1)S(1)}, u32[]{:S(2)}, u32[]{:S(2)}) %collective-permute-start.13) | collective-permute-done | bytes 16416 | tf_op jit(solution)/shard_map/ppermute | solution.py:313
  38.3 0.1 shard_map.54
  38.4 0.1 collective-permute-start.14
  38.5 1.3 %collective-permute-done.14.other = bf16[128,512]{1,0:T(8,128)(2,1)S(1)} collective-permute-done((bf16[128,512]{1,0:T(8,128)(2,1)S(1)}, bf16[128,512]{1,0:T(8,128)(2,1)S(1)}, u32[]{:S(2)}, u32[]{:S(2)}) %collective-permute-start.14) | collective-permute-done | bytes 131104 | tf_op jit(solution)/shard_map/ppermute | solution.py:313
  39.8 0.8 %shard_map.55 = bf16[1,128,1024]{2,1,0:T(8,128)(2,1)} custom-call(f32[128,512]{1,0:T(8,128)S(1)} %get-tuple-element.50.mine, bf16[128,512]{1,0:T(8,128)(2,1)S(1)} %collective-permute-done.14.other), custom_call_target="tpu_custom_call" | custom-call | flops 1000 | bytes 1000 | tf_op jit(solution)/shard_map/pallas_call | solution.py:367
  (4 shorter events, 0.1 us)
Async XLA Ops:
  0.0 16.2 %collective-permute-start.3 = (bf16[1,128,1024]{2,1,0:T(8,128)(2,1)}, bf16[1,128,1024]{2,1,0:T(8,128)(2,1)S(1)}, u32[]{:S(2)}, u32[]{:S(2)}) collective-permute-start(bf16[1,128,1024]{2,1,0:T(8,128)(2,1)} %param.7), channel_id=1, source_target_pairs={{16,0},{17,1},{18,2},{19,3},{20,4},{21,5},{22,6},{23,7},{24,8},{25... | collective-permute-start | bytes 786440 | tf_op jit(solution)/shard_map/ppermute | solution.py:310
  6.1 4.9 %collective-permute-start = (bf16[256,2048]{1,0:T(8,128)(2,1)S(1)}, bf16[256,2048]{1,0:T(8,128)(2,1)}, u32[]{:S(2)}, u32[]{:S(2)}) collective-permute-start(bf16[256,2048]{1,0:T(8,128)(2,1)S(1)} %get-tuple-element.11), channel_id=1, source_target_pairs={{0,1},{1,0},{2,3},{3,2},{4,5},{5,4},{6,7},{7,6},{8,9},{9,8},{10,11... | collective-permute-start | bytes 3145736 | tf_op jit(solution)/shard_map/cond/branch_1_fun/ppermute | solution.py:313
  6.2 3.9 %collective-permute-start.1 = (bf16[64,128]{1,0:T(8,128)(2,1)S(1)}, bf16[64,128]{1,0:T(8,128)(2,1)}, u32[]{:S(2)}, u32[]{:S(2)}) collective-permute-start(bf16[64,128]{1,0:T(8,128)(2,1)S(1)} %get-tuple-element.12), channel_id=1, source_target_pairs={{0,4},{1,5},{2,6},{3,7},{4,0},{5,1},{6,2},{7,3},{8,12},{9,13},{10,... | collective-permute-start | bytes 49160 | tf_op jit(solution)/shard_map/cond/branch_1_fun/ppermute | solution.py:313
  7.8 3.3 %collective-permute-start.2 = (bf16[64,128]{1,0:T(8,128)(2,1)S(1)}, bf16[64,128]{1,0:T(8,128)(2,1)}, u32[]{:S(2)}, u32[]{:S(2)}) collective-permute-start(bf16[64,128]{1,0:T(8,128)(2,1)S(1)} %get-tuple-element.13), channel_id=1, source_target_pairs={{0,5},{1,4},{2,7},{3,6},{4,1},{5,0},{6,3},{7,2},{8,13},{9,12},{10,... | collective-permute-start | bytes 49160 | tf_op jit(solution)/shard_map/cond/branch_1_fun/ppermute | solution.py:313
  11.0 13.7 %copy-start = (s32[2]{0:T(128)S(1)}, s32[2]{0:T(128)}, u32[]{:S(2)}) copy-start(s32[2]{0:T(128)} %len_ref.3) | copy-start | bytes 28
  16.2 2.2 %collective-permute-start.4 = (bf16[128,512]{1,0:T(8,128)(2,1)S(1)}, bf16[128,512]{1,0:T(8,128)(2,1)S(1)}, u32[]{:S(2)}, u32[]{:S(2)}) collective-permute-start(bf16[128,512]{1,0:T(8,128)(2,1)S(1)} %get-tuple-element.42), channel_id=1, source_target_pairs={{0,1},{1,0},{2,3},{3,2},{4,5},{5,4},{6,7},{7,6},{8,9},{9,8},{10,11... | collective-permute-start | bytes 393224 | tf_op jit(solution)/shard_map/ppermute | solution.py:313
  16.3 5.7 %collective-permute-start.6 = (bf16[128,256]{1,0:T(8,128)(2,1)S(1)}, bf16[128,256]{1,0:T(8,128)(2,1)S(1)}, u32[]{:S(2)}, u32[]{:S(2)}) collective-permute-start(bf16[128,256]{1,0:T(8,128)(2,1)S(1)} %get-tuple-element.43), channel_id=1, source_target_pairs={{0,3},{1,2},{2,1},{3,0},{4,7},{5,6},{6,5},{7,4},{8,11},{9,10},{10,... | collective-permute-start | bytes 196616 | tf_op jit(solution)/shard_map/ppermute | solution.py:313
  18.0 4.4 %collective-permute-start.5 = (bf16[128,256]{1,0:T(8,128)(2,1)S(1)}, bf16[128,256]{1,0:T(8,128)(2,1)S(1)}, u32[]{:S(2)}, u32[]{:S(2)}) collective-permute-start(bf16[128,256]{1,0:T(8,128)(2,1)S(1)} %get-tuple-element.41.refs_0_), channel_id=1, source_target_pairs={{0,2},{1,3},{2,0},{3,1},{4,6},{5,7},{6,4},{7,5},{8,10},{9,11},{10,... | collective-permute-start | bytes 196616 | tf_op jit(solution)/shard_map/ppermute | solution.py:313
  18.5 4.0 %collective-permute-start.8 = (bf16[16,512]{1,0:T(8,128)(2,1)S(1)}, bf16[16,512]{1,0:T(8,128)(2,1)S(1)}, u32[]{:S(2)}, u32[]{:S(2)}) collective-permute-start(bf16[16,512]{1,0:T(8,128)(2,1)S(1)} %shard_map.48), channel_id=1, source_target_pairs={{0,4},{1,5},{2,6},{3,7},{4,0},{5,1},{6,2},{7,3},{8,12},{9,13},{10,... | collective-permute-start | bytes 49160 | tf_op jit(solution)/shard_map/ppermute | solution.py:313
  20.1 4.6 %collective-permute-start.7 = (bf16[16,512]{1,0:T(8,128)(2,1)S(1)}, bf16[16,512]{1,0:T(8,128)(2,1)S(1)}, u32[]{:S(2)}, u32[]{:S(2)}) collective-permute-start(bf16[16,512]{1,0:T(8,128)(2,1)S(1)} %shard_map.48), channel_id=1, source_target_pairs={{0,2},{1,3},{2,4},{3,5},{4,6},{5,7},{6,0},{7,1},{8,10},{9,11},{10,... | collective-permute-start | bytes 49160 | tf_op jit(solution)/shard_map/ppermute | solution.py:313
  21.6 7.5 %collective-permute-start.9 = (bf16[128,256]{1,0:T(8,128)(2,1)S(1)}, bf16[128,256]{1,0:T(8,128)(2,1)S(1)}, u32[]{:S(2)}, u32[]{:S(2)}) collective-permute-start(bf16[128,256]{1,0:T(8,128)(2,1)S(1)} %get-tuple-element.44.refs_1_.refs_4_.refs_2_), channel_id=1, source_target_pairs={{0,2},{1,3},{2,0},{3,1},{4,6},{5,7},{6,4},{7,5},{8,10},{9,11},{10,... | collective-permute-start | bytes 196616 | tf_op jit(solution)/shard_map/ppermute | solution.py:313
  22.0 7.0 %collective-permute-start.10 = (bf16[128,256]{1,0:T(8,128)(2,1)S(1)}, bf16[128,256]{1,0:T(8,128)(2,1)S(1)}, u32[]{:S(2)}, u32[]{:S(2)}) collective-permute-start(bf16[128,256]{1,0:T(8,128)(2,1)S(1)} %get-tuple-element.47), channel_id=1, source_target_pairs={{0,3},{1,2},{2,1},{3,0},{4,7},{5,6},{6,5},{7,4},{8,11},{9,10},{10,... | collective-permute-start | bytes 196616 | tf_op jit(solution)/shard_map/ppermute | solution.py:313
  28.7 5.8 %collective-permute-start.11 = (bf16[144,512]{1,0:T(8,128)(2,1)S(1)}, bf16[144,512]{1,0:T(8,128)(2,1)S(1)}, u32[]{:S(2)}, u32[]{:S(2)}) collective-permute-start(bf16[144,512]{1,0:T(8,128)(2,1)S(1)} %shard_map.51), channel_id=1, source_target_pairs={{0,2},{1,3},{2,0},{3,1},{4,6},{5,7},{6,4},{7,5},{8,10},{9,11},{10,... | collective-permute-start | bytes 442376 | tf_op jit(solution)/shard_map/ppermute | solution.py:313
  30.5 6.9 %collective-permute-start.12 = (bf16[128,512]{1,0:T(8,128)(2,1)S(1)}, bf16[128,512]{1,0:T(8,128)(2,1)S(1)}, u32[]{:S(2)}, u32[]{:S(2)}) collective-permute-start(bf16[128,512]{1,0:T(8,128)(2,1)S(1)} %shard_map.52), channel_id=1, source_target_pairs={{0,2},{1,3},{2,0},{3,1},{4,6},{5,7},{6,4},{7,5},{8,10},{9,11},{10,... | collective-permute-start | bytes 393224 | tf_op jit(solution)/shard_map/ppermute | solution.py:313
  34.5 3.8 %collective-permute-start.13 = (bf16[16,512]{1,0:T(8,128)(2,1)S(1)}, bf16[16,512]{1,0:T(8,128)(2,1)S(1)}, u32[]{:S(2)}, u32[]{:S(2)}) collective-permute-start(bf16[16,512]{1,0:T(8,128)(2,1)S(1)} %shard_map.53), channel_id=1, source_target_pairs={{0,4},{1,5},{2,6},{3,7},{4,0},{5,1},{6,2},{7,3},{8,12},{9,13},{10,... | collective-permute-start | bytes 49160 | tf_op jit(solution)/shard_map/ppermute | solution.py:313
  38.4 1.4 %collective-permute-start.14 = (bf16[128,512]{1,0:T(8,128)(2,1)S(1)}, bf16[128,512]{1,0:T(8,128)(2,1)S(1)}, u32[]{:S(2)}, u32[]{:S(2)}) collective-permute-start(bf16[128,512]{1,0:T(8,128)(2,1)S(1)} %get-tuple-element.51), channel_id=1, source_target_pairs={{0,1},{1,0},{2,3},{3,2},{4,5},{5,4},{6,7},{7,6},{8,9},{9,8},{10,11... | collective-permute-start | bytes 393224 | tf_op jit(solution)/shard_map/ppermute | solution.py:313

commit v5 on v4

--- a/solution.py
+++ b/solution.py
@@ -286,14 +286,21 @@
 COST = 4 * 10**9
 
 
-def place_kernel(mine, other, out_ref):
+def place_kernel(other, block, *refs):
+    *_, out_ref, heads, sem = refs
     _, _, core = place()
-    for part in range(PARTS):
-        for kind in range(2):
-            cols = pl.ds((part * 2 + kind) * HD, HD)
-            for half in range(2):
-                total = jnp.where(core == half, mine[:, cols], other[:, cols].astype(F32))
-                out_ref[0, :, pl.ds((kind * KVH + half * PARTS + part) * HD, HD)] = total.astype(out_ref.dtype)
+    half = 1 - core if other else core
+    copies = []
+    for kind in range(2):
+        for part in range(PARTS):
+            to = (kind * PARTS + part) * HD
+            heads[:, to : to + HD] = block[:, pl.ds((part * 2 + kind) * HD, HD)].astype(BF16)
+        wide = PARTS * HD
+        to = pl.ds(pl.multiple_of((kind * KVH + half * PARTS) * HD, HD), wide)
+        copies.append(pltpu.make_async_copy(heads.at[:, pl.ds(kind * wide, wide)], out_ref.at[0, :, to], sem.at[kind]))
+        copies[-1].start()
+    for copy in copies:
+        copy.wait()
 
 
 def on_device(queries, stash, grad_out, lengths):
@@ -364,7 +371,16 @@
     mine, other = call(
         join_kernel, [jax.ShapeDtypeStruct((rows, edge_wide), F32), shape(rows, edge_wide)]
     )(*raw, first, second, ends)
-    return call(place_kernel, shape(1, rows, 2 * KVH * HD))(mine, along(other, flip[1]))
+    vmem = pl.BlockSpec(memory_space=pltpu.VMEM)
+    settle = dict(
+        out=shape(1, rows, 2 * KVH * HD),
+        out_specs=hbm,
+        scratch_shapes=[pltpu.VMEM((rows, edge_wide), BF16), pltpu.SemaphoreType.DMA((2,))],
+    )
+    out = call(functools.partial(place_kernel, False), in_specs=[vmem], **settle)(mine)
+    return call(
+        functools.partial(place_kernel, True), in_specs=[vmem, hbm], input_output_aliases={1: 0}, **settle
+    )(along(other, flip[1]), out)
 
 
 def solution(mesh):

time: 40.8 us -> 40.8 us (level)
  waiting for transfers between devices: 12.8 us -> 12.1 us
  Pallas kernels: 9.87 us -> 10.5 us
    ppermute x14, waiting for transfers between devices: 9.88 us -> 9.19 us  [along(): return lax.ppermute(block, 'ctx', pairs(pick))]
    pallas_call x1 -> x2, Pallas kernels: 0.78 us -> 1.37 us  [the longest x1 0.69 us: on_device(): call(functools.partial(place_kernel, False), in_specs=[vmem], **settle)]
  transfers between devices with their start and end apart: 15 -> 15, of which waited for: 8 -> 8; matrix products, arithmetic and copies ran while one was open for 0% -> 0% of each run, Pallas kernels for 22% -> 24%
where the time goes in v5:
time: 40.8 us; the launch traced here: 40.5 us
  starting transfers between devices  17.1 us (42%)
  waiting for transfers between devices  12.1 us (30%)
  Pallas kernels  10.5 us (26%)
  between operations  0.74 us (2%)
    ppermute x14, starting transfers between devices, along(): return lax.ppermute(block, 'ctx', pairs(pick))  13.1 us
    ppermute x14, waiting for transfers between devices, along(): return lax.ppermute(block, 'ctx', pairs(pick))  9.19 us
    pallas_call x2, Pallas kernels, grads(): call(functools.partial(grad_kernel, stage, halo), [jax.ShapeDtypeStruct(t...  5.3 us
    ppermute x1, starting transfers between devices, partner(): return lax.ppermute(block, ('pipe', 'ctx'), route)  4.04 us
    ppermute x1, waiting for transfers between devices, partner(): return lax.ppermute(block, ('pipe', 'ctx'), route)  2.93 us
    pallas_call x1, Pallas kernels, on_device(): call(stage_kernel, [shape(PARTS, 2 * WIDE + size, HD)] * 2, in_specs=[hbm...  2.2 us
    pallas_call x1, Pallas kernels, beside(): call(functools.partial(hand_kernel, halo, lengths.shape[0]), [shape(2 * r...  1.38 us
  transfers between devices with their start and end apart: 15, of which 8 were waited for; matrix products, arithmetic and copies ran while one was open for 0% of the time, Pallas kernels for 24%

profile of v5, /device:TPU:0, one launch (start us, length us, event | category | flops | bytes accessed | tf_op | source)
XLA Modules:
  0.0 40.5 jit_solution(15822569141013606124)
XLA Ops:
  0.0 4.0 %collective-permute-start.3 = (bf16[1,128,1024]{2,1,0:T(8,128)(2,1)}, bf16[1,128,1024]{2,1,0:T(8,128)(2,1)S(1)}, u32[]{:S(2)}, u32[]{:S(2)}) collective-permute-start(bf16[1,128,1024]{2,1,0:T(8,128)(2,1)} %param.7), channel_id=1, source_target_pairs={{16,0},{17,1},{18,2},{19,3},{20,4},{21,5},{22,6},{23,7},{24,8},{25... | collective-permute-start | bytes 786440 | tf_op jit(solution)/shard_map/ppermute | solution.py:317
  4.7 6.3 %conditional.1 = (bf16[256,2048]{1,0:T(8,128)(2,1)}, bf16[64,128]{1,0:T(8,128)(2,1)}, bf16[64,128]{1,0:T(8,128)(2,1)}) conditional(s32[]{:T(128)} %bitcast, () %tuple.14, (bf16[1,128,4096]{2,1,0:T(8,128)(2,1)}, bf16[1,128,4096]{2,1,0:T(8,128)(2,1)}) %tuple.15), branch_computations={%region_0.0_spmd, %region_1.0_spmd} | conditional | flops 1000 | bytes 4326520 | solution.py:350
  4.7 1.4 %branch_1_fun.1 = (bf16[256,2048]{1,0:T(8,128)(2,1)S(1)}, bf16[64,128]{1,0:T(8,128)(2,1)S(1)}, bf16[64,128]{1,0:T(8,128)(2,1)S(1)}) custom-call(bf16[1,128,4096]{2,1,0:T(8,128)(2,1)} %get-tuple-element.9.q_ref, bf16[1,128,4096]{2,1,0:T(8,128)(2,1)} %get-tuple-element.10.g_ref), custom_call_target="tpu_custom_call" | custom-call | flops 1000 | bytes 1000 | tf_op jit(solution)/shard_map/cond/branch_1_fun/pallas_call | solution.py:339
  6.1 0.1 collective-permute-start
  6.2 1.6 %collective-permute-start.1 = (bf16[64,128]{1,0:T(8,128)(2,1)S(1)}, bf16[64,128]{1,0:T(8,128)(2,1)}, u32[]{:S(2)}, u32[]{:S(2)}) collective-permute-start(bf16[64,128]{1,0:T(8,128)(2,1)S(1)} %get-tuple-element.12), channel_id=1, source_target_pairs={{0,4},{1,5},{2,6},{3,7},{4,0},{5,1},{6,2},{7,3},{8,12},{9,13},{10,... | collective-permute-start | bytes 49160 | tf_op jit(solution)/shard_map/cond/branch_1_fun/ppermute | solution.py:320
  7.8 0.3 collective-permute-start.2
  8.0 2.0 %collective-permute-done.1 = bf16[64,128]{1,0:T(8,128)(2,1)} collective-permute-done((bf16[64,128]{1,0:T(8,128)(2,1)S(1)}, bf16[64,128]{1,0:T(8,128)(2,1)}, u32[]{:S(2)}, u32[]{:S(2)}) %collective-permute-start.1) | collective-permute-done | bytes 16416 | tf_op jit(solution)/shard_map/cond/branch_1_fun/ppermute | solution.py:320
  10.1 0.9 %collective-permute-done.2 = bf16[64,128]{1,0:T(8,128)(2,1)} collective-permute-done((bf16[64,128]{1,0:T(8,128)(2,1)S(1)}, bf16[64,128]{1,0:T(8,128)(2,1)}, u32[]{:S(2)}, u32[]{:S(2)}) %collective-permute-start.2) | collective-permute-done | bytes 16416 | tf_op jit(solution)/shard_map/cond/branch_1_fun/ppermute | solution.py:320
  11.0 0.0 collective-permute-done
  11.0 0.0 copy-start
  11.0 2.2 %shard_map.46 = (bf16[2,2064,128]{2,1,0:T(8,128)(2,1)S(1)}, bf16[2,2064,128]{2,1,0:T(8,128)(2,1)S(1)}) custom-call(bf16[1,128,4096]{2,1,0:T(8,128)(2,1)} %q_ref.1, bf16[1,128,4096]{2,1,0:T(8,128)(2,1)} %g_ref.1, bf16[256,2048]{1,0:T(8,128)(2,1)} %get-tuple-element.33.far, bf16[64,128]{1,0:T(8,128)(2,1)} %get-tuple-element.34.edge0, ...), custom_call_target="tpu_custom_call" | custom-call | flops 1000 | bytes 1000 | tf_op jit(solution)/shard_map/pallas_call | solution.py:351
  13.2 2.9 %collective-permute-done.3.kv_ref = bf16[1,128,1024]{2,1,0:T(8,128)(2,1)S(1)} collective-permute-done((bf16[1,128,1024]{2,1,0:T(8,128)(2,1)}, bf16[1,128,1024]{2,1,0:T(8,128)(2,1)S(1)}, u32[]{:S(2)}, u32[]{:S(2)}) %collective-permute-start.3) | collective-permute-done | bytes 262176 | tf_op jit(solution)/shard_map/ppermute | solution.py:317
  16.2 0.1 shard_map.47
  16.2 0.1 collective-permute-start.4
  16.3 1.7 %collective-permute-start.6 = (bf16[128,256]{1,0:T(8,128)(2,1)S(1)}, bf16[128,256]{1,0:T(8,128)(2,1)S(1)}, u32[]{:S(2)}, u32[]{:S(2)}) collective-permute-start(bf16[128,256]{1,0:T(8,128)(2,1)S(1)} %get-tuple-element.43), channel_id=1, source_target_pairs={{0,3},{1,2},{2,1},{3,0},{4,7},{5,6},{6,5},{7,4},{8,11},{9,10},{10,... | collective-permute-start | bytes 196616 | tf_op jit(solution)/shard_map/ppermute | solution.py:320
  18.0 0.5 %collective-permute-start.5 = (bf16[128,256]{1,0:T(8,128)(2,1)S(1)}, bf16[128,256]{1,0:T(8,128)(2,1)S(1)}, u32[]{:S(2)}, u32[]{:S(2)}) collective-permute-start(bf16[128,256]{1,0:T(8,128)(2,1)S(1)} %get-tuple-element.41.refs_0_), channel_id=1, source_target_pairs={{0,2},{1,3},{2,0},{3,1},{4,6},{5,7},{6,4},{7,5},{8,10},{9,11},{10,... | collective-permute-start | bytes 196616 | tf_op jit(solution)/shard_map/ppermute | solution.py:320
  18.5 0.0 collective-permute-done.4.refs_2_.refs_1_.refs_3_
  18.5 1.6 %collective-permute-start.8 = (bf16[16,512]{1,0:T(8,128)(2,1)S(1)}, bf16[16,512]{1,0:T(8,128)(2,1)S(1)}, u32[]{:S(2)}, u32[]{:S(2)}) collective-permute-start(bf16[16,512]{1,0:T(8,128)(2,1)S(1)} %shard_map.48), channel_id=1, source_target_pairs={{0,4},{1,5},{2,6},{3,7},{4,0},{5,1},{6,2},{7,3},{8,12},{9,13},{10,... | collective-permute-start | bytes 49160 | tf_op jit(solution)/shard_map/ppermute | solution.py:320
  20.1 1.5 %collective-permute-start.7 = (bf16[16,512]{1,0:T(8,128)(2,1)S(1)}, bf16[16,512]{1,0:T(8,128)(2,1)S(1)}, u32[]{:S(2)}, u32[]{:S(2)}) collective-permute-start(bf16[16,512]{1,0:T(8,128)(2,1)S(1)} %shard_map.48), channel_id=1, source_target_pairs={{0,2},{1,3},{2,4},{3,5},{4,6},{5,7},{6,0},{7,1},{8,10},{9,11},{10,... | collective-permute-start | bytes 49160 | tf_op jit(solution)/shard_map/ppermute | solution.py:320
  21.6 0.4 %collective-permute-start.9 = (bf16[128,256]{1,0:T(8,128)(2,1)S(1)}, bf16[128,256]{1,0:T(8,128)(2,1)S(1)}, u32[]{:S(2)}, u32[]{:S(2)}) collective-permute-start(bf16[128,256]{1,0:T(8,128)(2,1)S(1)} %get-tuple-element.44.refs_1_.refs_4_.refs_2_), channel_id=1, source_target_pairs={{0,2},{1,3},{2,0},{3,1},{4,6},{5,7},{6,4},{7,5},{8,10},{9,11},{10,... | collective-permute-start | bytes 196616 | tf_op jit(solution)/shard_map/ppermute | solution.py:320
  22.0 0.0 collective-permute-done.6.refs_3_
  22.0 0.3 collective-permute-start.10
  22.3 0.1 collective-permute-done.5.refs_2_
  22.4 0.0 collective-permute-done.8.refs_6_.refs_7_
  22.4 2.3 %collective-permute-done.7.refs_5_.refs_6_ = bf16[16,512]{1,0:T(8,128)(2,1)S(1)} collective-permute-done((bf16[16,512]{1,0:T(8,128)(2,1)S(1)}, bf16[16,512]{1,0:T(8,128)(2,1)S(1)}, u32[]{:S(2)}, u32[]{:S(2)}) %collective-permute-start.7) | collective-permute-done | bytes 16416 | tf_op jit(solution)/shard_map/ppermute | solution.py:320
  24.7 0.0 copy-done
  24.7 3.9 %shard_map.49 = (f32[2,544,128]{2,1,0:T(8,128)S(1)}, f32[2,544,128]{2,1,0:T(8,128)S(1)}) custom-call(s32[2]{0:T(128)S(1)} %copy-done, bf16[2,2064,128]{2,1,0:T(8,128)(2,1)S(1)} %get-tuple-element.38.q_buf, bf16[2,2064,128]{2,1,0:T(8,128)(2,1)S(1)} %get-tuple-element.39.g_buf, bf16[128,256]{1,0:T(8,128)(2,1)S(1)} %get-tuple-element.41.refs_0_, ...), custom_call_target="tpu_custom_call" | custom-call | flops 4000000000 | bytes 1000 | tf_op jit(solution)/shard_map/pallas_call | solution.py:276
  28.7 0.4 collective-permute-start.11
  29.0 0.0 collective-permute-done.10.refs_5_
  29.0 0.0 collective-permute-done.9.refs_4_
  29.1 1.4 %shard_map.50 = (f32[2,544,128]{2,1,0:T(8,128)S(1)}, f32[2,544,128]{2,1,0:T(8,128)S(1)}) custom-call(s32[2]{0:T(128)S(1)} %copy-done, bf16[2,2064,128]{2,1,0:T(8,128)(2,1)S(1)} %get-tuple-element.38.q_buf, bf16[2,2064,128]{2,1,0:T(8,128)(2,1)S(1)} %get-tuple-element.39.g_buf, f32[2,544,128]{2,1,0:T(8,128)S(1)} %get-tuple-element.45.refs_0_.dk_ref, ...), custom_call_target="tpu_custom_call" | custom-call | flops 4000000000 | bytes 1000 | tf_op jit(solution)/shard_map/pallas_call | solution.py:276
  30.5 4.0 %collective-permute-start.12 = (bf16[128,512]{1,0:T(8,128)(2,1)S(1)}, bf16[128,512]{1,0:T(8,128)(2,1)S(1)}, u32[]{:S(2)}, u32[]{:S(2)}) collective-permute-start(bf16[128,512]{1,0:T(8,128)(2,1)S(1)} %shard_map.52), channel_id=1, source_target_pairs={{0,2},{1,3},{2,0},{3,1},{4,6},{5,7},{6,4},{7,5},{8,10},{9,11},{10,... | collective-permute-start | bytes 393224 | tf_op jit(solution)/shard_map/ppermute | solution.py:320
  34.5 0.0 collective-permute-done.11.across.across0
  34.5 0.7 %collective-permute-start.13 = (bf16[16,512]{1,0:T(8,128)(2,1)S(1)}, bf16[16,512]{1,0:T(8,128)(2,1)S(1)}, u32[]{:S(2)}, u32[]{:S(2)}) collective-permute-start(bf16[16,512]{1,0:T(8,128)(2,1)S(1)} %shard_map.53), channel_id=1, source_target_pairs={{0,4},{1,5},{2,6},{3,7},{4,0},{5,1},{6,2},{7,3},{8,12},{9,13},{10,... | collective-permute-start | bytes 49160 | tf_op jit(solution)/shard_map/ppermute | solution.py:320
  35.2 2.2 %collective-permute-done.12.across1 = bf16[128,512]{1,0:T(8,128)(2,1)S(1)} collective-permute-done((bf16[128,512]{1,0:T(8,128)(2,1)S(1)}, bf16[128,512]{1,0:T(8,128)(2,1)S(1)}, u32[]{:S(2)}, u32[]{:S(2)}) %collective-permute-start.12) | collective-permute-done | bytes 131104 | tf_op jit(solution)/shard_map/ppermute | solution.py:320
  37.4 0.9 %collective-permute-done.13.ends = bf16[16,512]{1,0:T(8,128)(2,1)S(1)} collective-permute-done((bf16[16,512]{1,0:T(8,128)(2,1)S(1)}, bf16[16,512]{1,0:T(8,128)(2,1)S(1)}, u32[]{:S(2)}, u32[]{:S(2)}) %collective-permute-start.13) | collective-permute-done | bytes 16416 | tf_op jit(solution)/shard_map/ppermute | solution.py:320
  38.3 0.1 shard_map.54
  38.4 0.1 collective-permute-start.14
  38.5 0.7 %shard_map.55.refs_0_ = bf16[1,128,1024]{2,1,0:T(8,128)(2,1)} custom-call(f32[128,512]{1,0:T(8,128)S(1)} %get-tuple-element.51.block), custom_call_target="tpu_custom_call" | custom-call | flops 1000 | bytes 1000 | tf_op jit(solution)/shard_map/pallas_call | solution.py:380
  39.2 0.6 %collective-permute-done.14.block = bf16[128,512]{1,0:T(8,128)(2,1)S(1)} collective-permute-done((bf16[128,512]{1,0:T(8,128)(2,1)S(1)}, bf16[128,512]{1,0:T(8,128)(2,1)S(1)}, u32[]{:S(2)}, u32[]{:S(2)}) %collective-permute-start.14) | collective-permute-done | bytes 131104 | tf_op jit(solution)/shard_map/ppermute | solution.py:320
  39.8 0.7 %shard_map.56 = bf16[1,128,1024]{2,1,0:T(8,128)(2,1)} custom-call(bf16[128,512]{1,0:T(8,128)(2,1)S(1)} %collective-permute-done.14.block, bf16[1,128,1024]{2,1,0:T(8,128)(2,1)} %shard_map.55.refs_0_), custom_call_target="tpu_custom_call", output_to_operand_aliasing={{}: (1, {})} | custom-call | flops 1000 | bytes 1000 | tf_op jit(solution)/shard_map/pallas_call | solution.py:381
  (4 shorter events, 0.1 us)
Async XLA Ops:
  0.0 16.2 %collective-permute-start.3 = (bf16[1,128,1024]{2,1,0:T(8,128)(2,1)}, bf16[1,128,1024]{2,1,0:T(8,128)(2,1)S(1)}, u32[]{:S(2)}, u32[]{:S(2)}) collective-permute-start(bf16[1,128,1024]{2,1,0:T(8,128)(2,1)} %param.7), channel_id=1, source_target_pairs={{16,0},{17,1},{18,2},{19,3},{20,4},{21,5},{22,6},{23,7},{24,8},{25... | collective-permute-start | bytes 786440 | tf_op jit(solution)/shard_map/ppermute | solution.py:317
  6.1 4.9 %collective-permute-start = (bf16[256,2048]{1,0:T(8,128)(2,1)S(1)}, bf16[256,2048]{1,0:T(8,128)(2,1)}, u32[]{:S(2)}, u32[]{:S(2)}) collective-permute-start(bf16[256,2048]{1,0:T(8,128)(2,1)S(1)} %get-tuple-element.11), channel_id=1, source_target_pairs={{0,1},{1,0},{2,3},{3,2},{4,5},{5,4},{6,7},{7,6},{8,9},{9,8},{10,11... | collective-permute-start | bytes 3145736 | tf_op jit(solution)/shard_map/cond/branch_1_fun/ppermute | solution.py:320
  6.2 3.9 %collective-permute-start.1 = (bf16[64,128]{1,0:T(8,128)(2,1)S(1)}, bf16[64,128]{1,0:T(8,128)(2,1)}, u32[]{:S(2)}, u32[]{:S(2)}) collective-permute-start(bf16[64,128]{1,0:T(8,128)(2,1)S(1)} %get-tuple-element.12), channel_id=1, source_target_pairs={{0,4},{1,5},{2,6},{3,7},{4,0},{5,1},{6,2},{7,3},{8,12},{9,13},{10,... | collective-permute-start | bytes 49160 | tf_op jit(solution)/shard_map/cond/branch_1_fun/ppermute | solution.py:320
  7.8 3.3 %collective-permute-start.2 = (bf16[64,128]{1,0:T(8,128)(2,1)S(1)}, bf16[64,128]{1,0:T(8,128)(2,1)}, u32[]{:S(2)}, u32[]{:S(2)}) collective-permute-start(bf16[64,128]{1,0:T(8,128)(2,1)S(1)} %get-tuple-element.13), channel_id=1, source_target_pairs={{0,5},{1,4},{2,7},{3,6},{4,1},{5,0},{6,3},{7,2},{8,13},{9,12},{10,... | collective-permute-start | bytes 49160 | tf_op jit(solution)/shard_map/cond/branch_1_fun/ppermute | solution.py:320
  11.0 13.7 %copy-start = (s32[2]{0:T(128)S(1)}, s32[2]{0:T(128)}, u32[]{:S(2)}) copy-start(s32[2]{0:T(128)} %len_ref.3) | copy-start | bytes 28
  16.2 2.2 %collective-permute-start.4 = (bf16[128,512]{1,0:T(8,128)(2,1)S(1)}, bf16[128,512]{1,0:T(8,128)(2,1)S(1)}, u32[]{:S(2)}, u32[]{:S(2)}) collective-permute-start(bf16[128,512]{1,0:T(8,128)(2,1)S(1)} %get-tuple-element.42), channel_id=1, source_target_pairs={{0,1},{1,0},{2,3},{3,2},{4,5},{5,4},{6,7},{7,6},{8,9},{9,8},{10,11... | collective-permute-start | bytes 393224 | tf_op jit(solution)/shard_map/ppermute | solution.py:320
  16.3 5.7 %collective-permute-start.6 = (bf16[128,256]{1,0:T(8,128)(2,1)S(1)}, bf16[128,256]{1,0:T(8,128)(2,1)S(1)}, u32[]{:S(2)}, u32[]{:S(2)}) collective-permute-start(bf16[128,256]{1,0:T(8,128)(2,1)S(1)} %get-tuple-element.43), channel_id=1, source_target_pairs={{0,3},{1,2},{2,1},{3,0},{4,7},{5,6},{6,5},{7,4},{8,11},{9,10},{10,... | collective-permute-start | bytes 196616 | tf_op jit(solution)/shard_map/ppermute | solution.py:320
  18.0 4.4 %collective-permute-start.5 = (bf16[128,256]{1,0:T(8,128)(2,1)S(1)}, bf16[128,256]{1,0:T(8,128)(2,1)S(1)}, u32[]{:S(2)}, u32[]{:S(2)}) collective-permute-start(bf16[128,256]{1,0:T(8,128)(2,1)S(1)} %get-tuple-element.41.refs_0_), channel_id=1, source_target_pairs={{0,2},{1,3},{2,0},{3,1},{4,6},{5,7},{6,4},{7,5},{8,10},{9,11},{10,... | collective-permute-start | bytes 196616 | tf_op jit(solution)/shard_map/ppermute | solution.py:320
  18.5 4.0 %collective-permute-start.8 = (bf16[16,512]{1,0:T(8,128)(2,1)S(1)}, bf16[16,512]{1,0:T(8,128)(2,1)S(1)}, u32[]{:S(2)}, u32[]{:S(2)}) collective-permute-start(bf16[16,512]{1,0:T(8,128)(2,1)S(1)} %shard_map.48), channel_id=1, source_target_pairs={{0,4},{1,5},{2,6},{3,7},{4,0},{5,1},{6,2},{7,3},{8,12},{9,13},{10,... | collective-permute-start | bytes 49160 | tf_op jit(solution)/shard_map/ppermute | solution.py:320
  20.1 4.6 %collective-permute-start.7 = (bf16[16,512]{1,0:T(8,128)(2,1)S(1)}, bf16[16,512]{1,0:T(8,128)(2,1)S(1)}, u32[]{:S(2)}, u32[]{:S(2)}) collective-permute-start(bf16[16,512]{1,0:T(8,128)(2,1)S(1)} %shard_map.48), channel_id=1, source_target_pairs={{0,2},{1,3},{2,4},{3,5},{4,6},{5,7},{6,0},{7,1},{8,10},{9,11},{10,... | collective-permute-start | bytes 49160 | tf_op jit(solution)/shard_map/ppermute | solution.py:320
  21.6 7.5 %collective-permute-start.9 = (bf16[128,256]{1,0:T(8,128)(2,1)S(1)}, bf16[128,256]{1,0:T(8,128)(2,1)S(1)}, u32[]{:S(2)}, u32[]{:S(2)}) collective-permute-start(bf16[128,256]{1,0:T(8,128)(2,1)S(1)} %get-tuple-element.44.refs_1_.refs_4_.refs_2_), channel_id=1, source_target_pairs={{0,2},{1,3},{2,0},{3,1},{4,6},{5,7},{6,4},{7,5},{8,10},{9,11},{10,... | collective-permute-start | bytes 196616 | tf_op jit(solution)/shard_map/ppermute | solution.py:320
  22.0 7.0 %collective-permute-start.10 = (bf16[128,256]{1,0:T(8,128)(2,1)S(1)}, bf16[128,256]{1,0:T(8,128)(2,1)S(1)}, u32[]{:S(2)}, u32[]{:S(2)}) collective-permute-start(bf16[128,256]{1,0:T(8,128)(2,1)S(1)} %get-tuple-element.47), channel_id=1, source_target_pairs={{0,3},{1,2},{2,1},{3,0},{4,7},{5,6},{6,5},{7,4},{8,11},{9,10},{10,... | collective-permute-start | bytes 196616 | tf_op jit(solution)/shard_map/ppermute | solution.py:320
  28.7 5.8 %collective-permute-start.11 = (bf16[144,512]{1,0:T(8,128)(2,1)S(1)}, bf16[144,512]{1,0:T(8,128)(2,1)S(1)}, u32[]{:S(2)}, u32[]{:S(2)}) collective-permute-start(bf16[144,512]{1,0:T(8,128)(2,1)S(1)} %shard_map.51), channel_id=1, source_target_pairs={{0,2},{1,3},{2,0},{3,1},{4,6},{5,7},{6,4},{7,5},{8,10},{9,11},{10,... | collective-permute-start | bytes 442376 | tf_op jit(solution)/shard_map/ppermute | solution.py:320
  30.5 6.9 %collective-permute-start.12 = (bf16[128,512]{1,0:T(8,128)(2,1)S(1)}, bf16[128,512]{1,0:T(8,128)(2,1)S(1)}, u32[]{:S(2)}, u32[]{:S(2)}) collective-permute-start(bf16[128,512]{1,0:T(8,128)(2,1)S(1)} %shard_map.52), channel_id=1, source_target_pairs={{0,2},{1,3},{2,0},{3,1},{4,6},{5,7},{6,4},{7,5},{8,10},{9,11},{10,... | collective-permute-start | bytes 393224 | tf_op jit(solution)/shard_map/ppermute | solution.py:320
  34.5 3.8 %collective-permute-start.13 = (bf16[16,512]{1,0:T(8,128)(2,1)S(1)}, bf16[16,512]{1,0:T(8,128)(2,1)S(1)}, u32[]{:S(2)}, u32[]{:S(2)}) collective-permute-start(bf16[16,512]{1,0:T(8,128)(2,1)S(1)} %shard_map.53), channel_id=1, source_target_pairs={{0,4},{1,5},{2,6},{3,7},{4,0},{5,1},{6,2},{7,3},{8,12},{9,13},{10,... | collective-permute-start | bytes 49160 | tf_op jit(solution)/shard_map/ppermute | solution.py:320
  38.4 1.4 %collective-permute-start.14 = (bf16[128,512]{1,0:T(8,128)(2,1)S(1)}, bf16[128,512]{1,0:T(8,128)(2,1)S(1)}, u32[]{:S(2)}, u32[]{:S(2)}) collective-permute-start(bf16[128,512]{1,0:T(8,128)(2,1)S(1)} %get-tuple-element.50), channel_id=1, source_target_pairs={{0,1},{1,0},{2,3},{3,2},{4,5},{5,4},{6,7},{7,6},{8,9},{9,8},{10,11... | collective-permute-start | bytes 393224 | tf_op jit(solution)/shard_map/ppermute | solution.py:320

commit v6 on v5

--- a/solution.py
+++ b/solution.py
@@ -214,6 +214,7 @@
                 bias = jnp.concatenate([bias] * times, axis=1)
                 return raise_scores(k_buf[part, pl.ds(low, high - low), :], q_buf[part, cols, :], bias)
 
+            tiles.reverse()
             scores = raised(tiles[0])
             for at, (part, cols, low, high, query_pos, start, keep, times) in enumerate(tiles):
                 keys = pl.ds(low, high - low)

time: 40.8 us -> 40.6 us (level)
  no operation moved by 1% of the time
where the time goes in v6:
time: 40.6 us; the launch traced here: 40.3 us
  starting transfers between devices  17.1 us (42%)
  waiting for transfers between devices  12.1 us (30%)
  Pallas kernels  10.3 us (25%)
  between operations  0.74 us (2%)
    ppermute x14, starting transfers between devices, along(): return lax.ppermute(block, 'ctx', pairs(pick))  13.1 us
    ppermute x14, waiting for transfers between devices, along(): return lax.ppermute(block, 'ctx', pairs(pick))  9.18 us
    pallas_call x2, Pallas kernels, grads(): call(functools.partial(grad_kernel, stage, halo), [jax.ShapeDtypeStruct(t...  5.15 us
    ppermute x1, starting transfers between devices, partner(): return lax.ppermute(block, ('pipe', 'ctx'), route)  4.04 us
    ppermute x1, waiting for transfers between devices, partner(): return lax.ppermute(block, ('pipe', 'ctx'), route)  2.93 us
    pallas_call x1, Pallas kernels, on_device(): call(stage_kernel, [shape(PARTS, 2 * WIDE + size, HD)] * 2, in_specs=[hbm...  2.2 us
    pallas_call x1, Pallas kernels, beside(): call(functools.partial(hand_kernel, halo, lengths.shape[0]), [shape(2 * r...  1.38 us
  transfers between devices with their start and end apart: 15, of which 8 were waited for; matrix products, arithmetic and copies ran while one was open for 0% of the time, Pallas kernels for 24%

profile of v6, /device:TPU:0, one launch (start us, length us, event | category | flops | bytes accessed | tf_op | source)
XLA Modules:
  0.0 40.3 jit_solution(14661140982252605327)
XLA Ops:
  0.0 4.0 %collective-permute-start.3 = (bf16[1,128,1024]{2,1,0:T(8,128)(2,1)}, bf16[1,128,1024]{2,1,0:T(8,128)(2,1)S(1)}, u32[]{:S(2)}, u32[]{:S(2)}) collective-permute-start(bf16[1,128,1024]{2,1,0:T(8,128)(2,1)} %param.7), channel_id=1, source_target_pairs={{16,0},{17,1},{18,2},{19,3},{20,4},{21,5},{22,6},{23,7},{24,8},{25... | collective-permute-start | bytes 786440 | tf_op jit(solution)/shard_map/ppermute | solution.py:318
  4.7 6.3 %conditional.1 = (bf16[256,2048]{1,0:T(8,128)(2,1)}, bf16[64,128]{1,0:T(8,128)(2,1)}, bf16[64,128]{1,0:T(8,128)(2,1)}) conditional(s32[]{:T(128)} %bitcast, () %tuple.14, (bf16[1,128,4096]{2,1,0:T(8,128)(2,1)}, bf16[1,128,4096]{2,1,0:T(8,128)(2,1)}) %tuple.15), branch_computations={%region_0.0_spmd, %region_1.0_spmd} | conditional | flops 1000 | bytes 4326520 | solution.py:351
  4.7 1.4 %branch_1_fun.1 = (bf16[256,2048]{1,0:T(8,128)(2,1)S(1)}, bf16[64,128]{1,0:T(8,128)(2,1)S(1)}, bf16[64,128]{1,0:T(8,128)(2,1)S(1)}) custom-call(bf16[1,128,4096]{2,1,0:T(8,128)(2,1)} %get-tuple-element.9.q_ref, bf16[1,128,4096]{2,1,0:T(8,128)(2,1)} %get-tuple-element.10.g_ref), custom_call_target="tpu_custom_call" | custom-call | flops 1000 | bytes 1000 | tf_op jit(solution)/shard_map/cond/branch_1_fun/pallas_call | solution.py:340
  6.1 0.1 collective-permute-start
  6.2 1.6 %collective-permute-start.1 = (bf16[64,128]{1,0:T(8,128)(2,1)S(1)}, bf16[64,128]{1,0:T(8,128)(2,1)}, u32[]{:S(2)}, u32[]{:S(2)}) collective-permute-start(bf16[64,128]{1,0:T(8,128)(2,1)S(1)} %get-tuple-element.12), channel_id=1, source_target_pairs={{0,4},{1,5},{2,6},{3,7},{4,0},{5,1},{6,2},{7,3},{8,12},{9,13},{10,... | collective-permute-start | bytes 49160 | tf_op jit(solution)/shard_map/cond/branch_1_fun/ppermute | solution.py:321
  7.8 0.3 collective-permute-start.2
  8.0 2.0 %collective-permute-done.1 = bf16[64,128]{1,0:T(8,128)(2,1)} collective-permute-done((bf16[64,128]{1,0:T(8,128)(2,1)S(1)}, bf16[64,128]{1,0:T(8,128)(2,1)}, u32[]{:S(2)}, u32[]{:S(2)}) %collective-permute-start.1) | collective-permute-done | bytes 16416 | tf_op jit(solution)/shard_map/cond/branch_1_fun/ppermute | solution.py:321
  10.1 0.9 %collective-permute-done.2 = bf16[64,128]{1,0:T(8,128)(2,1)} collective-permute-done((bf16[64,128]{1,0:T(8,128)(2,1)S(1)}, bf16[64,128]{1,0:T(8,128)(2,1)}, u32[]{:S(2)}, u32[]{:S(2)}) %collective-permute-start.2) | collective-permute-done | bytes 16416 | tf_op jit(solution)/shard_map/cond/branch_1_fun/ppermute | solution.py:321
  11.0 0.0 collective-permute-done
  11.0 0.0 copy-start
  11.0 2.2 %shard_map.46 = (bf16[2,2064,128]{2,1,0:T(8,128)(2,1)S(1)}, bf16[2,2064,128]{2,1,0:T(8,128)(2,1)S(1)}) custom-call(bf16[1,128,4096]{2,1,0:T(8,128)(2,1)} %q_ref.1, bf16[1,128,4096]{2,1,0:T(8,128)(2,1)} %g_ref.1, bf16[256,2048]{1,0:T(8,128)(2,1)} %get-tuple-element.33.far, bf16[64,128]{1,0:T(8,128)(2,1)} %get-tuple-element.34.edge0, ...), custom_call_target="tpu_custom_call" | custom-call | flops 1000 | bytes 1000 | tf_op jit(solution)/shard_map/pallas_call | solution.py:352
  13.2 2.9 %collective-permute-done.3.kv_ref = bf16[1,128,1024]{2,1,0:T(8,128)(2,1)S(1)} collective-permute-done((bf16[1,128,1024]{2,1,0:T(8,128)(2,1)}, bf16[1,128,1024]{2,1,0:T(8,128)(2,1)S(1)}, u32[]{:S(2)}, u32[]{:S(2)}) %collective-permute-start.3) | collective-permute-done | bytes 262176 | tf_op jit(solution)/shard_map/ppermute | solution.py:318
  16.2 0.1 shard_map.47
  16.2 0.1 collective-permute-start.4
  16.3 1.7 %collective-permute-start.6 = (bf16[128,256]{1,0:T(8,128)(2,1)S(1)}, bf16[128,256]{1,0:T(8,128)(2,1)S(1)}, u32[]{:S(2)}, u32[]{:S(2)}) collective-permute-start(bf16[128,256]{1,0:T(8,128)(2,1)S(1)} %get-tuple-element.43), channel_id=1, source_target_pairs={{0,3},{1,2},{2,1},{3,0},{4,7},{5,6},{6,5},{7,4},{8,11},{9,10},{10,... | collective-permute-start | bytes 196616 | tf_op jit(solution)/shard_map/ppermute | solution.py:321
  18.0 0.5 %collective-permute-start.5 = (bf16[128,256]{1,0:T(8,128)(2,1)S(1)}, bf16[128,256]{1,0:T(8,128)(2,1)S(1)}, u32[]{:S(2)}, u32[]{:S(2)}) collective-permute-start(bf16[128,256]{1,0:T(8,128)(2,1)S(1)} %get-tuple-element.41.refs_0_), channel_id=1, source_target_pairs={{0,2},{1,3},{2,0},{3,1},{4,6},{5,7},{6,4},{7,5},{8,10},{9,11},{10,... | collective-permute-start | bytes 196616 | tf_op jit(solution)/shard_map/ppermute | solution.py:321
  18.5 0.0 collective-permute-done.4.refs_2_.refs_1_.refs_3_
  18.5 1.6 %collective-permute-start.8 = (bf16[16,512]{1,0:T(8,128)(2,1)S(1)}, bf16[16,512]{1,0:T(8,128)(2,1)S(1)}, u32[]{:S(2)}, u32[]{:S(2)}) collective-permute-start(bf16[16,512]{1,0:T(8,128)(2,1)S(1)} %shard_map.48), channel_id=1, source_target_pairs={{0,4},{1,5},{2,6},{3,7},{4,0},{5,1},{6,2},{7,3},{8,12},{9,13},{10,... | collective-permute-start | bytes 49160 | tf_op jit(solution)/shard_map/ppermute | solution.py:321
  20.1 1.5 %collective-permute-start.7 = (bf16[16,512]{1,0:T(8,128)(2,1)S(1)}, bf16[16,512]{1,0:T(8,128)(2,1)S(1)}, u32[]{:S(2)}, u32[]{:S(2)}) collective-permute-start(bf16[16,512]{1,0:T(8,128)(2,1)S(1)} %shard_map.48), channel_id=1, source_target_pairs={{0,2},{1,3},{2,4},{3,5},{4,6},{5,7},{6,0},{7,1},{8,10},{9,11},{10,... | collective-permute-start | bytes 49160 | tf_op jit(solution)/shard_map/ppermute | solution.py:321
  21.6 0.4 %collective-permute-start.9 = (bf16[128,256]{1,0:T(8,128)(2,1)S(1)}, bf16[128,256]{1,0:T(8,128)(2,1)S(1)}, u32[]{:S(2)}, u32[]{:S(2)}) collective-permute-start(bf16[128,256]{1,0:T(8,128)(2,1)S(1)} %get-tuple-element.44.refs_1_.refs_4_.refs_2_), channel_id=1, source_target_pairs={{0,2},{1,3},{2,0},{3,1},{4,6},{5,7},{6,4},{7,5},{8,10},{9,11},{10,... | collective-permute-start | bytes 196616 | tf_op jit(solution)/shard_map/ppermute | solution.py:321
  22.0 0.0 collective-permute-done.6.refs_3_
  22.0 0.3 collective-permute-start.10
  22.3 0.1 collective-permute-done.5.refs_2_
  22.4 0.0 collective-permute-done.8.refs_6_.refs_7_
  22.4 2.3 %collective-permute-done.7.refs_5_.refs_6_ = bf16[16,512]{1,0:T(8,128)(2,1)S(1)} collective-permute-done((bf16[16,512]{1,0:T(8,128)(2,1)S(1)}, bf16[16,512]{1,0:T(8,128)(2,1)S(1)}, u32[]{:S(2)}, u32[]{:S(2)}) %collective-permute-start.7) | collective-permute-done | bytes 16416 | tf_op jit(solution)/shard_map/ppermute | solution.py:321
  24.7 0.0 copy-done
  24.7 3.8 %shard_map.49 = (f32[2,544,128]{2,1,0:T(8,128)S(1)}, f32[2,544,128]{2,1,0:T(8,128)S(1)}) custom-call(s32[2]{0:T(128)S(1)} %copy-done, bf16[2,2064,128]{2,1,0:T(8,128)(2,1)S(1)} %get-tuple-element.38.q_buf, bf16[2,2064,128]{2,1,0:T(8,128)(2,1)S(1)} %get-tuple-element.39.g_buf, bf16[128,256]{1,0:T(8,128)(2,1)S(1)} %get-tuple-element.41.refs_0_, ...), custom_call_target="tpu_custom_call" | custom-call | flops 4000000000 | bytes 1000 | tf_op jit(solution)/shard_map/pallas_call | solution.py:277
  28.5 0.5 %collective-permute-start.11 = (bf16[144,512]{1,0:T(8,128)(2,1)S(1)}, bf16[144,512]{1,0:T(8,128)(2,1)S(1)}, u32[]{:S(2)}, u32[]{:S(2)}) collective-permute-start(bf16[144,512]{1,0:T(8,128)(2,1)S(1)} %shard_map.51), channel_id=1, source_target_pairs={{0,2},{1,3},{2,0},{3,1},{4,6},{5,7},{6,4},{7,5},{8,10},{9,11},{10,... | collective-permute-start | bytes 442376 | tf_op jit(solution)/shard_map/ppermute | solution.py:321
  29.0 0.0 collective-permute-done.10.refs_5_
  29.1 0.0 collective-permute-done.9.refs_4_
  29.1 1.4 %shard_map.50 = (f32[2,544,128]{2,1,0:T(8,128)S(1)}, f32[2,544,128]{2,1,0:T(8,128)S(1)}) custom-call(s32[2]{0:T(128)S(1)} %copy-done, bf16[2,2064,128]{2,1,0:T(8,128)(2,1)S(1)} %get-tuple-element.38.q_buf, bf16[2,2064,128]{2,1,0:T(8,128)(2,1)S(1)} %get-tuple-element.39.g_buf, f32[2,544,128]{2,1,0:T(8,128)S(1)} %get-tuple-element.45.refs_0_.dk_ref, ...), custom_call_target="tpu_custom_call" | custom-call | flops 4000000000 | bytes 1000 | tf_op jit(solution)/shard_map/pallas_call | solution.py:277
  30.5 3.8 %collective-permute-start.12 = (bf16[128,512]{1,0:T(8,128)(2,1)S(1)}, bf16[128,512]{1,0:T(8,128)(2,1)S(1)}, u32[]{:S(2)}, u32[]{:S(2)}) collective-permute-start(bf16[128,512]{1,0:T(8,128)(2,1)S(1)} %shard_map.52), channel_id=1, source_target_pairs={{0,2},{1,3},{2,0},{3,1},{4,6},{5,7},{6,4},{7,5},{8,10},{9,11},{10,... | collective-permute-start | bytes 393224 | tf_op jit(solution)/shard_map/ppermute | solution.py:321
  34.3 0.0 collective-permute-done.11.across.across0
  34.4 0.7 %collective-permute-start.13 = (bf16[16,512]{1,0:T(8,128)(2,1)S(1)}, bf16[16,512]{1,0:T(8,128)(2,1)S(1)}, u32[]{:S(2)}, u32[]{:S(2)}) collective-permute-start(bf16[16,512]{1,0:T(8,128)(2,1)S(1)} %shard_map.53), channel_id=1, source_target_pairs={{0,4},{1,5},{2,6},{3,7},{4,0},{5,1},{6,2},{7,3},{8,12},{9,13},{10,... | collective-permute-start | bytes 49160 | tf_op jit(solution)/shard_map/ppermute | solution.py:321
  35.1 2.2 %collective-permute-done.12.across1 = bf16[128,512]{1,0:T(8,128)(2,1)S(1)} collective-permute-done((bf16[128,512]{1,0:T(8,128)(2,1)S(1)}, bf16[128,512]{1,0:T(8,128)(2,1)S(1)}, u32[]{:S(2)}, u32[]{:S(2)}) %collective-permute-start.12) | collective-permute-done | bytes 131104 | tf_op jit(solution)/shard_map/ppermute | solution.py:321
  37.3 0.9 %collective-permute-done.13.ends = bf16[16,512]{1,0:T(8,128)(2,1)S(1)} collective-permute-done((bf16[16,512]{1,0:T(8,128)(2,1)S(1)}, bf16[16,512]{1,0:T(8,128)(2,1)S(1)}, u32[]{:S(2)}, u32[]{:S(2)}) %collective-permute-start.13) | collective-permute-done | bytes 16416 | tf_op jit(solution)/shard_map/ppermute | solution.py:321
  38.2 0.1 shard_map.54
  38.2 0.1 collective-permute-start.14
  38.3 0.7 %shard_map.55.refs_0_ = bf16[1,128,1024]{2,1,0:T(8,128)(2,1)} custom-call(f32[128,512]{1,0:T(8,128)S(1)} %get-tuple-element.51.block), custom_call_target="tpu_custom_call" | custom-call | flops 1000 | bytes 1000 | tf_op jit(solution)/shard_map/pallas_call | solution.py:381
  39.0 0.6 %collective-permute-done.14.block = bf16[128,512]{1,0:T(8,128)(2,1)S(1)} collective-permute-done((bf16[128,512]{1,0:T(8,128)(2,1)S(1)}, bf16[128,512]{1,0:T(8,128)(2,1)S(1)}, u32[]{:S(2)}, u32[]{:S(2)}) %collective-permute-start.14) | collective-permute-done | bytes 131104 | tf_op jit(solution)/shard_map/ppermute | solution.py:321
  39.7 0.7 %shard_map.56 = bf16[1,128,1024]{2,1,0:T(8,128)(2,1)} custom-call(bf16[128,512]{1,0:T(8,128)(2,1)S(1)} %collective-permute-done.14.block, bf16[1,128,1024]{2,1,0:T(8,128)(2,1)} %shard_map.55.refs_0_), custom_call_target="tpu_custom_call", output_to_operand_aliasing={{}: (1, {})} | custom-call | flops 1000 | bytes 1000 | tf_op jit(solution)/shard_map/pallas_call | solution.py:382
  (4 shorter events, 0.1 us)
Async XLA Ops:
  0.0 16.2 %collective-permute-start.3 = (bf16[1,128,1024]{2,1,0:T(8,128)(2,1)}, bf16[1,128,1024]{2,1,0:T(8,128)(2,1)S(1)}, u32[]{:S(2)}, u32[]{:S(2)}) collective-permute-start(bf16[1,128,1024]{2,1,0:T(8,128)(2,1)} %param.7), channel_id=1, source_target_pairs={{16,0},{17,1},{18,2},{19,3},{20,4},{21,5},{22,6},{23,7},{24,8},{25... | collective-permute-start | bytes 786440 | tf_op jit(solution)/shard_map/ppermute | solution.py:318
  6.1 4.9 %collective-permute-start = (bf16[256,2048]{1,0:T(8,128)(2,1)S(1)}, bf16[256,2048]{1,0:T(8,128)(2,1)}, u32[]{:S(2)}, u32[]{:S(2)}) collective-permute-start(bf16[256,2048]{1,0:T(8,128)(2,1)S(1)} %get-tuple-element.11), channel_id=1, source_target_pairs={{0,1},{1,0},{2,3},{3,2},{4,5},{5,4},{6,7},{7,6},{8,9},{9,8},{10,11... | collective-permute-start | bytes 3145736 | tf_op jit(solution)/shard_map/cond/branch_1_fun/ppermute | solution.py:321
  6.2 3.9 %collective-permute-start.1 = (bf16[64,128]{1,0:T(8,128)(2,1)S(1)}, bf16[64,128]{1,0:T(8,128)(2,1)}, u32[]{:S(2)}, u32[]{:S(2)}) collective-permute-start(bf16[64,128]{1,0:T(8,128)(2,1)S(1)} %get-tuple-element.12), channel_id=1, source_target_pairs={{0,4},{1,5},{2,6},{3,7},{4,0},{5,1},{6,2},{7,3},{8,12},{9,13},{10,... | collective-permute-start | bytes 49160 | tf_op jit(solution)/shard_map/cond/branch_1_fun/ppermute | solution.py:321
  7.8 3.3 %collective-permute-start.2 = (bf16[64,128]{1,0:T(8,128)(2,1)S(1)}, bf16[64,128]{1,0:T(8,128)(2,1)}, u32[]{:S(2)}, u32[]{:S(2)}) collective-permute-start(bf16[64,128]{1,0:T(8,128)(2,1)S(1)} %get-tuple-element.13), channel_id=1, source_target_pairs={{0,5},{1,4},{2,7},{3,6},{4,1},{5,0},{6,3},{7,2},{8,13},{9,12},{10,... | collective-permute-start | bytes 49160 | tf_op jit(solution)/shard_map/cond/branch_1_fun/ppermute | solution.py:321
  11.0 13.7 %copy-start = (s32[2]{0:T(128)S(1)}, s32[2]{0:T(128)}, u32[]{:S(2)}) copy-start(s32[2]{0:T(128)} %len_ref.3) | copy-start | bytes 28
  16.2 2.2 %collective-permute-start.4 = (bf16[128,512]{1,0:T(8,128)(2,1)S(1)}, bf16[128,512]{1,0:T(8,128)(2,1)S(1)}, u32[]{:S(2)}, u32[]{:S(2)}) collective-permute-start(bf16[128,512]{1,0:T(8,128)(2,1)S(1)} %get-tuple-element.42), channel_id=1, source_target_pairs={{0,1},{1,0},{2,3},{3,2},{4,5},{5,4},{6,7},{7,6},{8,9},{9,8},{10,11... | collective-permute-start | bytes 393224 | tf_op jit(solution)/shard_map/ppermute | solution.py:321
  16.3 5.7 %collective-permute-start.6 = (bf16[128,256]{1,0:T(8,128)(2,1)S(1)}, bf16[128,256]{1,0:T(8,128)(2,1)S(1)}, u32[]{:S(2)}, u32[]{:S(2)}) collective-permute-start(bf16[128,256]{1,0:T(8,128)(2,1)S(1)} %get-tuple-element.43), channel_id=1, source_target_pairs={{0,3},{1,2},{2,1},{3,0},{4,7},{5,6},{6,5},{7,4},{8,11},{9,10},{10,... | collective-permute-start | bytes 196616 | tf_op jit(solution)/shard_map/ppermute | solution.py:321
  18.0 4.4 %collective-permute-start.5 = (bf16[128,256]{1,0:T(8,128)(2,1)S(1)}, bf16[128,256]{1,0:T(8,128)(2,1)S(1)}, u32[]{:S(2)}, u32[]{:S(2)}) collective-permute-start(bf16[128,256]{1,0:T(8,128)(2,1)S(1)} %get-tuple-element.41.refs_0_), channel_id=1, source_target_pairs={{0,2},{1,3},{2,0},{3,1},{4,6},{5,7},{6,4},{7,5},{8,10},{9,11},{10,... | collective-permute-start | bytes 196616 | tf_op jit(solution)/shard_map/ppermute | solution.py:321
  18.5 4.0 %collective-permute-start.8 = (bf16[16,512]{1,0:T(8,128)(2,1)S(1)}, bf16[16,512]{1,0:T(8,128)(2,1)S(1)}, u32[]{:S(2)}, u32[]{:S(2)}) collective-permute-start(bf16[16,512]{1,0:T(8,128)(2,1)S(1)} %shard_map.48), channel_id=1, source_target_pairs={{0,4},{1,5},{2,6},{3,7},{4,0},{5,1},{6,2},{7,3},{8,12},{9,13},{10,... | collective-permute-start | bytes 49160 | tf_op jit(solution)/shard_map/ppermute | solution.py:321
  20.1 4.6 %collective-permute-start.7 = (bf16[16,512]{1,0:T(8,128)(2,1)S(1)}, bf16[16,512]{1,0:T(8,128)(2,1)S(1)}, u32[]{:S(2)}, u32[]{:S(2)}) collective-permute-start(bf16[16,512]{1,0:T(8,128)(2,1)S(1)} %shard_map.48), channel_id=1, source_target_pairs={{0,2},{1,3},{2,4},{3,5},{4,6},{5,7},{6,0},{7,1},{8,10},{9,11},{10,... | collective-permute-start | bytes 49160 | tf_op jit(solution)/shard_map/ppermute | solution.py:321
  21.6 7.5 %collective-permute-start.9 = (bf16[128,256]{1,0:T(8,128)(2,1)S(1)}, bf16[128,256]{1,0:T(8,128)(2,1)S(1)}, u32[]{:S(2)}, u32[]{:S(2)}) collective-permute-start(bf16[128,256]{1,0:T(8,128)(2,1)S(1)} %get-tuple-element.44.refs_1_.refs_4_.refs_2_), channel_id=1, source_target_pairs={{0,2},{1,3},{2,0},{3,1},{4,6},{5,7},{6,4},{7,5},{8,10},{9,11},{10,... | collective-permute-start | bytes 196616 | tf_op jit(solution)/shard_map/ppermute | solution.py:321
  22.0 7.0 %collective-permute-start.10 = (bf16[128,256]{1,0:T(8,128)(2,1)S(1)}, bf16[128,256]{1,0:T(8,128)(2,1)S(1)}, u32[]{:S(2)}, u32[]{:S(2)}) collective-permute-start(bf16[128,256]{1,0:T(8,128)(2,1)S(1)} %get-tuple-element.47), channel_id=1, source_target_pairs={{0,3},{1,2},{2,1},{3,0},{4,7},{5,6},{6,5},{7,4},{8,11},{9,10},{10,... | collective-permute-start | bytes 196616 | tf_op jit(solution)/shard_map/ppermute | solution.py:321
  28.5 5.8 %collective-permute-start.11 = (bf16[144,512]{1,0:T(8,128)(2,1)S(1)}, bf16[144,512]{1,0:T(8,128)(2,1)S(1)}, u32[]{:S(2)}, u32[]{:S(2)}) collective-permute-start(bf16[144,512]{1,0:T(8,128)(2,1)S(1)} %shard_map.51), channel_id=1, source_target_pairs={{0,2},{1,3},{2,0},{3,1},{4,6},{5,7},{6,4},{7,5},{8,10},{9,11},{10,... | collective-permute-start | bytes 442376 | tf_op jit(solution)/shard_map/ppermute | solution.py:321
  30.5 6.8 %collective-permute-start.12 = (bf16[128,512]{1,0:T(8,128)(2,1)S(1)}, bf16[128,512]{1,0:T(8,128)(2,1)S(1)}, u32[]{:S(2)}, u32[]{:S(2)}) collective-permute-start(bf16[128,512]{1,0:T(8,128)(2,1)S(1)} %shard_map.52), channel_id=1, source_target_pairs={{0,2},{1,3},{2,0},{3,1},{4,6},{5,7},{6,4},{7,5},{8,10},{9,11},{10,... | collective-permute-start | bytes 393224 | tf_op jit(solution)/shard_map/ppermute | solution.py:321
  34.4 3.8 %collective-permute-start.13 = (bf16[16,512]{1,0:T(8,128)(2,1)S(1)}, bf16[16,512]{1,0:T(8,128)(2,1)S(1)}, u32[]{:S(2)}, u32[]{:S(2)}) collective-permute-start(bf16[16,512]{1,0:T(8,128)(2,1)S(1)} %shard_map.53), channel_id=1, source_target_pairs={{0,4},{1,5},{2,6},{3,7},{4,0},{5,1},{6,2},{7,3},{8,12},{9,13},{10,... | collective-permute-start | bytes 49160 | tf_op jit(solution)/shard_map/ppermute | solution.py:321
  38.2 1.4 %collective-permute-start.14 = (bf16[128,512]{1,0:T(8,128)(2,1)S(1)}, bf16[128,512]{1,0:T(8,128)(2,1)S(1)}, u32[]{:S(2)}, u32[]{:S(2)}) collective-permute-start(bf16[128,512]{1,0:T(8,128)(2,1)S(1)} %get-tuple-element.50), channel_id=1, source_target_pairs={{0,1},{1,0},{2,3},{3,2},{4,5},{5,4},{6,7},{7,6},{8,9},{9,8},{10,11... | collective-permute-start | bytes 393224 | tf_op jit(solution)/shard_map/ppermute | solution.py:321

commit v7 on v6

--- a/solution.py
+++ b/solution.py
@@ -220,10 +220,10 @@
                 keys = pl.ds(low, high - low)
                 query, cot = q_buf[part, cols, :], g_buf[part, cols, :]
                 weights = softmax(scores, jnp.concatenate([keep] * times, axis=1))
+                if at + 1 < len(tiles):
+                    scores = raised(tiles[at + 1])
                 dweights = lax.dot_general(v_buf[part, keys, :], cot, NT, preferred_element_type=F32)
                 dv_ref[part, keys, :] += lax.dot_general(weights.astype(BF16), cot, NN, preferred_element_type=F32)
-                if at + 1 < len(tiles):
-                    scores = raised(tiles[at + 1])
                 delta = jnp.sum(weights * dweights, axis=0, keepdims=True)
                 dscores = (weights * (dweights - delta)).astype(BF16)
                 dk_ref[part, keys, :] += lax.dot_general(dscores, query, NN, preferred_element_type=F32)

time: 40.6 us -> 40.7 us (level)
  transfers between devices with their start and end apart: 15 -> 15, of which waited for: 8 -> 8; matrix products, arithmetic and copies ran while one was open for 0% -> 0% of each run, Pallas kernels for 24% -> 23%
where the time goes in v7:
time: 40.7 us; the launch traced here: 40.5 us
  starting transfers between devices  17.3 us (43%)
  waiting for transfers between devices  12.1 us (30%)
  Pallas kernels  10.3 us (25%)
  between operations  0.74 us (2%)
    ppermute x14, starting transfers between devices, along(): return lax.ppermute(block, 'ctx', pairs(pick))  13.2 us
    ppermute x14, waiting for transfers between devices, along(): return lax.ppermute(block, 'ctx', pairs(pick))  9.18 us
    pallas_call x2, Pallas kernels, grads(): call(functools.partial(grad_kernel, stage, halo), [jax.ShapeDtypeStruct(t...  5.14 us
    ppermute x1, starting transfers between devices, partner(): return lax.ppermute(block, ('pipe', 'ctx'), route)  4.04 us
    ppermute x1, waiting for transfers between devices, partner(): return lax.ppermute(block, ('pipe', 'ctx'), route)  2.93 us
    pallas_call x1, Pallas kernels, on_device(): call(stage_kernel, [shape(PARTS, 2 * WIDE + size, HD)] * 2, in_specs=[hbm...  2.2 us
    pallas_call x1, Pallas kernels, beside(): call(functools.partial(hand_kernel, halo, lengths.shape[0]), [shape(2 * r...  1.38 us
  transfers between devices with their start and end apart: 15, of which 8 were waited for; matrix products, arithmetic and copies ran while one was open for 0% of the time, Pallas kernels for 23%

profile of v7, /device:TPU:0, one launch (start us, length us, event | category | flops | bytes accessed | tf_op | source)
XLA Modules:
  0.0 40.5 jit_solution(13040335615586670133)
XLA Ops:
  0.0 4.0 %collective-permute-start.3 = (bf16[1,128,1024]{2,1,0:T(8,128)(2,1)}, bf16[1,128,1024]{2,1,0:T(8,128)(2,1)S(1)}, u32[]{:S(2)}, u32[]{:S(2)}) collective-permute-start(bf16[1,128,1024]{2,1,0:T(8,128)(2,1)} %param.7), channel_id=1, source_target_pairs={{16,0},{17,1},{18,2},{19,3},{20,4},{21,5},{22,6},{23,7},{24,8},{25... | collective-permute-start | bytes 786440 | tf_op jit(solution)/shard_map/ppermute | solution.py:318
  4.7 6.3 %conditional.1 = (bf16[256,2048]{1,0:T(8,128)(2,1)}, bf16[64,128]{1,0:T(8,128)(2,1)}, bf16[64,128]{1,0:T(8,128)(2,1)}) conditional(s32[]{:T(128)} %bitcast, () %tuple.14, (bf16[1,128,4096]{2,1,0:T(8,128)(2,1)}, bf16[1,128,4096]{2,1,0:T(8,128)(2,1)}) %tuple.15), branch_computations={%region_0.0_spmd, %region_1.0_spmd} | conditional | flops 1000 | bytes 4326520 | solution.py:351
  4.7 1.4 %branch_1_fun.1 = (bf16[256,2048]{1,0:T(8,128)(2,1)S(1)}, bf16[64,128]{1,0:T(8,128)(2,1)S(1)}, bf16[64,128]{1,0:T(8,128)(2,1)S(1)}) custom-call(bf16[1,128,4096]{2,1,0:T(8,128)(2,1)} %get-tuple-element.9.q_ref, bf16[1,128,4096]{2,1,0:T(8,128)(2,1)} %get-tuple-element.10.g_ref), custom_call_target="tpu_custom_call" | custom-call | flops 1000 | bytes 1000 | tf_op jit(solution)/shard_map/cond/branch_1_fun/pallas_call | solution.py:340
  6.1 0.1 collective-permute-start
  6.2 1.6 %collective-permute-start.1 = (bf16[64,128]{1,0:T(8,128)(2,1)S(1)}, bf16[64,128]{1,0:T(8,128)(2,1)}, u32[]{:S(2)}, u32[]{:S(2)}) collective-permute-start(bf16[64,128]{1,0:T(8,128)(2,1)S(1)} %get-tuple-element.12), channel_id=1, source_target_pairs={{0,4},{1,5},{2,6},{3,7},{4,0},{5,1},{6,2},{7,3},{8,12},{9,13},{10,... | collective-permute-start | bytes 49160 | tf_op jit(solution)/shard_map/cond/branch_1_fun/ppermute | solution.py:321
  7.8 0.3 collective-permute-start.2
  8.0 2.0 %collective-permute-done.1 = bf16[64,128]{1,0:T(8,128)(2,1)} collective-permute-done((bf16[64,128]{1,0:T(8,128)(2,1)S(1)}, bf16[64,128]{1,0:T(8,128)(2,1)}, u32[]{:S(2)}, u32[]{:S(2)}) %collective-permute-start.1) | collective-permute-done | bytes 16416 | tf_op jit(solution)/shard_map/cond/branch_1_fun/ppermute | solution.py:321
  10.1 0.9 %collective-permute-done.2 = bf16[64,128]{1,0:T(8,128)(2,1)} collective-permute-done((bf16[64,128]{1,0:T(8,128)(2,1)S(1)}, bf16[64,128]{1,0:T(8,128)(2,1)}, u32[]{:S(2)}, u32[]{:S(2)}) %collective-permute-start.2) | collective-permute-done | bytes 16416 | tf_op jit(solution)/shard_map/cond/branch_1_fun/ppermute | solution.py:321
  11.0 0.0 collective-permute-done
  11.0 0.0 copy-start
  11.0 2.2 %shard_map.46 = (bf16[2,2064,128]{2,1,0:T(8,128)(2,1)S(1)}, bf16[2,2064,128]{2,1,0:T(8,128)(2,1)S(1)}) custom-call(bf16[1,128,4096]{2,1,0:T(8,128)(2,1)} %q_ref.1, bf16[1,128,4096]{2,1,0:T(8,128)(2,1)} %g_ref.1, bf16[256,2048]{1,0:T(8,128)(2,1)} %get-tuple-element.33.far, bf16[64,128]{1,0:T(8,128)(2,1)} %get-tuple-element.34.edge0, ...), custom_call_target="tpu_custom_call" | custom-call | flops 1000 | bytes 1000 | tf_op jit(solution)/shard_map/pallas_call | solution.py:352
  13.2 2.9 %collective-permute-done.3.kv_ref = bf16[1,128,1024]{2,1,0:T(8,128)(2,1)S(1)} collective-permute-done((bf16[1,128,1024]{2,1,0:T(8,128)(2,1)}, bf16[1,128,1024]{2,1,0:T(8,128)(2,1)S(1)}, u32[]{:S(2)}, u32[]{:S(2)}) %collective-permute-start.3) | collective-permute-done | bytes 262176 | tf_op jit(solution)/shard_map/ppermute | solution.py:318
  16.2 0.1 shard_map.47
  16.2 0.1 collective-permute-start.4
  16.3 1.7 %collective-permute-start.6 = (bf16[128,256]{1,0:T(8,128)(2,1)S(1)}, bf16[128,256]{1,0:T(8,128)(2,1)S(1)}, u32[]{:S(2)}, u32[]{:S(2)}) collective-permute-start(bf16[128,256]{1,0:T(8,128)(2,1)S(1)} %get-tuple-element.43), channel_id=1, source_target_pairs={{0,3},{1,2},{2,1},{3,0},{4,7},{5,6},{6,5},{7,4},{8,11},{9,10},{10,... | collective-permute-start | bytes 196616 | tf_op jit(solution)/shard_map/ppermute | solution.py:321
  18.0 0.5 %collective-permute-start.5 = (bf16[128,256]{1,0:T(8,128)(2,1)S(1)}, bf16[128,256]{1,0:T(8,128)(2,1)S(1)}, u32[]{:S(2)}, u32[]{:S(2)}) collective-permute-start(bf16[128,256]{1,0:T(8,128)(2,1)S(1)} %get-tuple-element.41.refs_0_), channel_id=1, source_target_pairs={{0,2},{1,3},{2,0},{3,1},{4,6},{5,7},{6,4},{7,5},{8,10},{9,11},{10,... | collective-permute-start | bytes 196616 | tf_op jit(solution)/shard_map/ppermute | solution.py:321
  18.5 0.0 collective-permute-done.4.refs_2_.refs_1_.refs_3_
  18.5 1.6 %collective-permute-start.8 = (bf16[16,512]{1,0:T(8,128)(2,1)S(1)}, bf16[16,512]{1,0:T(8,128)(2,1)S(1)}, u32[]{:S(2)}, u32[]{:S(2)}) collective-permute-start(bf16[16,512]{1,0:T(8,128)(2,1)S(1)} %shard_map.48), channel_id=1, source_target_pairs={{0,4},{1,5},{2,6},{3,7},{4,0},{5,1},{6,2},{7,3},{8,12},{9,13},{10,... | collective-permute-start | bytes 49160 | tf_op jit(solution)/shard_map/ppermute | solution.py:321
  20.1 1.5 %collective-permute-start.7 = (bf16[16,512]{1,0:T(8,128)(2,1)S(1)}, bf16[16,512]{1,0:T(8,128)(2,1)S(1)}, u32[]{:S(2)}, u32[]{:S(2)}) collective-permute-start(bf16[16,512]{1,0:T(8,128)(2,1)S(1)} %shard_map.48), channel_id=1, source_target_pairs={{0,2},{1,3},{2,4},{3,5},{4,6},{5,7},{6,0},{7,1},{8,10},{9,11},{10,... | collective-permute-start | bytes 49160 | tf_op jit(solution)/shard_map/ppermute | solution.py:321
  21.6 0.4 %collective-permute-start.9 = (bf16[128,256]{1,0:T(8,128)(2,1)S(1)}, bf16[128,256]{1,0:T(8,128)(2,1)S(1)}, u32[]{:S(2)}, u32[]{:S(2)}) collective-permute-start(bf16[128,256]{1,0:T(8,128)(2,1)S(1)} %get-tuple-element.44.refs_1_.refs_4_.refs_2_), channel_id=1, source_target_pairs={{0,2},{1,3},{2,0},{3,1},{4,6},{5,7},{6,4},{7,5},{8,10},{9,11},{10,... | collective-permute-start | bytes 196616 | tf_op jit(solution)/shard_map/ppermute | solution.py:321
  22.0 0.0 collective-permute-done.6.refs_3_
  22.0 0.3 collective-permute-start.10
  22.3 0.1 collective-permute-done.5.refs_2_
  22.4 0.0 collective-permute-done.8.refs_6_.refs_7_
  22.4 2.3 %collective-permute-done.7.refs_5_.refs_6_ = bf16[16,512]{1,0:T(8,128)(2,1)S(1)} collective-permute-done((bf16[16,512]{1,0:T(8,128)(2,1)S(1)}, bf16[16,512]{1,0:T(8,128)(2,1)S(1)}, u32[]{:S(2)}, u32[]{:S(2)}) %collective-permute-start.7) | collective-permute-done | bytes 16416 | tf_op jit(solution)/shard_map/ppermute | solution.py:321
  24.7 0.0 copy-done
  24.7 3.7 %shard_map.49 = (f32[2,544,128]{2,1,0:T(8,128)S(1)}, f32[2,544,128]{2,1,0:T(8,128)S(1)}) custom-call(s32[2]{0:T(128)S(1)} %copy-done, bf16[2,2064,128]{2,1,0:T(8,128)(2,1)S(1)} %get-tuple-element.38.q_buf, bf16[2,2064,128]{2,1,0:T(8,128)(2,1)S(1)} %get-tuple-element.39.g_buf, bf16[128,256]{1,0:T(8,128)(2,1)S(1)} %get-tuple-element.41.refs_0_, ...), custom_call_target="tpu_custom_call" | custom-call | flops 4000000000 | bytes 1000 | tf_op jit(solution)/shard_map/pallas_call | solution.py:277
  28.5 0.7 %collective-permute-start.11 = (bf16[144,512]{1,0:T(8,128)(2,1)S(1)}, bf16[144,512]{1,0:T(8,128)(2,1)S(1)}, u32[]{:S(2)}, u32[]{:S(2)}) collective-permute-start(bf16[144,512]{1,0:T(8,128)(2,1)S(1)} %shard_map.51), channel_id=1, source_target_pairs={{0,2},{1,3},{2,0},{3,1},{4,6},{5,7},{6,4},{7,5},{8,10},{9,11},{10,... | collective-permute-start | bytes 442376 | tf_op jit(solution)/shard_map/ppermute | solution.py:321
  29.2 0.0 collective-permute-done.10.refs_5_
  29.2 0.0 collective-permute-done.9.refs_4_
  29.2 1.4 %shard_map.50 = (f32[2,544,128]{2,1,0:T(8,128)S(1)}, f32[2,544,128]{2,1,0:T(8,128)S(1)}) custom-call(s32[2]{0:T(128)S(1)} %copy-done, bf16[2,2064,128]{2,1,0:T(8,128)(2,1)S(1)} %get-tuple-element.38.q_buf, bf16[2,2064,128]{2,1,0:T(8,128)(2,1)S(1)} %get-tuple-element.39.g_buf, f32[2,544,128]{2,1,0:T(8,128)S(1)} %get-tuple-element.45.refs_0_.dk_ref, ...), custom_call_target="tpu_custom_call" | custom-call | flops 4000000000 | bytes 1000 | tf_op jit(solution)/shard_map/pallas_call | solution.py:277
  30.6 3.8 %collective-permute-start.12 = (bf16[128,512]{1,0:T(8,128)(2,1)S(1)}, bf16[128,512]{1,0:T(8,128)(2,1)S(1)}, u32[]{:S(2)}, u32[]{:S(2)}) collective-permute-start(bf16[128,512]{1,0:T(8,128)(2,1)S(1)} %shard_map.52), channel_id=1, source_target_pairs={{0,2},{1,3},{2,0},{3,1},{4,6},{5,7},{6,4},{7,5},{8,10},{9,11},{10,... | collective-permute-start | bytes 393224 | tf_op jit(solution)/shard_map/ppermute | solution.py:321
  34.5 0.0 collective-permute-done.11.across.across0
  34.5 0.7 %collective-permute-start.13 = (bf16[16,512]{1,0:T(8,128)(2,1)S(1)}, bf16[16,512]{1,0:T(8,128)(2,1)S(1)}, u32[]{:S(2)}, u32[]{:S(2)}) collective-permute-start(bf16[16,512]{1,0:T(8,128)(2,1)S(1)} %shard_map.53), channel_id=1, source_target_pairs={{0,4},{1,5},{2,6},{3,7},{4,0},{5,1},{6,2},{7,3},{8,12},{9,13},{10,... | collective-permute-start | bytes 49160 | tf_op jit(solution)/shard_map/ppermute | solution.py:321
  35.2 2.2 %collective-permute-done.12.across1 = bf16[128,512]{1,0:T(8,128)(2,1)S(1)} collective-permute-done((bf16[128,512]{1,0:T(8,128)(2,1)S(1)}, bf16[128,512]{1,0:T(8,128)(2,1)S(1)}, u32[]{:S(2)}, u32[]{:S(2)}) %collective-permute-start.12) | collective-permute-done | bytes 131104 | tf_op jit(solution)/shard_map/ppermute | solution.py:321
  37.4 0.9 %collective-permute-done.13.ends = bf16[16,512]{1,0:T(8,128)(2,1)S(1)} collective-permute-done((bf16[16,512]{1,0:T(8,128)(2,1)S(1)}, bf16[16,512]{1,0:T(8,128)(2,1)S(1)}, u32[]{:S(2)}, u32[]{:S(2)}) %collective-permute-start.13) | collective-permute-done | bytes 16416 | tf_op jit(solution)/shard_map/ppermute | solution.py:321
  38.3 0.1 shard_map.54
  38.4 0.1 collective-permute-start.14
  38.4 0.7 %shard_map.55.refs_0_ = bf16[1,128,1024]{2,1,0:T(8,128)(2,1)} custom-call(f32[128,512]{1,0:T(8,128)S(1)} %get-tuple-element.51.block), custom_call_target="tpu_custom_call" | custom-call | flops 1000 | bytes 1000 | tf_op jit(solution)/shard_map/pallas_call | solution.py:381
  39.1 0.6 %collective-permute-done.14.block = bf16[128,512]{1,0:T(8,128)(2,1)S(1)} collective-permute-done((bf16[128,512]{1,0:T(8,128)(2,1)S(1)}, bf16[128,512]{1,0:T(8,128)(2,1)S(1)}, u32[]{:S(2)}, u32[]{:S(2)}) %collective-permute-start.14) | collective-permute-done | bytes 131104 | tf_op jit(solution)/shard_map/ppermute | solution.py:321
  39.8 0.7 %shard_map.56 = bf16[1,128,1024]{2,1,0:T(8,128)(2,1)} custom-call(bf16[128,512]{1,0:T(8,128)(2,1)S(1)} %collective-permute-done.14.block, bf16[1,128,1024]{2,1,0:T(8,128)(2,1)} %shard_map.55.refs_0_), custom_call_target="tpu_custom_call", output_to_operand_aliasing={{}: (1, {})} | custom-call | flops 1000 | bytes 1000 | tf_op jit(solution)/shard_map/pallas_call | solution.py:382
  (4 shorter events, 0.1 us)
Async XLA Ops:
  0.0 16.2 %collective-permute-start.3 = (bf16[1,128,1024]{2,1,0:T(8,128)(2,1)}, bf16[1,128,1024]{2,1,0:T(8,128)(2,1)S(1)}, u32[]{:S(2)}, u32[]{:S(2)}) collective-permute-start(bf16[1,128,1024]{2,1,0:T(8,128)(2,1)} %param.7), channel_id=1, source_target_pairs={{16,0},{17,1},{18,2},{19,3},{20,4},{21,5},{22,6},{23,7},{24,8},{25... | collective-permute-start | bytes 786440 | tf_op jit(solution)/shard_map/ppermute | solution.py:318
  6.1 4.9 %collective-permute-start = (bf16[256,2048]{1,0:T(8,128)(2,1)S(1)}, bf16[256,2048]{1,0:T(8,128)(2,1)}, u32[]{:S(2)}, u32[]{:S(2)}) collective-permute-start(bf16[256,2048]{1,0:T(8,128)(2,1)S(1)} %get-tuple-element.11), channel_id=1, source_target_pairs={{0,1},{1,0},{2,3},{3,2},{4,5},{5,4},{6,7},{7,6},{8,9},{9,8},{10,11... | collective-permute-start | bytes 3145736 | tf_op jit(solution)/shard_map/cond/branch_1_fun/ppermute | solution.py:321
  6.2 3.9 %collective-permute-start.1 = (bf16[64,128]{1,0:T(8,128)(2,1)S(1)}, bf16[64,128]{1,0:T(8,128)(2,1)}, u32[]{:S(2)}, u32[]{:S(2)}) collective-permute-start(bf16[64,128]{1,0:T(8,128)(2,1)S(1)} %get-tuple-element.12), channel_id=1, source_target_pairs={{0,4},{1,5},{2,6},{3,7},{4,0},{5,1},{6,2},{7,3},{8,12},{9,13},{10,... | collective-permute-start | bytes 49160 | tf_op jit(solution)/shard_map/cond/branch_1_fun/ppermute | solution.py:321
  7.8 3.3 %collective-permute-start.2 = (bf16[64,128]{1,0:T(8,128)(2,1)S(1)}, bf16[64,128]{1,0:T(8,128)(2,1)}, u32[]{:S(2)}, u32[]{:S(2)}) collective-permute-start(bf16[64,128]{1,0:T(8,128)(2,1)S(1)} %get-tuple-element.13), channel_id=1, source_target_pairs={{0,5},{1,4},{2,7},{3,6},{4,1},{5,0},{6,3},{7,2},{8,13},{9,12},{10,... | collective-permute-start | bytes 49160 | tf_op jit(solution)/shard_map/cond/branch_1_fun/ppermute | solution.py:321
  11.0 13.7 %copy-start = (s32[2]{0:T(128)S(1)}, s32[2]{0:T(128)}, u32[]{:S(2)}) copy-start(s32[2]{0:T(128)} %len_ref.3) | copy-start | bytes 28
  16.2 2.2 %collective-permute-start.4 = (bf16[128,512]{1,0:T(8,128)(2,1)S(1)}, bf16[128,512]{1,0:T(8,128)(2,1)S(1)}, u32[]{:S(2)}, u32[]{:S(2)}) collective-permute-start(bf16[128,512]{1,0:T(8,128)(2,1)S(1)} %get-tuple-element.42), channel_id=1, source_target_pairs={{0,1},{1,0},{2,3},{3,2},{4,5},{5,4},{6,7},{7,6},{8,9},{9,8},{10,11... | collective-permute-start | bytes 393224 | tf_op jit(solution)/shard_map/ppermute | solution.py:321
  16.3 5.7 %collective-permute-start.6 = (bf16[128,256]{1,0:T(8,128)(2,1)S(1)}, bf16[128,256]{1,0:T(8,128)(2,1)S(1)}, u32[]{:S(2)}, u32[]{:S(2)}) collective-permute-start(bf16[128,256]{1,0:T(8,128)(2,1)S(1)} %get-tuple-element.43), channel_id=1, source_target_pairs={{0,3},{1,2},{2,1},{3,0},{4,7},{5,6},{6,5},{7,4},{8,11},{9,10},{10,... | collective-permute-start | bytes 196616 | tf_op jit(solution)/shard_map/ppermute | solution.py:321
  18.0 4.4 %collective-permute-start.5 = (bf16[128,256]{1,0:T(8,128)(2,1)S(1)}, bf16[128,256]{1,0:T(8,128)(2,1)S(1)}, u32[]{:S(2)}, u32[]{:S(2)}) collective-permute-start(bf16[128,256]{1,0:T(8,128)(2,1)S(1)} %get-tuple-element.41.refs_0_), channel_id=1, source_target_pairs={{0,2},{1,3},{2,0},{3,1},{4,6},{5,7},{6,4},{7,5},{8,10},{9,11},{10,... | collective-permute-start | bytes 196616 | tf_op jit(solution)/shard_map/ppermute | solution.py:321
  18.5 4.0 %collective-permute-start.8 = (bf16[16,512]{1,0:T(8,128)(2,1)S(1)}, bf16[16,512]{1,0:T(8,128)(2,1)S(1)}, u32[]{:S(2)}, u32[]{:S(2)}) collective-permute-start(bf16[16,512]{1,0:T(8,128)(2,1)S(1)} %shard_map.48), channel_id=1, source_target_pairs={{0,4},{1,5},{2,6},{3,7},{4,0},{5,1},{6,2},{7,3},{8,12},{9,13},{10,... | collective-permute-start | bytes 49160 | tf_op jit(solution)/shard_map/ppermute | solution.py:321
  20.1 4.6 %collective-permute-start.7 = (bf16[16,512]{1,0:T(8,128)(2,1)S(1)}, bf16[16,512]{1,0:T(8,128)(2,1)S(1)}, u32[]{:S(2)}, u32[]{:S(2)}) collective-permute-start(bf16[16,512]{1,0:T(8,128)(2,1)S(1)} %shard_map.48), channel_id=1, source_target_pairs={{0,2},{1,3},{2,4},{3,5},{4,6},{5,7},{6,0},{7,1},{8,10},{9,11},{10,... | collective-permute-start | bytes 49160 | tf_op jit(solution)/shard_map/ppermute | solution.py:321
  21.6 7.6 %collective-permute-start.9 = (bf16[128,256]{1,0:T(8,128)(2,1)S(1)}, bf16[128,256]{1,0:T(8,128)(2,1)S(1)}, u32[]{:S(2)}, u32[]{:S(2)}) collective-permute-start(bf16[128,256]{1,0:T(8,128)(2,1)S(1)} %get-tuple-element.44.refs_1_.refs_4_.refs_2_), channel_id=1, source_target_pairs={{0,2},{1,3},{2,0},{3,1},{4,6},{5,7},{6,4},{7,5},{8,10},{9,11},{10,... | collective-permute-start | bytes 196616 | tf_op jit(solution)/shard_map/ppermute | solution.py:321
  22.0 7.2 %collective-permute-start.10 = (bf16[128,256]{1,0:T(8,128)(2,1)S(1)}, bf16[128,256]{1,0:T(8,128)(2,1)S(1)}, u32[]{:S(2)}, u32[]{:S(2)}) collective-permute-start(bf16[128,256]{1,0:T(8,128)(2,1)S(1)} %get-tuple-element.47), channel_id=1, source_target_pairs={{0,3},{1,2},{2,1},{3,0},{4,7},{5,6},{6,5},{7,4},{8,11},{9,10},{10,... | collective-permute-start | bytes 196616 | tf_op jit(solution)/shard_map/ppermute | solution.py:321
  28.5 5.9 %collective-permute-start.11 = (bf16[144,512]{1,0:T(8,128)(2,1)S(1)}, bf16[144,512]{1,0:T(8,128)(2,1)S(1)}, u32[]{:S(2)}, u32[]{:S(2)}) collective-permute-start(bf16[144,512]{1,0:T(8,128)(2,1)S(1)} %shard_map.51), channel_id=1, source_target_pairs={{0,2},{1,3},{2,0},{3,1},{4,6},{5,7},{6,4},{7,5},{8,10},{9,11},{10,... | collective-permute-start | bytes 442376 | tf_op jit(solution)/shard_map/ppermute | solution.py:321
  30.6 6.8 %collective-permute-start.12 = (bf16[128,512]{1,0:T(8,128)(2,1)S(1)}, bf16[128,512]{1,0:T(8,128)(2,1)S(1)}, u32[]{:S(2)}, u32[]{:S(2)}) collective-permute-start(bf16[128,512]{1,0:T(8,128)(2,1)S(1)} %shard_map.52), channel_id=1, source_target_pairs={{0,2},{1,3},{2,0},{3,1},{4,6},{5,7},{6,4},{7,5},{8,10},{9,11},{10,... | collective-permute-start | bytes 393224 | tf_op jit(solution)/shard_map/ppermute | solution.py:321
  34.5 3.8 %collective-permute-start.13 = (bf16[16,512]{1,0:T(8,128)(2,1)S(1)}, bf16[16,512]{1,0:T(8,128)(2,1)S(1)}, u32[]{:S(2)}, u32[]{:S(2)}) collective-permute-start(bf16[16,512]{1,0:T(8,128)(2,1)S(1)} %shard_map.53), channel_id=1, source_target_pairs={{0,4},{1,5},{2,6},{3,7},{4,0},{5,1},{6,2},{7,3},{8,12},{9,13},{10,... | collective-permute-start | bytes 49160 | tf_op jit(solution)/shard_map/ppermute | solution.py:321
  38.4 1.4 %collective-permute-start.14 = (bf16[128,512]{1,0:T(8,128)(2,1)S(1)}, bf16[128,512]{1,0:T(8,128)(2,1)S(1)}, u32[]{:S(2)}, u32[]{:S(2)}) collective-permute-start(bf16[128,512]{1,0:T(8,128)(2,1)S(1)} %get-tuple-element.50), channel_id=1, source_target_pairs={{0,1},{1,0},{2,3},{3,2},{4,5},{5,4},{6,7},{7,6},{8,9},{9,8},{10,11... | collective-permute-start | bytes 393224 | tf_op jit(solution)/shard_map/ppermute | solution.py:321
